TPU v7x, 128 devices: a whole 4x4x4 slice. The times are simulated.
128 devices in a mesh: grp: 32 (over z, y, x_hi), ep: 2 (over core), tp: 2 (over x_lo).
Axes of the slice: x: 4 (x_hi: 2, x_lo: 2; x = x_hi * 2 + x_lo), y: 4, z: 4, core: 2. Of those that a mesh axis runs over, the one named last changes fastest.
Arguments:
- queries: bfloat16 [3, 32, 6144], P(None, 'grp', 'ep')
- new_keys: bfloat16 [3, 32, 1024], P(None, 'grp', 'ep'), may hold values from -6 to 6
- new_values: bfloat16 [3, 32, 1024], P(None, 'grp', 'ep'), may hold values from -6 to 6
- cache_keys: bfloat16 [32, 1024, 1024], P('grp', 'tp', 'ep')
- cache_values: bfloat16 [32, 1024, 1024], P('grp', 'tp', 'ep'), may hold values from -6 to 6
- lengths: int32 [32], P('grp'), may hold values from 2 to 1024, as said below
- residual: bfloat16 [3, 32, 6144], P(None, 'grp', 'tp'), may hold values from -6 to 6
- out_weight: bfloat16 [6144, 6144], P('ep', 'tp'), may hold values from -0.078125 to 0.078125
- norm_gain: float32 [6144], P('tp'), may hold values from 0.1 to 1.9
- router_weight: bfloat16 [6144, 8], P('tp'), may hold values from -0.078125 to 0.078125
- routes: int32 [3, 32, 2], replicated, may hold values from 0 to 7, all different within a row; in each aligned block of 96 rows (0 to 95, 96 to 191, ..., all dimensions but the last counted through in order) at most 48 rows name the same one
- expert_gate: bfloat16 [8, 6144, 8192], P('ep', 'tp', 'grp'), may hold values from -0.078125 to 0.078125
- expert_up: bfloat16 [8, 6144, 8192], P('ep', 'tp', 'grp'), may hold values from -0.078125 to 0.078125
- expert_down: bfloat16 [8, 8192, 6144], P('ep', 'grp', 'tp'), may hold values from -0.0625 to 0.0625
Outputs:
- mixed: bfloat16 [3, 32, 6144], P(None, 'grp', 'tp')
Inputs may be any that keep to these rules, and one draw needn't show every extreme that they name: `lengths`: one sequence has exactly 1024 valid positions. `routes`: the two experts of a token differ, every expert is named by some token, and over all 96 tokens no expert is named by more than 48 of them; one expert is named by exactly 48.
All inputs are finite; a program needn't handle non-finite values.
Results may differ from a plain program's by a relative error of at most 0.02.
Values may be sent and summed in bfloat16 or wider, within the bound.
No kernel may reach another device: no remote copies, remote signals or barrier semaphores. Data moves between devices by JAX's collectives and lax.ppermute only.
A program may use at most 128 MiB of HBM per device.

v0:
```python
import jax
import jax.numpy as jnp
from jax import lax
from jax.sharding import PartitionSpec as P

D = 6144
HD = 128
E = 8


far_below = -1e30
epsilon = 1e-05


def joined(value, axis, join):
    gathered = jax.tree.map(
        lambda a, kind: lax.all_gather(a.astype(kind), axis),
        value,
        jax.tree.map(lambda a: jnp.bfloat16 if a.dtype == jnp.float32 else a.dtype, value),
    )

    def take(source):
        return jax.tree.map(
            lambda a, own: lax.dynamic_index_in_dim(a, source, 0, False).astype(own.dtype),
            gathered,
            value,
        )

    return lax.fori_loop(
        1, lax.axis_size(axis), lambda source, state: join(state, take(source)), take(0)
    )


def combine_parts(earlier, latter):
    highest = jnp.maximum(earlier[0], latter[0])
    first_factor = jnp.exp(earlier[0] - highest)
    second_factor = jnp.exp(latter[0] - highest)
    totals = earlier[1] * first_factor + latter[1] * second_factor
    weighted = earlier[2] * first_factor[..., None] + latter[2] * second_factor[..., None]
    return (highest, totals, weighted)


def partial_attention(scores, allowed, values_in, formula):
    scores = jnp.where(allowed, scores, far_below)
    highest = jnp.max(scores, axis=-1)
    exponent = jnp.where(allowed, jnp.exp(scores - highest[..., None]), 0.0)
    totals = jnp.sum(exponent, axis=-1)
    weighted = jnp.einsum(
        formula, exponent.astype(jnp.bfloat16), values_in, preferred_element_type=jnp.float32
    )
    return (highest, totals, weighted)


def activate(paired, row_inverse):
    gate = paired[:, :, 0, :] * row_inverse[..., None]
    upward = paired[:, :, 1, :] * row_inverse[..., None]
    return (jax.nn.silu(gate) * upward).astype(jnp.bfloat16)


def on_device(
    queries,
    new_keys,
    new_values,
    cache_keys,
    cache_values,
    lengths,
    residual,
    out_weight,
    norm_gain,
    router_weight,
    routes,
    expert_gate,
    expert_up,
    expert_down,
):
    step_count, seq_rows, query_width = queries.shape
    kv_local = cache_keys.shape[2] // HD
    group_size = query_width // (kv_local * HD)
    cache_rows = cache_keys.shape[1]
    scale = HD ** (-0.5)
    query_heads = queries.reshape(step_count, seq_rows, kv_local, group_size, HD)
    cache_key = cache_keys.reshape(seq_rows, cache_rows, kv_local, HD)
    cache_value = cache_values.reshape(seq_rows, cache_rows, kv_local, HD)
    fresh_key = new_keys.reshape(step_count, seq_rows, kv_local, HD)
    fresh_value = new_values.reshape(step_count, seq_rows, kv_local, HD)
    positions = lax.axis_index("tp") * cache_rows + jnp.arange(cache_rows, dtype=jnp.int32)
    stored_ok = (positions[None, :] < lengths[:, None])[None, :, None, None, :]
    stored_scores = (
        jnp.einsum("sbkgd,bpkd->sbkgp", query_heads, cache_key, preferred_element_type=jnp.float32)
        * scale
    )
    stored_part = partial_attention(stored_scores, stored_ok, cache_value, "sbkgp,bpkd->sbkgd")
    stored_part = joined(stored_part, "tp", combine_parts)
    order = jnp.arange(step_count, dtype=jnp.int32)
    fresh_ok = (order[:, None] >= order[None, :])[:, None, None, None, :]
    fresh_scores = (
        jnp.einsum("sbkgd,tbkd->sbkgt", query_heads, fresh_key, preferred_element_type=jnp.float32)
        * scale
    )
    fresh_part = partial_attention(fresh_scores, fresh_ok, fresh_value, "sbkgt,tbkd->sbkgd")
    highest, totals, weighted = combine_parts(stored_part, fresh_part)
    attended = (
        (weighted / totals[..., None])
        .astype(jnp.bfloat16)
        .reshape(step_count * seq_rows, query_width)
    )
    head_terms = jnp.dot(attended, out_weight, preferred_element_type=jnp.float32)
    attn_out = lax.psum(head_terms.astype(jnp.bfloat16), "ep").astype(jnp.float32)
    width_cols = residual.shape[2]
    state = (
        residual.reshape(step_count * seq_rows, width_cols).astype(jnp.float32) + attn_out
    ).astype(jnp.bfloat16)
    state = state.reshape(step_count, seq_rows, width_cols)
    all_state = lax.all_gather(state, "grp", axis=1, tiled=True)
    token_count = all_state.shape[1]
    row_total = step_count * token_count
    flat_state = all_state.reshape(row_total, width_cols).astype(jnp.float32)
    squares = jnp.sum(flat_state * flat_state, axis=-1)
    scaled = (flat_state * norm_gain).astype(jnp.bfloat16)
    router_terms = jnp.dot(scaled, router_weight, preferred_element_type=jnp.float32)
    chosen = routes.reshape(row_total, 2)
    local_count = expert_gate.shape[0]
    local_ids = lax.axis_index("ep") * local_count + jnp.arange(local_count, dtype=jnp.int32)
    local_match = chosen[:, :, None] == local_ids[None, None, :]
    local_table = local_match.astype(jnp.float32)
    gate_terms = jnp.einsum("nd,edf->nef", scaled, expert_gate, preferred_element_type=jnp.float32)
    up_terms = jnp.einsum("nd,edf->nef", scaled, expert_up, preferred_element_type=jnp.float32)
    paired = jnp.stack([gate_terms, up_terms], axis=2)
    paired, router_logits, squares = (
        lax.psum(paired.astype(jnp.bfloat16), "tp").astype(jnp.float32),
        lax.psum(router_terms.astype(jnp.bfloat16), "tp").astype(jnp.float32),
        lax.psum(squares.astype(jnp.bfloat16), "tp").astype(jnp.float32),
    )
    inverse = lax.rsqrt(squares / D + epsilon)
    row_inverse = inverse[:, None]
    activated = activate(paired, row_inverse)
    logits = router_logits * inverse[:, None]
    every_expert = jnp.arange(E, dtype=jnp.int32)
    choose_table = (chosen[:, :, None] == every_expert[None, None, :]).astype(jnp.float32)
    picked = jnp.sum(logits[:, None, :] * choose_table, axis=-1)
    shares = jax.nn.softmax(picked, axis=-1)
    expert_share = jnp.sum(shares[:, :, None] * local_table, axis=1)
    down_terms = jnp.einsum(
        "nef,efd->ned", activated, expert_down, preferred_element_type=jnp.float32
    )
    expert_terms = jnp.sum(down_terms * expert_share[:, :, None], axis=1).reshape(
        step_count, token_count, width_cols
    )
    everything = lax.psum(expert_terms, ("grp", "ep"))
    combined = lax.dynamic_slice_in_dim(everything, lax.axis_index("grp") * seq_rows, seq_rows, 1)
    return (state.astype(jnp.float32) + combined).astype(jnp.bfloat16)


def solution(mesh):
    in_specs = (
        P(None, "grp", "ep"),
        P(None, "grp", "ep"),
        P(None, "grp", "ep"),
        P("grp", "tp", "ep"),
        P("grp", "tp", "ep"),
        P("grp"),
        P(None, "grp", "tp"),
        P("ep", "tp"),
        P("tp"),
        P("tp", None),
        P(),
        P("ep", "tp", "grp"),
        P("ep", "tp", "grp"),
        P("ep", "grp", "tp"),
    )
    out_specs = P(None, "grp", "tp")
    return jax.shard_map(
        on_device, mesh=mesh, in_specs=in_specs, out_specs=out_specs, check_vma=False
    )
```

profile of v0, /device:TPU:1, one launch (start us, length us, event | category | flops | bytes accessed | tf_op | source)
XLA Modules:
  0.0 831.2 jit_solution(14176052417267597345)
XLA Ops:
  6.5 1.2 reshape.339
  7.7 0.8 reshape.337
  8.5 1.2 reshape.336
  11.2 3.9 all-gather
  15.1 3.2 all-gather.2
  18.3 3.2 all-gather.1
  21.5 0.9 fusion.63
  22.5 1.0 fusion.9
  23.5 8.9 %convolution_convert_fusion = bf16[3,3072]{1,0:T(4,128)(2,1)S(1)} fusion(bf16[3,3072]{1,0:T(4,128)(2,1)S(1)} %reshape.343, bf16[3072,3072]{1,0:T(8,128)(2,1)} %param.21), kind=kOutput, calls=%fused_computation.2 | convolution fusion | flops 56632320 | bytes 18911232 | tf_op jit(solution)/shard_map/dot_general | solution.py:107
  32.4 7.6 psum.35
  40.0 89.6 %all-gather.3 = bf16[3,98304]{1,0:T(4,128)(2,1)S(1)} all-gather(bf16[3,3072]{1,0:T(4,128)(2,1)S(1)} %fusion.32), channel_id=5, replica_groups=mesh['grp'=32,'ep'=2,'tp'=2] {'grp'}, dimensions={1}, use_global_device_ids=true | all-gather | bytes 608256 | tf_op jit(solution)/shard_map/all_gather | solution.py:114
  129.6 0.8 reshape.352
  130.5 4.0 fusion.2
  134.6 0.5 slice-done.1
  135.1 1.1 fusion.1
  136.3 0.8 pad_maximum_fusion
  137.7 0.7 bitcast_reduce_fusion
  138.5 4.1 all-reduce
  142.8 33.7 %all-reduce.4.cloned.1.call-done = bf16[96,4,2,256]{3,0,1,2:T(8,128)(2,1)} async-done(((bf16[96,4,2,256]{3,0,1,2:T(8,128)(2,1)}), bf16[96,4,2,256]{3,0,1,2:T(8,128)(2,1)}) %all-reduce.4.cloned.1.call-update) | async-done | bytes 393232 | tf_op jit(solution)/shard_map/psum | solution.py:130
  176.5 1.1 convert_element_type.255
  177.6 4.2 fusion
  181.8 2.0 copy.100
  183.8 639.2 %all-reduce.6.cloned.1.call-done = f32[3,32,3072]{2,0,1:T(4,128)} async-done(((f32[3,32,3072]{2,0,1:T(4,128)}), f32[3,32,3072]{2,0,1:T(4,128)}) %all-reduce.6.cloned.1.call-update) | async-done | bytes 1179664 | tf_op jit(solution)/shard_map/psum | solution.py:149
  822.9 1.4 fusion.31
  (44 shorter events, 2.1 us)
Async XLA Ops:
  6.5 130.9 %copy-start = (bf16[3072,8]{0,1:T(8,128)(2,1)S(1)}, bf16[3072,8]{0,1:T(8,128)(2,1)}, u32[]{:S(2)}) copy-start(bf16[3072,8]{0,1:T(8,128)(2,1)} %param.23) | copy-start | bytes 147460
  6.5 170.0 %all-reduce.4.cloned.1.call-start = ((), (), s32[]{:S(2)}) async-start(), calls=%async_computation | async-start | bytes 786432 | tf_op jit(solution)/shard_map/psum | solution.py:130
  23.5 16.5 %copy-start.1 = (bf16[3,1,3072]{2,0,1:T(4,128)(2,1)S(1)}, bf16[3,1,3072]{2,0,1:T(4,128)(2,1)}, u32[]{:S(2)}) copy-start(bf16[3,1,3072]{2,0,1:T(4,128)(2,1)} %param.20) | copy-start | bytes 55300
  23.5 106.9 %copy-start.2 = (f32[3072]{0:T(1024)S(1)}, f32[3072]{0:T(1024)}, u32[]{:S(2)}) copy-start(f32[3072]{0:T(1024)} %param.22) | copy-start | bytes 36868
  130.4 4.2 slice-start
  130.5 4.6 slice-start.1
  136.2 6.3 copy-start.3
  137.1 685.8 %all-reduce.6.cloned.1.call-start = ((), (), s32[]{:S(2)}) async-start(), calls=%async_computation.1 | async-start | bytes 3145728 | tf_op jit(solution)/shard_map/psum | solution.py:149
Sparse Core Ops, SparseCore 0:
  137.2 39.2 all-reduce.3
  183.9 638.9 all-reduce.5
where the time goes:
time: 832 us; the launch traced here: 831 us
  waiting for transfers between devices  673 us (81%)
  blocking collectives  112 us (13%)
  matrix products  21 us (3%)
  between operations  14.3 us (2%)
    psum x1, waiting for transfers between devices, on_device(): everything = lax.psum(expert_terms, ('grp', 'ep'))  639 us
    all_gather x1, blocking collectives, on_device(): all_state = lax.all_gather(state, 'grp', axis=1, tiled=True)  89.6 us
    psum x1, waiting for transfers between devices, on_device(): lax.psum(paired.astype(jnp.bfloat16), 'tp').astype(jnp.float32)  33.7 us
  transfers between devices with their start and end apart: 2, of which 2 were waited for; matrix products, arithmetic and copies ran while one was open for 0% of the time, Pallas kernels for 0%

commit v1 on v0

v1 whole, which is shorter than its diff:
```python
import functools

import jax
import jax.numpy as jnp
from jax import lax
from jax.experimental import pallas as pl
from jax.experimental.pallas import tpu as pltpu
from jax.sharding import PartitionSpec as P

D = 6144
HD = 128
E = 8
CAP = 48
LANES = 128

far_below = -1e30
epsilon = 1e-05
VMEM = pl.BlockSpec(memory_space=pltpu.VMEM)
SMEM = pl.BlockSpec(memory_space=pltpu.SMEM)
swap = [(0, 1), (1, 0)]
f32 = jnp.float32
bf16 = jnp.bfloat16


def call(kernel, out, operands, specs, scratch=(), limit=16):
    return pl.pallas_call(
        kernel,
        out_shape=out,
        in_specs=specs,
        out_specs=jax.tree.map(lambda _: VMEM, out),
        scratch_shapes=scratch,
        compiler_params=pltpu.CompilerParams(vmem_limit_bytes=limit * 2**20),
    )(*operands)


def iota(shape, dim):
    return lax.broadcasted_iota(jnp.int32, shape, dim)


def pieces(value):
    high = value.astype(bf16).astype(f32)
    rest = value - high
    middle = rest.astype(bf16).astype(f32)
    return high, middle, rest - middle


def attention_kernel(
    length_ref, query_ref, key_ref, value_ref, new_key_ref, new_value_ref, out_ref, rows_ref
):
    steps = query_ref.shape[0]
    heads = query_ref.shape[1] // HD
    kv = key_ref.shape[1] // HD
    cached = key_ref.shape[0]
    rows = heads * steps
    per_kv = rows // kv
    part = lax.axis_index("tp")
    for h in range(heads):
        rows_ref[h * steps : (h + 1) * steps, :] = query_ref[:, h * HD : (h + 1) * HD].astype(f32)
    query = rows_ref[...]
    row = iota((rows, 1), 0)
    owner = [(row >= k * per_kv) & (row < (k + 1) * per_kv) for k in range(kv)]
    step = row % steps
    scale = HD ** (-0.5)
    spread = jnp.concatenate(
        [jnp.where(owner[k], query, 0.0).astype(bf16) for k in range(kv)], axis=1
    )
    scores = (
        lax.dot_general(
            spread, key_ref[...], (((1,), (1,)), ((), ())), preferred_element_type=f32
        )
        * scale
    )
    allowed = (iota((1, cached), 1) + part * cached) < length_ref[0]
    scores = jnp.where(allowed, scores, far_below)
    new_key = new_key_ref[...].astype(f32)
    new_value = new_value_ref[...].astype(f32)

    def chosen(wide, t):
        out = jnp.zeros((rows, HD), f32)
        for k in range(kv):
            out = jnp.where(owner[k], wide[t : t + 1, k * HD : (k + 1) * HD], out)
        return out

    fresh_ok = [(step >= t) & (part == 0) for t in range(steps)]
    fresh = [
        jnp.where(
            fresh_ok[t],
            jnp.sum(query * chosen(new_key, t), axis=1, keepdims=True) * scale,
            far_below,
        )
        for t in range(steps)
    ]
    highest = jnp.max(scores, axis=1, keepdims=True)
    for t in range(steps):
        highest = jnp.maximum(highest, fresh[t])
    exponent = jnp.where(allowed, jnp.exp(scores - highest), 0.0)
    totals = jnp.sum(exponent, axis=1, keepdims=True)
    wide = jnp.dot(exponent.astype(bf16), value_ref[...], preferred_element_type=f32)
    weighted = jnp.zeros((rows, HD), f32)
    for k in range(kv):
        weighted = jnp.where(owner[k], wide[:, k * HD : (k + 1) * HD], weighted)
    for t in range(steps):
        term = jnp.where(fresh_ok[t], jnp.exp(fresh[t] - highest), 0.0)
        totals = totals + term
        weighted = weighted + term.astype(bf16).astype(f32) * chosen(new_value, t)
    present = totals > 0.0
    safe = jnp.where(present, totals, 1.0)
    out_ref[:, :HD] = (weighted / safe).astype(bf16)
    level = jnp.where(present, highest + jnp.log(safe), far_below)
    high, middle, low = pieces(level)
    lane = iota((rows, LANES), 1)
    out_ref[:, HD:] = jnp.where(lane == 0, high, jnp.where(lane == 1, middle, low)).astype(bf16)


def project_kernel(own_ref, other_ref, weight_ref, out_ref, rows_ref):
    steps = 3
    heads = weight_ref.shape[0] // HD

    def read(ref):
        tail = ref[:, HD:].astype(f32)
        return ref[:, :HD].astype(f32), tail[:, 0:1] + tail[:, 1:2] + tail[:, 2:3]

    own, own_level = read(own_ref)
    other, other_level = read(other_ref)
    top = jnp.maximum(own_level, other_level)
    own_factor = jnp.exp(own_level - top)
    other_factor = jnp.exp(other_level - top)
    rows_ref[...] = (own * own_factor + other * other_factor) / (own_factor + other_factor)
    attended = jnp.concatenate(
        [rows_ref[h * steps : (h + 1) * steps, :] for h in range(heads)], axis=1
    ).astype(bf16)
    terms = jnp.dot(attended, weight_ref[...], preferred_element_type=f32)
    for k in range(heads):
        rows_ref[k * steps : (k + 1) * steps, :] = terms[:, k * LANES : (k + 1) * LANES]
    out_ref[...] = rows_ref[...].astype(bf16)


def rows_kernel(wide_ref, out_ref):
    steps, width = wide_ref.shape
    for k in range(width // LANES):
        out_ref[k * steps : (k + 1) * steps, :] = wide_ref[:, k * LANES : (k + 1) * LANES].astype(
            f32
        )


def matched(routes_ref, first, count):
    wanted = iota((count, LANES), 0) + first
    return (routes_ref[0:1, :] == wanted) | (routes_ref[1:2, :] == wanted)


def places(routes_ref):
    count = E // 2
    mask = matched(routes_ref, lax.axis_index("ep") * count, 8)
    earlier = (iota((LANES, LANES), 0) < iota((LANES, LANES), 1)).astype(f32).astype(bf16)
    ones = mask.astype(f32)
    place = jnp.dot(ones.astype(bf16), earlier, preferred_element_type=f32).astype(jnp.int32)
    slot = iota((CAP, LANES), 0)
    return [
        jnp.where(place[e : e + 1, :] == slot, ones[e : e + 1, :], 0.0) for e in range(count)
    ]


def hidden_kernel(
    state_ref, gain_ref, router_ref, routes_ref, gate_ref, up_ref, out_ref, wide_ref, scaled_ref, both_ref
):
    groups = state_ref.shape[0] // 72
    steps = 3
    blocks = 24
    tokens = groups * steps
    wide_ref[...] = state_ref[...].astype(f32)
    squares = [jnp.zeros((groups, LANES), f32) for _ in range(steps)]
    for k in range(blocks):
        gain = gain_ref[:, k * LANES : (k + 1) * LANES]
        for s in range(steps):
            block = wide_ref[pl.ds(k * steps + s, groups, stride=72), :]
            squares[s] = squares[s] + block * block
            scaled_ref[s * groups : (s + 1) * groups, k * LANES : (k + 1) * LANES] = (
                block * gain
            ).astype(bf16)
    scaled = scaled_ref[...]
    square = jnp.sum(jnp.concatenate(squares, axis=0), axis=1, keepdims=True)
    diagonal = iota((tokens, LANES), 0) == iota((tokens, LANES), 1)
    square = jnp.sum(jnp.where(diagonal, square, 0.0), axis=0, keepdims=True)
    router = lax.dot_general(
        router_ref[...], scaled, (((1,), (1,)), ((), ())), preferred_element_type=f32
    )
    router = jnp.concatenate([router, jnp.zeros((E, LANES - tokens), f32)], axis=1)
    tables = places(routes_ref)
    width = gate_ref.shape[2]
    both_ref[tokens:, :] = jnp.zeros((LANES - tokens, 2 * width), bf16)
    for e in range(gate_ref.shape[0]):
        both_ref[:tokens, :width] = jnp.dot(
            scaled, gate_ref[e], preferred_element_type=f32
        ).astype(bf16)
        both_ref[:tokens, width:] = jnp.dot(scaled, up_ref[e], preferred_element_type=f32).astype(
            bf16
        )
        out_ref[e * CAP : (e + 1) * CAP, :] = jnp.dot(
            tables[e].astype(bf16), both_ref[...], preferred_element_type=f32
        ).astype(bf16)
    high, middle, _ = pieces(router)
    square_high, square_middle, _ = pieces(square)
    line = iota((8, LANES), 0)
    extra = jnp.concatenate(
        [
            high,
            middle,
            jnp.where(line == 0, square_high, jnp.where(line == 1, square_middle, 0.0)),
            jnp.zeros((8, LANES), f32),
        ],
        axis=1,
    )
    extra = jnp.concatenate([extra, jnp.zeros((8, 4 * LANES), f32)], axis=0)
    out_ref[4 * CAP :, :] = extra.astype(bf16)


def down_kernel(own_ref, other_ref, routes_ref, down_ref, out_ref, mixed_ref, wide_ref):
    groups = out_ref.shape[0] // 72
    steps = 3
    tokens = groups * steps
    width = down_ref.shape[1]
    count = down_ref.shape[0]
    tail = own_ref[4 * CAP :, :].astype(f32) + other_ref[4 * CAP :, :].astype(f32)
    square = tail[0:1, 2 * LANES : 3 * LANES] + tail[1:2, 2 * LANES : 3 * LANES]
    inverse = lax.rsqrt(square / D + epsilon)
    logits = (tail[:E, :LANES] + tail[:E, LANES : 2 * LANES]) * inverse
    every = iota((E, LANES), 0)
    picked = [
        jnp.sum(jnp.where(routes_ref[c : c + 1, :] == every, logits, 0.0), axis=0, keepdims=True)
        for c in range(2)
    ]
    top = jnp.maximum(picked[0], picked[1])
    raised = [jnp.exp(p - top) for p in picked]
    total = raised[0] + raised[1]
    shares = [r / total for r in raised]
    first = lax.axis_index("ep") * count
    tables = places(routes_ref)
    for e in range(count):
        table = tables[e]
        share = jnp.zeros((1, LANES), f32)
        for c in range(2):
            share = share + jnp.where(routes_ref[c : c + 1, :] == first + e, shares[c], 0.0)
        slot_inverse = jnp.sum(table * inverse, axis=1, keepdims=True)
        slot_share = jnp.sum(table * share, axis=1, keepdims=True)
        both = own_ref[e * CAP : (e + 1) * CAP, :].astype(f32) + other_ref[
            e * CAP : (e + 1) * CAP, :
        ].astype(f32)
        both = both * slot_inverse
        gate, up = both[:, :width], both[:, width:]
        activated = (gate / (1.0 + jnp.exp(-gate)) * up).astype(bf16).astype(f32)
        weighted = (activated * slot_share).astype(bf16)
        spread = lax.dot_general(
            table.astype(bf16), weighted, (((0,), (0,)), ((), ())), preferred_element_type=f32
        )
        mixed_ref[:, e * width : (e + 1) * width] = spread[:tokens, :].astype(bf16)
    mixed = mixed_ref[...]
    chunk = 4 * LANES
    for n in range(down_ref.shape[2] // chunk):
        terms = jnp.zeros((tokens, chunk), f32)
        for e in range(count):
            terms = terms + jnp.dot(
                mixed[:, e * width : (e + 1) * width],
                down_ref[e, :, n * chunk : (n + 1) * chunk],
                preferred_element_type=f32,
            )
        for j in range(chunk // LANES):
            k = n * (chunk // LANES) + j
            for s in range(steps):
                wide_ref[pl.ds(k * steps + s, groups, stride=72), :] = terms[
                    s * groups : (s + 1) * groups, j * LANES : (j + 1) * LANES
                ]
    out_ref[...] = wide_ref[...].astype(bf16)


def output_kernel(state_ref, own_ref, other_ref, out_ref, rows_ref):
    steps, width = out_ref.shape
    rows_ref[...] = state_ref[...].astype(f32) + (own_ref[...] + other_ref[...])
    for k in range(width // LANES):
        out_ref[:, k * LANES : (k + 1) * LANES] = rows_ref[k * steps : (k + 1) * steps, :].astype(
            bf16
        )


def on_device(
    queries,
    new_keys,
    new_values,
    cache_keys,
    cache_values,
    lengths,
    residual,
    out_weight,
    norm_gain,
    router_weight,
    routes,
    expert_gate,
    expert_up,
    expert_down,
):
    groups = lax.axis_size("grp")
    steps, _, query_width = queries.shape
    rows = steps * query_width // HD
    struct = jax.ShapeDtypeStruct
    token_count = groups * steps
    routes_row = jnp.pad(
        routes.reshape(token_count, 2).T, ((0, 0), (0, LANES - token_count)), constant_values=-1
    )
    partial = call(
        attention_kernel,
        struct((rows, 2 * HD), bf16),
        (
            lengths,
            queries.reshape(steps, query_width),
            cache_keys[0],
            cache_values[0],
            new_keys[:, 0],
            new_values[:, 0],
        ),
        [SMEM] + [VMEM] * 5,
        [pltpu.VMEM((rows, HD), f32)],
    )
    other = lax.ppermute(partial, "tp", swap)
    terms = call(
        project_kernel,
        struct((rows, LANES), bf16),
        (partial, other, out_weight),
        [VMEM] * 3,
        [pltpu.VMEM((rows, LANES), f32)],
        limit=30,
    )
    residual_rows = call(
        rows_kernel, struct((rows, LANES), f32), (residual[:, 0],), [VMEM]
    )
    other_terms = lax.ppermute(terms, "ep", swap)
    state = (residual_rows + (terms.astype(f32) + other_terms.astype(f32))).astype(bf16)
    all_state = lax.all_to_all(
        jnp.broadcast_to(state[None], (groups, rows, LANES)), "grp", 0, 0
    ).reshape(groups * rows, LANES)
    hidden_rows = 4 * CAP + 16
    width = expert_gate.shape[2]
    hidden = call(
        hidden_kernel,
        struct((hidden_rows, 2 * width), bf16),
        (
            all_state,
            norm_gain.reshape(1, -1),
            router_weight.T,
            routes_row,
            expert_gate,
            expert_up,
        ),
        [VMEM] * 6,
        [
            pltpu.VMEM((groups * rows, LANES), f32),
            pltpu.VMEM((token_count, residual.shape[2]), bf16),
            pltpu.VMEM((LANES, 2 * width), bf16),
        ],
        limit=30,
    )
    other_hidden = lax.ppermute(hidden, "tp", swap)
    sent = call(
        down_kernel,
        struct((groups * rows, LANES), bf16),
        (hidden, other_hidden, routes_row, expert_down),
        [VMEM] * 4,
        [
            pltpu.VMEM((token_count, 4 * width), bf16),
            pltpu.VMEM((groups * rows, LANES), f32),
        ],
        limit=30,
    )
    received = lax.all_to_all(sent.reshape(groups, rows, LANES), "grp", 0, 0)
    summed = jnp.sum(received.astype(f32), axis=0)
    other_summed = lax.ppermute(summed, "ep", swap)
    mixed = call(
        output_kernel,
        struct((steps, residual.shape[2]), bf16),
        (state, summed, other_summed),
        [VMEM] * 3,
        [pltpu.VMEM((rows, LANES), f32)],
    )
    return mixed[:, None]


def solution(mesh):
    in_specs = (
        P(None, "grp", "ep"),
        P(None, "grp", "ep"),
        P(None, "grp", "ep"),
        P("grp", "tp", "ep"),
        P("grp", "tp", "ep"),
        P("grp"),
        P(None, "grp", "tp"),
        P("ep", "tp"),
        P("tp"),
        P("tp", None),
        P(),
        P("ep", "tp", "grp"),
        P("ep", "tp", "grp"),
        P("ep", "grp", "tp"),
    )
    out_specs = P(None, "grp", "tp")
    return jax.shard_map(
        on_device, mesh=mesh, in_specs=in_specs, out_specs=out_specs, check_vma=False
    )
```

time: 832 us -> 83.1 us (0.10)
  waiting for transfers between devices: 673 us -> 20.9 us
  blocking collectives: 112 us -> 16.8 us
  matrix products: 21 us -> 0 us
  starting transfers between devices: 0.04 us -> 18.2 us
  between operations: 14.3 us -> 0.73 us
  local copies, waits for them, and re-layouts: 6.62 us -> 17.1 us
  Pallas kernels: 0 us -> 8.54 us
    psum x2 -> x0, waiting for transfers between devices: 673 us -> none  [the longest x1 639 us: on_device(): everything = lax.psum(expert_terms, ('grp', 'ep'))]
    all_gather x4 -> x0, blocking collectives: 99.9 us -> none  [the longest x1 89.6 us: on_device(): all_state = lax.all_gather(state, 'grp', axis=1, tiled=True)]
    dot_general x9 -> x0, matrix products: 21 us -> none  [the longest x1 8.91 us: on_device(): jnp.dot(attended, out_weight, preferred_element_type=jnp.float32)]
    all_to_all x0 -> x1, blocking collectives: none -> 16.8 us  [on_device(): received = lax.all_to_all(sent.reshape(groups, rows, LANES), 'grp', 0, 0)]
    unnamed x13 -> x27, local copies, waits for them, and re-layouts: 0.57 us -> 16.1 us
    all_to_all x0 -> x1, waiting for transfers between devices: none -> 13.5 us  [on_device(): lax.all_to_all(jnp.broadcast_to(state[None], (groups, rows, LANES)), 'grp...]
    psum x2 -> x0, blocking collectives: 11.6 us -> none  [the longest x1 7.56 us: on_device(): lax.psum(head_terms.astype(jnp.bfloat16), 'ep').astype(jnp.float32)]
    all_to_all x0 -> x1, starting transfers between devices: none -> 10.6 us  [on_device(): lax.all_to_all(jnp.broadcast_to(state[None], (groups, rows, LANES)), 'grp...]
  transfers between devices with their start and end apart: 2 -> 5, of which waited for: 2 -> 5; matrix products, arithmetic and copies ran while one was open for 0% -> 0% of each run, Pallas kernels for 0% -> 0%
where the time goes in v1:
time: 83.1 us; the launch traced here: 82.5 us
  waiting for transfers between devices  20.9 us (25%)
  starting transfers between devices  18.2 us (22%)
  local copies, waits for them, and re-layouts  17.1 us (21%)
  blocking collectives  16.8 us (20%)
  Pallas kernels  8.54 us (10%)
    all_to_all x1, blocking collectives, on_device(): received = lax.all_to_all(sent.reshape(groups, rows, LANES), 'grp', 0, 0)  16.8 us
    unnamed x27, local copies, waits for them, and re-layouts  16.1 us
    all_to_all x1, waiting for transfers between devices, on_device(): lax.all_to_all(jnp.broadcast_to(state[None], (groups, rows, LANES)), 'grp...  13.5 us
    all_to_all x1, starting transfers between devices, on_device(): lax.all_to_all(jnp.broadcast_to(state[None], (groups, rows, LANES)), 'grp...  10.6 us
    pallas_call x6, Pallas kernels, call(): pl.pallas_call(kernel, out_shape=out, in_specs=specs, out_specs=jax.tree....  8.54 us
    ppermute x1, waiting for transfers between devices, on_device(): other_hidden = lax.ppermute(hidden, 'tp', swap)  4.39 us
    ppermute x1, starting transfers between devices, on_device(): other_summed = lax.ppermute(summed, 'ep', swap)  3.14 us
    ppermute x1, starting transfers between devices, on_device(): other = lax.ppermute(partial, 'tp', swap)  2.12 us
  transfers between devices with their start and end apart: 5, of which 5 were waited for; matrix products, arithmetic and copies ran while one was open for 0% of the time, Pallas kernels for 0%

profile of v1, /device:TPU:1, one launch (start us, length us, event | category | flops | bytes accessed | tf_op | source)
XLA Modules:
  0.0 82.5 jit_solution(13470667922943299021)
XLA Ops:
  0.7 1.0 %copy-done.4 = bf16[1,512,512]{2,1,0:T(8,128)(2,1)S(1)} copy-done((bf16[1,512,512]{2,1,0:T(8,128)(2,1)S(1)}, bf16[1,512,512]{2,1,0:T(8,128)(2,1)}, u32[]{:S(2)}) %copy-start.4) | copy-done | bytes 524312
  1.7 1.0 %copy-done.5 = bf16[1,512,512]{2,1,0:T(8,128)(2,1)S(1)} copy-done((bf16[1,512,512]{2,1,0:T(8,128)(2,1)S(1)}, bf16[1,512,512]{2,1,0:T(8,128)(2,1)}, u32[]{:S(2)}) %copy-start.5) | copy-done | bytes 524312
  2.7 0.7 copy-done.8
  3.5 0.7 copy-done.10
  4.2 0.7 copy-done.11
  4.9 0.6 shard_map.137.own_ref
  5.4 2.1 %collective-permute-start = (bf16[72,256]{1,0:T(8,128)(2,1)S(1)}, bf16[72,256]{1,0:T(8,128)(2,1)S(1)}, u32[]{:S(2)}, u32[]{:S(2)}) collective-permute-start(bf16[72,256]{1,0:T(8,128)(2,1)S(1)} %shard_map.137.own_ref), channel_id=1, source_target_pairs={{0,1},{1,0},{2,3},{3,2},{4,5},{5,4},{6,7},{7,6},{8,9},{9,8},{10,11... | collective-permute-start | bytes 110600 | tf_op jit(solution)/shard_map/ppermute | solution.py:322
  7.5 1.3 %collective-permute-done.other_ref = bf16[72,256]{1,0:T(8,128)(2,1)S(1)} collective-permute-done((bf16[72,256]{1,0:T(8,128)(2,1)S(1)}, bf16[72,256]{1,0:T(8,128)(2,1)S(1)}, u32[]{:S(2)}, u32[]{:S(2)}) %collective-permute-start) | collective-permute-done | bytes 36896 | tf_op jit(solution)/shard_map/ppermute | solution.py:322
  8.9 6.4 %copy-done = bf16[3072,3072]{1,0:T(8,128)(2,1)S(1)} copy-done((bf16[3072,3072]{1,0:T(8,128)(2,1)S(1)}, bf16[3072,3072]{1,0:T(8,128)(2,1)}, u32[]{:S(2)}) %copy-start) | copy-done | bytes 18874392
  15.3 2.8 %shard_map.138 = bf16[72,128]{1,0:T(8,128)(2,1)S(1)} custom-call(bf16[72,256]{1,0:T(8,128)(2,1)S(1)} %shard_map.137.own_ref, bf16[72,256]{1,0:T(8,128)(2,1)S(1)} %collective-permute-done.other_ref, bf16[3072,3072]{1,0:T(8,128)(2,1)S(1)} %copy-done), custom_call_target="tpu_custom_call" | custom-call | tf_op jit(solution)/shard_map/pallas_call | solution.py:26
  18.0 2.0 %collective-permute-start.1 = (bf16[72,128]{1,0:T(8,128)(2,1)S(1)}, bf16[72,128]{1,0:T(8,128)(2,1)S(1)}, u32[]{:S(2)}, u32[]{:S(2)}) collective-permute-start(bf16[72,128]{1,0:T(8,128)(2,1)S(1)} %shard_map.138), channel_id=1, source_target_pairs={{0,2},{2,0},{1,3},{3,1},{4,6},{6,4},{5,7},{7,5},{8,10},{10,8},{9,1... | collective-permute-start | bytes 55304 | tf_op jit(solution)/shard_map/ppermute | solution.py:334
  20.0 0.8 %collective-permute-done.1 = bf16[72,128]{1,0:T(8,128)(2,1)S(1)} collective-permute-done((bf16[72,128]{1,0:T(8,128)(2,1)S(1)}, bf16[72,128]{1,0:T(8,128)(2,1)S(1)}, u32[]{:S(2)}, u32[]{:S(2)}) %collective-permute-start.1) | collective-permute-done | bytes 18464 | tf_op jit(solution)/shard_map/ppermute | solution.py:334
  20.9 0.9 %broadcast_in_dim.4 = bf16[32,72,128]{2,1,0:T(8,128)(2,1)} broadcast(bf16[72,128]{1,0:T(8,128)(2,1)S(1)} %add_convert_fusion.state_ref), dimensions={1,2} | broadcast | bytes 608256 | tf_op jit(solution)/shard_map/broadcast_in_dim | solution.py:337
  21.8 10.6 %all-to-all-start = ((bf16[32,72,128]{2,1,0:T(8,128)(2,1)}), bf16[32,72,128]{2,1,0:T(8,128)(2,1)S(1)}, u32[]{:S(2)}, u32[]{:S(2)}) async-start(bf16[32,72,128]{2,1,0:T(8,128)(2,1)} %broadcast_in_dim.4), calls=%async_computation | async-start | bytes 1179648 | tf_op jit(solution)/shard_map/all_to_all | solution.py:336
  32.5 13.5 %all-to-all-done = bf16[32,72,128]{2,1,0:T(8,128)(2,1)S(1)} async-done(((bf16[32,72,128]{2,1,0:T(8,128)(2,1)}), bf16[32,72,128]{2,1,0:T(8,128)(2,1)S(1)}, u32[]{:S(2)}, u32[]{:S(2)}) %all-to-all-start) | async-done | bytes 589856 | tf_op jit(solution)/shard_map/all_to_all | solution.py:336
  46.0 2.8 %copy-done.1 = bf16[4,3072,256]{2,1,0:T(8,128)(2,1)S(1)} copy-done((bf16[4,3072,256]{2,1,0:T(8,128)(2,1)S(1)}, bf16[4,3072,256]{2,1,0:T(8,128)(2,1)}, u32[]{:S(2)}) %copy-start.1) | copy-done | bytes 6291480
  48.8 2.8 %copy-done.2 = bf16[4,3072,256]{2,1,0:T(8,128)(2,1)S(1)} copy-done((bf16[4,3072,256]{2,1,0:T(8,128)(2,1)S(1)}, bf16[4,3072,256]{2,1,0:T(8,128)(2,1)}, u32[]{:S(2)}) %copy-start.2) | copy-done | bytes 6291480
  51.6 3.0 %shard_map.139.own_ref = bf16[208,512]{1,0:T(8,128)(2,1)S(1)} custom-call(bf16[2304,128]{1,0:T(8,128)(2,1)S(1)} %bitcast.14, f32[1,3072]{1,0:T(1,128)S(1)} %bitcast.21, bf16[8,3072]{1,0:T(8,128)(2,1)S(1)} %bitcast.18, s32[2,128]{1,0:T(2,128)S(1)} %pad.4.routes_ref, bf16[4,3072,256]{2,1,0:T(8,128)(2,1)S(1)} %copy-done.1, bf16[4,3072,256]{2,1,0:T(8,128)(2,1)S(1)} %copy-done.2), custom_call_target="tpu_custom_call" | custom-call | tf_op jit(solution)/shard_map/pallas_call | solution.py:26
  55.0 4.4 %collective-permute-done.2.other_ref = bf16[208,512]{1,0:T(8,128)(2,1)S(1)} collective-permute-done((bf16[208,512]{1,0:T(8,128)(2,1)S(1)}, bf16[208,512]{1,0:T(8,128)(2,1)S(1)}, u32[]{:S(2)}, u32[]{:S(2)}) %collective-permute-start.2) | collective-permute-done | bytes 213024 | tf_op jit(solution)/shard_map/ppermute | solution.py:360
  59.4 1.5 %shard_map.140 = bf16[2304,128]{1,0:T(8,128)(2,1)S(1)} custom-call(bf16[208,512]{1,0:T(8,128)(2,1)S(1)} %shard_map.139.own_ref, bf16[208,512]{1,0:T(8,128)(2,1)S(1)} %collective-permute-done.2.other_ref, s32[2,128]{1,0:T(2,128)S(1)} %pad.4.routes_ref, bf16[4,256,3072]{2,1,0:T(8,128)(2,1)S(1)} %copy-done.3), custom_call_target="tpu_custom_call" | custom-call | tf_op jit(solution)/shard_map/pallas_call | solution.py:26
  60.9 16.8 %all_to_all.10 = bf16[32,72,128]{2,1,0:T(8,128)(2,1)S(1)} all-to-all(bf16[32,72,128]{2,1,0:T(8,128)(2,1)S(1)} %bitcast.15), channel_id=1, replica_groups=mesh['grp'=32,'ep'=2,'tp'=2] {'grp'}, dimensions={0} | all-to-all | bytes 1179648 | tf_op jit(solution)/shard_map/all_to_all | solution.py:372
  77.8 3.1 %collective-permute-start.3 = (f32[72,128]{1,0:T(8,128)S(1)}, f32[72,128]{1,0:T(8,128)S(1)}, u32[]{:S(2)}, u32[]{:S(2)}) collective-permute-start(f32[72,128]{1,0:T(8,128)S(1)} %convert_reduce_fusion.own_ref), channel_id=1, source_target_pairs={{0,2},{2,0},{1,3},{3,1},{4,6},{6,4},{5,7},{7,5},{8,10},{10,8},{9,1... | collective-permute-start | bytes 110600 | tf_op jit(solution)/shard_map/ppermute | solution.py:374
  81.0 0.9 %collective-permute-done.3.other_ref = f32[72,128]{1,0:T(8,128)S(1)} collective-permute-done((f32[72,128]{1,0:T(8,128)S(1)}, f32[72,128]{1,0:T(8,128)S(1)}, u32[]{:S(2)}, u32[]{:S(2)}) %collective-permute-start.3) | collective-permute-done | bytes 36896 | tf_op jit(solution)/shard_map/ppermute | solution.py:374
  81.9 0.6 shard_map.141
  (25 shorter events, 0.6 us)
Async XLA Ops:
  0.7 1.0 %copy-start.4 = (bf16[1,512,512]{2,1,0:T(8,128)(2,1)S(1)}, bf16[1,512,512]{2,1,0:T(8,128)(2,1)}, u32[]{:S(2)}) copy-start(bf16[1,512,512]{2,1,0:T(8,128)(2,1)} %param.17) | copy-start | bytes 1572868
  1.7 1.0 %copy-start.5 = (bf16[1,512,512]{2,1,0:T(8,128)(2,1)S(1)}, bf16[1,512,512]{2,1,0:T(8,128)(2,1)}, u32[]{:S(2)}) copy-start(bf16[1,512,512]{2,1,0:T(8,128)(2,1)} %param.18) | copy-start | bytes 1572868
  2.7 0.7 copy-start.8
  3.5 0.7 copy-start.10
  4.2 0.7 copy-start.11
  4.8 15.2 %copy-start.7 = (bf16[3,1,3072]{2,0,1:T(4,128)(2,1)S(1)}, bf16[3,1,3072]{2,0,1:T(4,128)(2,1)}, u32[]{:S(2)}) copy-start(bf16[3,1,3072]{2,0,1:T(4,128)(2,1)} %param.20) | copy-start | bytes 55300
  4.9 27.5 %copy-start.12 = (s32[3,32,2]{1,2,0:T(2,128)S(1)}, s32[3,32,2]{1,2,0:T(2,128)}, u32[]{:S(2)}) copy-start(s32[3,32,2]{1,2,0:T(2,128)} %param.24) | copy-start | bytes 2308
  4.9 41.1 %copy-start.6 = (bf16[3072,8]{0,1:T(8,128)(2,1)S(1)}, bf16[3072,8]{0,1:T(8,128)(2,1)}, u32[]{:S(2)}) copy-start(bf16[3072,8]{0,1:T(8,128)(2,1)} %param.23) | copy-start | bytes 147460
  4.9 41.1 %copy-start.9 = (f32[3072]{0:T(1024)S(1)}, f32[3072]{0:T(1024)}, u32[]{:S(2)}) copy-start(f32[3072]{0:T(1024)} %param.22) | copy-start | bytes 36868
  5.4 3.5 %collective-permute-start = (bf16[72,256]{1,0:T(8,128)(2,1)S(1)}, bf16[72,256]{1,0:T(8,128)(2,1)S(1)}, u32[]{:S(2)}, u32[]{:S(2)}) collective-permute-start(bf16[72,256]{1,0:T(8,128)(2,1)S(1)} %shard_map.137.own_ref), channel_id=1, source_target_pairs={{0,1},{1,0},{2,3},{3,2},{4,5},{5,4},{6,7},{7,6},{8,9},{9,8},{10,11... | collective-permute-start | bytes 110600 | tf_op jit(solution)/shard_map/ppermute | solution.py:322
  8.9 6.4 %copy-start = (bf16[3072,3072]{1,0:T(8,128)(2,1)S(1)}, bf16[3072,3072]{1,0:T(8,128)(2,1)}, u32[]{:S(2)}) copy-start(bf16[3072,3072]{1,0:T(8,128)(2,1)} %weight_ref.1) | copy-start | bytes 56623108
  18.0 2.8 %collective-permute-start.1 = (bf16[72,128]{1,0:T(8,128)(2,1)S(1)}, bf16[72,128]{1,0:T(8,128)(2,1)S(1)}, u32[]{:S(2)}, u32[]{:S(2)}) collective-permute-start(bf16[72,128]{1,0:T(8,128)(2,1)S(1)} %shard_map.138), channel_id=1, source_target_pairs={{0,2},{2,0},{1,3},{3,1},{4,6},{6,4},{5,7},{7,5},{8,10},{10,8},{9,1... | collective-permute-start | bytes 55304 | tf_op jit(solution)/shard_map/ppermute | solution.py:334
  21.8 24.2 %all-to-all-start = ((bf16[32,72,128]{2,1,0:T(8,128)(2,1)}), bf16[32,72,128]{2,1,0:T(8,128)(2,1)S(1)}, u32[]{:S(2)}, u32[]{:S(2)}) async-start(bf16[32,72,128]{2,1,0:T(8,128)(2,1)} %broadcast_in_dim.4), calls=%async_computation | async-start | bytes 1179648 | tf_op jit(solution)/shard_map/all_to_all | solution.py:336
  46.0 2.8 %copy-start.1 = (bf16[4,3072,256]{2,1,0:T(8,128)(2,1)S(1)}, bf16[4,3072,256]{2,1,0:T(8,128)(2,1)}, u32[]{:S(2)}) copy-start(bf16[4,3072,256]{2,1,0:T(8,128)(2,1)} %gate_ref.1) | copy-start | bytes 18874372
  48.8 2.8 %copy-start.2 = (bf16[4,3072,256]{2,1,0:T(8,128)(2,1)S(1)}, bf16[4,3072,256]{2,1,0:T(8,128)(2,1)}, u32[]{:S(2)}) copy-start(bf16[4,3072,256]{2,1,0:T(8,128)(2,1)} %up_ref.1) | copy-start | bytes 18874372
  51.6 7.8 %copy-start.3 = (bf16[4,256,3072]{2,1,0:T(8,128)(2,1)S(1)}, bf16[4,256,3072]{2,1,0:T(8,128)(2,1)}, u32[]{:S(2)}) copy-start(bf16[4,256,3072]{2,1,0:T(8,128)(2,1)} %down_ref.1) | copy-start | bytes 18874372
  54.6 4.8 %collective-permute-start.2 = (bf16[208,512]{1,0:T(8,128)(2,1)S(1)}, bf16[208,512]{1,0:T(8,128)(2,1)S(1)}, u32[]{:S(2)}, u32[]{:S(2)}) collective-permute-start(bf16[208,512]{1,0:T(8,128)(2,1)S(1)} %shard_map.139.own_ref), channel_id=1, source_target_pairs={{0,1},{1,0},{2,3},{3,2},{4,5},{5,4},{6,7},{7,6},{8,9},{9,8},{10,11... | collective-permute-start | bytes 638984 | tf_op jit(solution)/shard_map/ppermute | solution.py:360
  77.8 4.0 %collective-permute-start.3 = (f32[72,128]{1,0:T(8,128)S(1)}, f32[72,128]{1,0:T(8,128)S(1)}, u32[]{:S(2)}, u32[]{:S(2)}) collective-permute-start(f32[72,128]{1,0:T(8,128)S(1)} %convert_reduce_fusion.own_ref), channel_id=1, source_target_pairs={{0,2},{2,0},{1,3},{3,1},{4,6},{6,4},{5,7},{7,5},{8,10},{10,8},{9,1... | collective-permute-start | bytes 110600 | tf_op jit(solution)/shard_map/ppermute | solution.py:374

commit v2 on v1

v2 whole, which is shorter than its diff:
```python
import functools

import jax
import jax.numpy as jnp
from jax import lax
from jax.experimental import pallas as pl
from jax.experimental.pallas import tpu as pltpu
from jax.sharding import PartitionSpec as P

D = 6144
HD = 128
E = 8
CAP = 48
PAIRS = 2
STEPS = 3
LANES = 128

far_below = -1e30
epsilon = 1e-05
VMEM = pl.BlockSpec(memory_space=pltpu.VMEM)
SMEM = pl.BlockSpec(memory_space=pltpu.SMEM)
swap = [(0, 1), (1, 0)]
f32 = jnp.float32
bf16 = jnp.bfloat16


def call(kernel, out, operands, specs, scratch=(), limit=4, beside=0):
    return pl.pallas_call(
        kernel,
        out_shape=out,
        in_specs=specs,
        out_specs=jax.tree.map(lambda _: VMEM, out),
        scratch_shapes=scratch,
        compiler_params=pltpu.CompilerParams(vmem_limit_bytes=limit * 2**20),
        cost_estimate=pl.CostEstimate(
            flops=beside * 10**9, bytes_accessed=0, transcendentals=0
        )
        if beside
        else None,
    )(*operands)


def iota(shape, dim):
    return lax.broadcasted_iota(jnp.int32, shape, dim)


def pieces(value):
    high = value.astype(bf16).astype(f32)
    rest = value - high
    middle = rest.astype(bf16).astype(f32)
    return high, middle, rest - middle


def mask_kernel(length_ref, out_ref):
    cached = out_ref.shape[1]
    place = iota(out_ref.shape, 1) + lax.axis_index("tp") * cached
    out_ref[...] = jnp.where(place < length_ref[0], 1.0, 0.0)


def rows_kernel(residual_ref, routes_ref, rows_ref, routes_row_ref, tables_ref, turned_ref):
    steps, width = residual_ref.shape
    groups = routes_ref.shape[2]
    for k in range(width // LANES):
        rows_ref[k * steps : (k + 1) * steps, :] = residual_ref[
            :, k * LANES : (k + 1) * LANES
        ].astype(f32)
    routes_row_ref[...] = jnp.full(routes_row_ref.shape, -1, jnp.int32)
    for s in range(steps):
        routes_row_ref[:, s * groups : (s + 1) * groups] = routes_ref[s]
    count = E // 2
    wanted = iota((E, LANES), 0) + lax.axis_index("ep") * count
    ones = jnp.where(
        (routes_row_ref[0:1, :] == wanted) | (routes_row_ref[1:2, :] == wanted), 1.0, 0.0
    )
    earlier = jnp.where(iota((LANES, LANES), 0) < iota((LANES, LANES), 1), 1.0, 0.0)
    place = jnp.dot(
        ones.astype(bf16), earlier.astype(bf16), preferred_element_type=f32
    ).astype(jnp.int32)
    slot = iota((CAP, LANES), 0)
    for pair in range(PAIRS):
        table = jnp.concatenate(
            [
                jnp.where(place[e : e + 1, :] == slot, ones[e : e + 1, :], 0.0)
                for e in (2 * pair, 2 * pair + 1)
            ]
            + [jnp.zeros((LANES - 2 * CAP, LANES), f32)],
            axis=0,
        )
        tables_ref[pair] = table.astype(bf16)
        turned_ref[pair] = table.T.astype(bf16)


def attention_kernel(
    mask_ref, query_ref, key_ref, value_ref, new_key_ref, new_value_ref, out_ref, rows_ref
):
    steps = query_ref.shape[0]
    heads = query_ref.shape[1] // HD
    kv = key_ref.shape[1] // HD
    rows = heads * steps
    per_kv = rows // kv
    part = lax.axis_index("tp")
    for h in range(heads):
        rows_ref[h * steps : (h + 1) * steps, :] = query_ref[:, h * HD : (h + 1) * HD].astype(f32)
    query = rows_ref[...]
    row = iota((rows, 1), 0)
    owner = [(row >= k * per_kv) & (row < (k + 1) * per_kv) for k in range(kv)]
    step = row % steps
    scale = HD ** (-0.5)
    spread = jnp.concatenate(
        [jnp.where(owner[k], query, 0.0).astype(bf16) for k in range(kv)], axis=1
    )
    scores = (
        lax.dot_general(
            spread, key_ref[...], (((1,), (1,)), ((), ())), preferred_element_type=f32
        )
        * scale
    )
    allowed = mask_ref[0:1, :] > 0.0
    scores = jnp.where(allowed, scores, far_below)
    new_key = new_key_ref[...].astype(f32)

    def chosen(wide, t):
        out = jnp.zeros((rows, HD), f32)
        for k in range(kv):
            out = jnp.where(owner[k], wide[t : t + 1, k * HD : (k + 1) * HD], out)
        return out

    fresh_ok = [(step >= t) & (part == 0) for t in range(steps)]
    fresh = [
        jnp.where(
            fresh_ok[t],
            jnp.sum(query * chosen(new_key, t), axis=1, keepdims=True) * scale,
            far_below,
        )
        for t in range(steps)
    ]
    highest = jnp.max(scores, axis=1, keepdims=True)
    for t in range(steps):
        highest = jnp.maximum(highest, fresh[t])
    exponent = jnp.where(allowed, jnp.exp(scores - highest), 0.0)
    totals = jnp.sum(exponent, axis=1, keepdims=True)
    new_value = new_value_ref[...].astype(f32)
    wide = jnp.dot(exponent.astype(bf16), value_ref[...], preferred_element_type=f32)
    weighted = jnp.zeros((rows, HD), f32)
    for k in range(kv):
        weighted = jnp.where(owner[k], wide[:, k * HD : (k + 1) * HD], weighted)
    for t in range(steps):
        term = jnp.where(fresh_ok[t], jnp.exp(fresh[t] - highest), 0.0)
        totals = totals + term
        weighted = weighted + term.astype(bf16).astype(f32) * chosen(new_value, t)
    present = totals > 0.0
    safe = jnp.where(present, totals, 1.0)
    out_ref[:, :HD] = (weighted / safe).astype(bf16)
    level = jnp.where(present, highest + jnp.log(safe), far_below)
    high, middle, low = pieces(level)
    lane = iota((rows, LANES), 1)
    out_ref[:, HD:] = jnp.where(lane == 0, high, jnp.where(lane == 1, middle, low)).astype(bf16)


def project_kernel(own_ref, other_ref, weight_ref, out_ref, rows_ref):
    steps = 3
    heads = weight_ref.shape[0] // HD

    def read(ref):
        tail = ref[:, HD:].astype(f32)
        return ref[:, :HD].astype(f32), tail[:, 0:1] + tail[:, 1:2] + tail[:, 2:3]

    own, own_level = read(own_ref)
    other, other_level = read(other_ref)
    top = jnp.maximum(own_level, other_level)
    own_factor = jnp.exp(own_level - top)
    other_factor = jnp.exp(other_level - top)
    rows_ref[...] = (own * own_factor + other * other_factor) / (own_factor + other_factor)
    attended = jnp.concatenate(
        [rows_ref[h * steps : (h + 1) * steps, :] for h in range(heads)], axis=1
    ).astype(bf16)
    terms = jnp.dot(attended, weight_ref[...], preferred_element_type=f32)
    for k in range(heads):
        rows_ref[k * steps : (k + 1) * steps, :] = terms[:, k * LANES : (k + 1) * LANES]
    out_ref[...] = rows_ref[...].astype(bf16)


def pack_pair(pair, scaled, tables_ref, gate_ref, up_ref, out_ref, both_ref):
    tokens = scaled.shape[0]
    width = gate_ref.shape[2]
    both_ref[tokens:, :] = jnp.zeros((LANES - tokens, 2 * width), bf16)
    for i in range(2):
        e = 2 * pair + i
        both_ref[:tokens, :width] = jnp.dot(
            scaled, gate_ref[e], preferred_element_type=f32
        ).astype(bf16)
        both_ref[:tokens, width:] = jnp.dot(scaled, up_ref[e], preferred_element_type=f32).astype(
            bf16
        )
        out_ref[i * CAP : (i + 1) * CAP, :] = jnp.dot(
            tables_ref[pair, i * CAP : (i + 1) * CAP, :],
            both_ref[...],
            preferred_element_type=f32,
        ).astype(bf16)


def hidden_kernel(
    state_ref, gain_ref, router_ref, tables_ref, gate_ref, up_ref, out_ref, scaled_ref, wide_ref, both_ref
):
    tokens, width = scaled_ref.shape
    blocks = width // LANES
    stride = STEPS * blocks
    groups = state_ref.shape[0] // stride
    wide_ref[...] = state_ref[...].astype(f32)
    squares = [jnp.zeros((groups, LANES), f32) for _ in range(STEPS)]
    for k in range(blocks):
        gain = gain_ref[:, k * LANES : (k + 1) * LANES]
        for s in range(STEPS):
            block = wide_ref[pl.ds(k * STEPS + s, groups, stride=stride), :]
            squares[s] = squares[s] + block * block
            scaled_ref[s * groups : (s + 1) * groups, k * LANES : (k + 1) * LANES] = (
                block * gain
            ).astype(bf16)
    scaled = scaled_ref[...]
    pack_pair(0, scaled, tables_ref, gate_ref, up_ref, out_ref, both_ref)
    square = jnp.sum(jnp.concatenate(squares, axis=0), axis=1, keepdims=True)
    diagonal = iota((tokens, LANES), 0) == iota((tokens, LANES), 1)
    square = jnp.sum(jnp.where(diagonal, square, 0.0), axis=0, keepdims=True)
    router = lax.dot_general(
        router_ref[...], scaled, (((1,), (1,)), ((), ())), preferred_element_type=f32
    )
    router = jnp.concatenate([router, jnp.zeros((E, LANES - tokens), f32)], axis=1)
    high, middle, _ = pieces(router)
    square_high, square_middle, _ = pieces(square)
    line = iota((E, LANES), 0)
    extra = jnp.concatenate(
        [
            high,
            middle,
            jnp.where(line == 0, square_high, jnp.where(line == 1, square_middle, 0.0)),
            jnp.zeros((E, LANES), f32),
        ],
        axis=1,
    )
    extra = jnp.concatenate([extra, jnp.zeros((8, 4 * LANES), f32)], axis=0)
    out_ref[2 * CAP :, :] = extra.astype(bf16)


def hidden_rest_kernel(scaled_ref, tables_ref, gate_ref, up_ref, out_ref, both_ref):
    pack_pair(1, scaled_ref[...], tables_ref, gate_ref, up_ref, out_ref, both_ref)


def spread_pair(own_ref, other_ref, factors, turned, side_ref, tokens):
    width = side_ref.shape[1] // 2
    side_ref[...] = jnp.zeros(side_ref.shape, bf16)
    both = own_ref[: 2 * CAP, :].astype(f32) + other_ref[: 2 * CAP, :].astype(f32)
    both = both * factors[:, 0:1]
    gate, up = both[:, :width], both[:, width:]
    activated = (gate / (1.0 + jnp.exp(-gate)) * up).astype(bf16).astype(f32)
    weighted = (activated * factors[:, 1:2]).astype(bf16)
    for i in range(2):
        side_ref[i * CAP : (i + 1) * CAP, i * width : (i + 1) * width] = weighted[
            i * CAP : (i + 1) * CAP, :
        ]
    return jnp.dot(turned[:tokens, :], side_ref[...], preferred_element_type=f32).astype(bf16)


def down_kernel(
    own_ref, other_ref, routes_ref, tables_ref, turned_ref, down_ref, terms_ref, factors_ref, side_ref
):
    tokens = terms_ref.shape[0]
    width = down_ref.shape[1]
    tail = own_ref[2 * CAP :, :].astype(f32) + other_ref[2 * CAP :, :].astype(f32)
    square = tail[0:1, 2 * LANES : 3 * LANES] + tail[1:2, 2 * LANES : 3 * LANES]
    inverse = lax.rsqrt(square / D + epsilon)
    logits = (tail[:E, :LANES] + tail[:E, LANES : 2 * LANES]) * inverse
    every = iota((E, LANES), 0)
    picked = [
        jnp.sum(jnp.where(routes_ref[c : c + 1, :] == every, logits, 0.0), axis=0, keepdims=True)
        for c in range(2)
    ]
    top = jnp.maximum(picked[0], picked[1])
    raised = [jnp.exp(p - top) for p in picked]
    total = raised[0] + raised[1]
    shares = [r / total for r in raised]
    first = lax.axis_index("ep") * (2 * PAIRS)

    def factors_of(pair):
        slots = []
        for i in range(2):
            share = jnp.zeros((1, LANES), f32)
            for c in range(2):
                share = share + jnp.where(
                    routes_ref[c : c + 1, :] == first + 2 * pair + i, shares[c], 0.0
                )
            slots.append(jnp.broadcast_to(share, (CAP, LANES)))
        table = tables_ref[pair, : 2 * CAP, :].astype(f32)
        slot_inverse = jnp.sum(table * inverse, axis=1, keepdims=True)
        slot_share = jnp.sum(table * jnp.concatenate(slots, axis=0), axis=1, keepdims=True)
        return jnp.where(iota((2 * CAP, LANES), 1) == 0, slot_inverse, slot_share)

    factors_ref[...] = factors_of(1)
    mixed = spread_pair(own_ref, other_ref, factors_of(0), turned_ref[0], side_ref, tokens)
    terms_ref[...] = sum(
        jnp.dot(
            mixed[:, e * width : (e + 1) * width], down_ref[e], preferred_element_type=f32
        )
        for e in range(2)
    )


def down_rest_kernel(
    own_ref, other_ref, terms_ref, factors_ref, turned_ref, down_ref, out_ref, side_ref, wide_ref
):
    tokens = terms_ref.shape[0]
    width = down_ref.shape[1]
    blocks = down_ref.shape[2] // LANES
    stride = STEPS * blocks
    groups = tokens // STEPS
    mixed = spread_pair(own_ref, other_ref, factors_ref[...], turned_ref[1], side_ref, tokens)
    chunk = 4 * LANES
    for n in range(down_ref.shape[2] // chunk):
        terms = terms_ref[:, n * chunk : (n + 1) * chunk]
        for i in range(2):
            terms = terms + jnp.dot(
                mixed[:, i * width : (i + 1) * width],
                down_ref[2 + i, :, n * chunk : (n + 1) * chunk],
                preferred_element_type=f32,
            )
        for j in range(chunk // LANES):
            k = n * (chunk // LANES) + j
            for s in range(STEPS):
                wide_ref[pl.ds(k * STEPS + s, groups, stride=stride), :] = terms[
                    s * groups : (s + 1) * groups, j * LANES : (j + 1) * LANES
                ]
    out_ref[...] = wide_ref[...].astype(bf16)


def output_kernel(state_ref, own_ref, other_ref, out_ref, rows_ref):
    steps, width = out_ref.shape
    rows_ref[...] = state_ref[...].astype(f32) + (own_ref[...] + other_ref[...])
    for k in range(width // LANES):
        out_ref[:, k * LANES : (k + 1) * LANES] = rows_ref[k * steps : (k + 1) * steps, :].astype(
            bf16
        )


def on_device(
    queries,
    new_keys,
    new_values,
    cache_keys,
    cache_values,
    lengths,
    residual,
    out_weight,
    norm_gain,
    router_weight,
    routes,
    expert_gate,
    expert_up,
    expert_down,
):
    groups = lax.axis_size("grp")
    steps, _, query_width = queries.shape
    rows = steps * query_width // HD
    struct = jax.ShapeDtypeStruct
    token_count = groups * steps
    width = residual.shape[2]
    kv_width = cache_keys.shape[2]
    cached = cache_keys.shape[1]
    mask = call(mask_kernel, struct((8, cached), f32), (lengths,), [SMEM], beside=3)
    partial = call(
        attention_kernel,
        struct((rows, 2 * HD), bf16),
        (
            mask,
            queries.reshape(steps, query_width),
            cache_keys.reshape(cached, kv_width),
            cache_values.reshape(cached, kv_width),
            new_keys.reshape(steps, kv_width),
            new_values.reshape(steps, kv_width),
        ),
        [VMEM] * 6,
        [pltpu.VMEM((rows, HD), f32)],
        beside=7,
    )
    square = struct((PAIRS, LANES, LANES), bf16)
    residual_rows, routes_row, tables, turned = call(
        rows_kernel,
        (struct((rows, LANES), f32), struct((2, LANES), jnp.int32), square, square),
        (residual.reshape(steps, width), routes.transpose(0, 2, 1)),
        [VMEM] * 2,
    )
    other = lax.ppermute(partial, "tp", swap)
    terms = call(
        project_kernel,
        struct((rows, LANES), bf16),
        (partial, other, out_weight),
        [VMEM] * 3,
        [pltpu.VMEM((rows, LANES), f32)],
        beside=20,
    )
    other_terms = lax.ppermute(terms, "ep", swap)
    state = (residual_rows + (terms.astype(f32) + other_terms.astype(f32))).astype(bf16)
    all_state = lax.all_to_all(
        jnp.broadcast_to(state[None], (groups, rows, LANES)), "grp", 0, 0
    ).reshape(groups * rows, LANES)
    hidden_width = 2 * expert_gate.shape[2]
    both = pltpu.VMEM((LANES, hidden_width), bf16)
    hidden, scaled = call(
        hidden_kernel,
        (struct((2 * CAP + 16, hidden_width), bf16), struct((token_count, width), bf16)),
        (
            all_state,
            norm_gain.reshape(1, -1),
            router_weight.T,
            tables,
            expert_gate,
            expert_up,
        ),
        [VMEM] * 6,
        [pltpu.VMEM((groups * rows, LANES), f32), both],
        limit=8,
    )
    other_hidden = lax.ppermute(hidden, "tp", swap)
    hidden_rest = call(
        hidden_rest_kernel,
        struct((2 * CAP, hidden_width), bf16),
        (scaled, tables, expert_gate, expert_up),
        [VMEM] * 4,
        [both],
    )
    other_hidden_rest = lax.ppermute(hidden_rest, "tp", swap)
    side = pltpu.VMEM((LANES, hidden_width), bf16)
    down_terms, factors = call(
        down_kernel,
        (struct((token_count, width), f32), struct((2 * CAP, LANES), f32)),
        (hidden, other_hidden, routes_row, tables, turned, expert_down),
        [VMEM] * 6,
        [side],
        limit=8,
    )
    sent = call(
        down_rest_kernel,
        struct((groups * rows, LANES), bf16),
        (hidden_rest, other_hidden_rest, down_terms, factors, turned, expert_down),
        [VMEM] * 6,
        [side, pltpu.VMEM((groups * rows, LANES), f32)],
        limit=8,
    )
    received = lax.all_to_all(sent.reshape(groups, rows, LANES), "grp", 0, 0)
    summed = jnp.sum(received.astype(f32), axis=0)
    other_summed = lax.ppermute(summed, "ep", swap)
    mixed = call(
        output_kernel,
        struct((steps, width), bf16),
        (state, summed, other_summed),
        [VMEM] * 3,
        [pltpu.VMEM((rows, LANES), f32)],
    )
    return mixed[:, None]


def solution(mesh):
    in_specs = (
        P(None, "grp", "ep"),
        P(None, "grp", "ep"),
        P(None, "grp", "ep"),
        P("grp", "tp", "ep"),
        P("grp", "tp", "ep"),
        P("grp"),
        P(None, "grp", "tp"),
        P("ep", "tp"),
        P("tp"),
        P("tp", None),
        P(),
        P("ep", "tp", "grp"),
        P("ep", "tp", "grp"),
        P("ep", "grp", "tp"),
    )
    out_specs = P(None, "grp", "tp")
    return jax.shard_map(
        on_device, mesh=mesh, in_specs=in_specs, out_specs=out_specs, check_vma=False
    )
```

time: 83.1 us -> 66.5 us (0.80)
  blocking collectives: 16.8 us -> 39.5 us
  waiting for transfers between devices: 20.9 us -> 5.15 us
  local copies, waits for them, and re-layouts: 17.1 us -> 2.47 us
  starting transfers between devices: 18.2 us -> 8.86 us
    all_to_all x0 -> x1, blocking collectives: none -> 24 us  [on_device(): lax.all_to_all(jnp.broadcast_to(state[None], (groups, rows, LANES)), 'grp...]
    unnamed x27 -> x32, local copies, waits for them, and re-layouts: 16.1 us -> 2.39 us
    all_to_all x1 -> x0, waiting for transfers between devices: 13.5 us -> none  [on_device(): lax.all_to_all(jnp.broadcast_to(state[None], (groups, rows, LANES)), 'grp...]
    all_to_all x1 -> x0, starting transfers between devices: 10.6 us -> none  [on_device(): lax.all_to_all(jnp.broadcast_to(state[None], (groups, rows, LANES)), 'grp...]
    ppermute x1, waiting for transfers between devices: 4.39 us -> 0.64 us  [on_device(): other_hidden = lax.ppermute(hidden, 'tp', swap)]
    ppermute x0 -> x1, waiting for transfers between devices: none -> 1.75 us  [on_device(): other_hidden_rest = lax.ppermute(hidden_rest, 'tp', swap)]
    all_to_all x1, blocking collectives: 16.8 us -> 15.5 us  [on_device(): received = lax.all_to_all(sent.reshape(groups, rows, LANES), 'grp', 0, 0)]
    ppermute x0 -> x1, starting transfers between devices: none -> 1.24 us  [on_device(): other_hidden_rest = lax.ppermute(hidden_rest, 'tp', swap)]
  transfers between devices with their start and end apart: 5 -> 5, of which waited for: 5 -> 5; matrix products, arithmetic and copies ran while one was open for 0% -> 0% of each run, Pallas kernels for 0% -> 4%
where the time goes in v2:
time: 66.5 us; the launch traced here: 66.3 us
  blocking collectives  39.5 us (59%)
  Pallas kernels  9.29 us (14%)
  starting transfers between devices  8.86 us (13%)
  waiting for transfers between devices  5.15 us (8%)
  local copies, waits for them, and re-layouts  2.47 us (4%)
  between operations  0.94 us (1%)
    all_to_all x1, blocking collectives, on_device(): lax.all_to_all(jnp.broadcast_to(state[None], (groups, rows, LANES)), 'grp...  24 us
    all_to_all x1, blocking collectives, on_device(): received = lax.all_to_all(sent.reshape(groups, rows, LANES), 'grp', 0, 0)  15.5 us
    pallas_call x9, Pallas kernels, call(): pl.pallas_call(kernel, out_shape=out, in_specs=specs, out_specs=jax.tree....  9.29 us
    ppermute x1, starting transfers between devices, on_device(): other_summed = lax.ppermute(summed, 'ep', swap)  3.69 us
    unnamed x32, local copies, waits for them, and re-layouts  2.39 us
    ppermute x1, starting transfers between devices, on_device(): other = lax.ppermute(partial, 'tp', swap)  2.12 us
    ppermute x1, waiting for transfers between devices, on_device(): other_hidden_rest = lax.ppermute(hidden_rest, 'tp', swap)  1.75 us
    ppermute x1, starting transfers between devices, on_device(): other_terms = lax.ppermute(terms, 'ep', swap)  1.42 us
  transfers between devices with their start and end apart: 5, of which 5 were waited for; matrix products, arithmetic and copies ran while one was open for 0% of the time, Pallas kernels for 4%

profile of v2, /device:TPU:1, one launch (start us, length us, event | category | flops | bytes accessed | tf_op | source)
XLA Modules:
  0.0 66.3 jit_solution(7898607554406170853)
XLA Ops:
  0.8 0.3 copy-done.6
  1.1 0.2 copy-done.5
  1.2 0.6 shard_map.138.own_ref
  1.9 2.1 %collective-permute-start = (bf16[72,256]{1,0:T(8,128)(2,1)S(1)}, bf16[72,256]{1,0:T(8,128)(2,1)S(1)}, u32[]{:S(2)}, u32[]{:S(2)}) collective-permute-start(bf16[72,256]{1,0:T(8,128)(2,1)S(1)} %shard_map.138.own_ref), channel_id=1, source_target_pairs={{0,1},{1,0},{2,3},{3,2},{4,5},{5,4},{6,7},{7,6},{8,9},{9,8},{10,11... | collective-permute-start | bytes 110600 | tf_op jit(solution)/shard_map/ppermute | solution.py:390
  4.0 1.3 %collective-permute-done.other_ref = bf16[72,256]{1,0:T(8,128)(2,1)S(1)} collective-permute-done((bf16[72,256]{1,0:T(8,128)(2,1)S(1)}, bf16[72,256]{1,0:T(8,128)(2,1)S(1)}, u32[]{:S(2)}, u32[]{:S(2)}) %collective-permute-start) | collective-permute-done | bytes 36896 | tf_op jit(solution)/shard_map/ppermute | solution.py:390
  5.4 1.9 %copy-done.4 = bf16[3072,3072]{1,0:T(8,128)(2,1)S(1)} copy-done((bf16[3072,3072]{1,0:T(8,128)(2,1)S(1)}, bf16[3072,3072]{1,0:T(8,128)(2,1)}, u32[]{:S(2)}) %copy-start.4) | copy-done | bytes 18874392
  7.2 2.8 %shard_map.139 = bf16[72,128]{1,0:T(8,128)(2,1)S(1)} custom-call(bf16[72,256]{1,0:T(8,128)(2,1)S(1)} %shard_map.138.own_ref, bf16[72,256]{1,0:T(8,128)(2,1)S(1)} %collective-permute-done.other_ref, bf16[3072,3072]{1,0:T(8,128)(2,1)S(1)} %copy-done.4), custom_call_target="tpu_custom_call" | custom-call | flops 20000000000 | tf_op jit(solution)/shard_map/pallas_call | solution.py:28
  10.0 1.4 %collective-permute-start.1 = (bf16[72,128]{1,0:T(8,128)(2,1)S(1)}, bf16[72,128]{1,0:T(8,128)(2,1)S(1)}, u32[]{:S(2)}, u32[]{:S(2)}) collective-permute-start(bf16[72,128]{1,0:T(8,128)(2,1)S(1)} %shard_map.139), channel_id=1, source_target_pairs={{0,2},{2,0},{1,3},{3,1},{4,6},{6,4},{5,7},{7,5},{8,10},{10,8},{9,1... | collective-permute-start | bytes 55304 | tf_op jit(solution)/shard_map/ppermute | solution.py:399
  11.4 0.3 shard_map.136
  11.7 0.5 collective-permute-done.1
  12.4 24.0 %all_to_all.10 = bf16[32,72,128]{2,1,0:T(8,128)(2,1)S(1)} all-to-all(bf16[32,72,128]{2,1,0:T(8,128)(2,1)S(1)} %broadcast_in_dim.4), channel_id=1, replica_groups=mesh['grp'=32,'ep'=2,'tp'=2] {'grp'}, dimensions={0} | all-to-all | bytes 1179648 | tf_op jit(solution)/shard_map/all_to_all | solution.py:401
  36.4 1.7 %shard_map.140 = (bf16[112,512]{1,0:T(8,128)(2,1)S(1)}, bf16[96,3072]{1,0:T(8,128)(2,1)S(1)}) custom-call(bf16[2304,128]{1,0:T(8,128)(2,1)S(1)} %bitcast.19, f32[1,3072]{1,0:T(1,128)S(1)} %bitcast.22, bf16[8,3072]{1,0:T(8,128)(2,1)S(1)} %bitcast.20, bf16[2,128,128]{2,1,0:T(8,128)(2,1)S(1)} %get-tuple-element.14.tables_ref, ...), custom_call_target="tpu_custom_call" | custom-call | tf_op jit(solution)/shard_map/pallas_call | solution.py:28
  38.2 0.4 collective-permute-start.3
  38.6 1.4 %shard_map.141.own_ref = bf16[96,512]{1,0:T(8,128)(2,1)S(1)} custom-call(bf16[96,3072]{1,0:T(8,128)(2,1)S(1)} %get-tuple-element.15.scaled_ref, bf16[2,128,128]{2,1,0:T(8,128)(2,1)S(1)} %get-tuple-element.14.tables_ref, bf16[4,3072,256]{2,1,0:T(8,128)(2,1)S(1)} %bitcast.13, bf16[4,3072,256]{2,1,0:T(8,128)(2,1)S(1)} %bitcast.15), custom_call_target="tpu_custom_call" | custom-call | tf_op jit(solution)/shard_map/pallas_call | solution.py:28
  40.0 1.2 %collective-permute-start.2 = (bf16[96,512]{1,0:T(8,128)(2,1)S(1)}, bf16[96,512]{1,0:T(8,128)(2,1)S(1)}, u32[]{:S(2)}, u32[]{:S(2)}) collective-permute-start(bf16[96,512]{1,0:T(8,128)(2,1)S(1)} %shard_map.141.own_ref), channel_id=1, source_target_pairs={{0,1},{1,0},{2,3},{3,2},{4,5},{5,4},{6,7},{7,6},{8,9},{9,8},{10,11... | collective-permute-start | bytes 294920 | tf_op jit(solution)/shard_map/ppermute | solution.py:429
  41.3 0.6 collective-permute-done.3.other_ref
  41.9 0.9 %shard_map.142 = (f32[96,3072]{1,0:T(8,128)S(1)}, f32[96,128]{1,0:T(8,128)S(1)}) custom-call(bf16[112,512]{1,0:T(8,128)(2,1)S(1)} %get-tuple-element.16.own_ref, bf16[112,512]{1,0:T(8,128)(2,1)S(1)} %collective-permute-done.3.other_ref, s32[2,128]{1,0:T(2,128)S(1)} %get-tuple-element.17.routes_ref, bf16[2,128,128]{2,1,0:T(8,128)(2,1)S(1)} %get-tuple-element.14.tables_ref, ...), custom_call_target="tpu_custom_call" | custom-call | tf_op jit(solution)/shard_map/pallas_call | solution.py:28
  42.9 1.8 %collective-permute-done.2.other_ref = bf16[96,512]{1,0:T(8,128)(2,1)S(1)} collective-permute-done((bf16[96,512]{1,0:T(8,128)(2,1)S(1)}, bf16[96,512]{1,0:T(8,128)(2,1)S(1)}, u32[]{:S(2)}, u32[]{:S(2)}) %collective-permute-start.2) | collective-permute-done | bytes 98336 | tf_op jit(solution)/shard_map/ppermute | solution.py:429
  44.6 0.9 %shard_map.143 = bf16[2304,128]{1,0:T(8,128)(2,1)S(1)} custom-call(bf16[96,512]{1,0:T(8,128)(2,1)S(1)} %shard_map.141.own_ref, bf16[96,512]{1,0:T(8,128)(2,1)S(1)} %collective-permute-done.2.other_ref, f32[96,3072]{1,0:T(8,128)S(1)} %get-tuple-element.19.terms_ref, f32[96,128]{1,0:T(8,128)S(1)} %get-tuple-element.20.factors_ref, ...), custom_call_target="tpu_custom_call" | custom-call | tf_op jit(solution)/shard_map/pallas_call | solution.py:28
  45.5 15.5 %all_to_all.11 = bf16[32,72,128]{2,1,0:T(8,128)(2,1)S(1)} all-to-all(bf16[32,72,128]{2,1,0:T(8,128)(2,1)S(1)} %bitcast.18), channel_id=1, replica_groups=mesh['grp'=32,'ep'=2,'tp'=2] {'grp'}, dimensions={0} | all-to-all | bytes 1179648 | tf_op jit(solution)/shard_map/all_to_all | solution.py:447
  61.1 0.1 convert_reduce_fusion.own_ref
  61.2 3.7 %collective-permute-start.4 = (f32[72,128]{1,0:T(8,128)S(1)}, f32[72,128]{1,0:T(8,128)S(1)}, u32[]{:S(2)}, u32[]{:S(2)}) collective-permute-start(f32[72,128]{1,0:T(8,128)S(1)} %convert_reduce_fusion.own_ref), channel_id=1, source_target_pairs={{0,2},{2,0},{1,3},{3,1},{4,6},{6,4},{5,7},{7,5},{8,10},{10,8},{9,1... | collective-permute-start | bytes 110600 | tf_op jit(solution)/shard_map/ppermute | solution.py:449
  64.8 0.9 %collective-permute-done.4.other_ref = f32[72,128]{1,0:T(8,128)S(1)} collective-permute-done((f32[72,128]{1,0:T(8,128)S(1)}, f32[72,128]{1,0:T(8,128)S(1)}, u32[]{:S(2)}, u32[]{:S(2)}) %collective-permute-start.4) | collective-permute-done | bytes 36896 | tf_op jit(solution)/shard_map/ppermute | solution.py:449
  65.7 0.6 shard_map.144
  (35 shorter events, 0.2 us)
Async XLA Ops:
  0.0 1.1 %copy-start.6 = (bf16[1,512,512]{2,1,0:T(8,128)(2,1)S(1)}, bf16[1,512,512]{2,1,0:T(8,128)(2,1)}, u32[]{:S(2)}) copy-start(bf16[1,512,512]{2,1,0:T(8,128)(2,1)} %param.18) | copy-start | bytes 1572868
  0.0 1.2 %copy-start.5 = (bf16[1,512,512]{2,1,0:T(8,128)(2,1)S(1)}, bf16[1,512,512]{2,1,0:T(8,128)(2,1)}, u32[]{:S(2)}) copy-start(bf16[1,512,512]{2,1,0:T(8,128)(2,1)} %param.17) | copy-start | bytes 1572868
  0.0 1.2 %copy-start.9 = (bf16[3,1,512]{2,0,1:T(4,128)(2,1)S(1)}, bf16[3,1,512]{2,0,1:T(4,128)(2,1)}, u32[]{:S(2)}) copy-start(bf16[3,1,512]{2,0,1:T(4,128)(2,1)} %param.16) | copy-start | bytes 9220
  0.0 1.2 %copy-start.8 = (bf16[3,1,512]{2,0,1:T(4,128)(2,1)S(1)}, bf16[3,1,512]{2,0,1:T(4,128)(2,1)}, u32[]{:S(2)}) copy-start(bf16[3,1,512]{2,0,1:T(4,128)(2,1)} %param.15) | copy-start | bytes 9220
  0.0 1.2 %copy-start.7 = (bf16[3,1,3072]{2,0,1:T(4,128)(2,1)S(1)}, bf16[3,1,3072]{2,0,1:T(4,128)(2,1)}, u32[]{:S(2)}) copy-start(bf16[3,1,3072]{2,0,1:T(4,128)(2,1)} %param.14) | copy-start | bytes 55300
  0.8 6.5 %copy-start.4 = (bf16[3072,3072]{1,0:T(8,128)(2,1)S(1)}, bf16[3072,3072]{1,0:T(8,128)(2,1)}, u32[]{:S(2)}) copy-start(bf16[3072,3072]{1,0:T(8,128)(2,1)} %weight_ref.1) | copy-start | bytes 56623108
  1.2 35.2 %slice-start = ((s8[6291456]{0:T(1024)(128)(4,1)}), s8[4194304]{0:T(1024)(128)(4,1)S(1)}, s32[]{:S(2)}) async-start(s8[6291456]{0:T(1024)(128)(4,1)} %bitcast.12), calls=%async_computation.2 | async-start | bytes 8388608
  1.2 35.1 %slice-start.2 = ((s8[6291456]{0:T(1024)(128)(4,1)}), s8[4194304]{0:T(1024)(128)(4,1)S(1)}, s32[]{:S(2)}) async-start(s8[6291456]{0:T(1024)(128)(4,1)} %bitcast.14), calls=%async_computation.4 | async-start | bytes 8388608
  1.8 9.6 %copy-start.1 = (bf16[3,1,3072]{2,0,1:T(4,128)(2,1)S(1)}, bf16[3,1,3072]{2,0,1:T(4,128)(2,1)}, u32[]{:S(2)}) copy-start(bf16[3,1,3072]{2,0,1:T(4,128)(2,1)} %param.20) | copy-start | bytes 55300
  1.8 9.6 %copy-start.3 = (s32[3,32,2]{1,2,0:T(2,128)S(1)}, s32[3,32,2]{1,2,0:T(2,128)}, u32[]{:S(2)}) copy-start(s32[3,32,2]{1,2,0:T(2,128)} %param.24) | copy-start | bytes 2308
  1.8 34.5 %slice-start.1 = ((s8[6291456]{0:T(1024)(128)(4,1)}), s8[2097152]{0:T(1024)(128)(4,1)S(1)}, s32[]{:S(2)}) async-start(s8[6291456]{0:T(1024)(128)(4,1)} %bitcast.12), calls=%async_computation.3 | async-start | bytes 4194304
  1.8 34.5 %slice-start.3 = ((s8[6291456]{0:T(1024)(128)(4,1)}), s8[2097152]{0:T(1024)(128)(4,1)S(1)}, s32[]{:S(2)}) async-start(s8[6291456]{0:T(1024)(128)(4,1)} %bitcast.14), calls=%async_computation.5 | async-start | bytes 4194304
  1.9 34.5 %copy-start = (bf16[3072,8]{0,1:T(8,128)(2,1)S(1)}, bf16[3072,8]{0,1:T(8,128)(2,1)}, u32[]{:S(2)}) copy-start(bf16[3072,8]{0,1:T(8,128)(2,1)} %param.23) | copy-start | bytes 147460
  1.9 34.5 %copy-start.2 = (f32[3072]{0:T(1024)S(1)}, f32[3072]{0:T(1024)}, u32[]{:S(2)}) copy-start(f32[3072]{0:T(1024)} %param.22) | copy-start | bytes 36868
  1.9 3.5 %collective-permute-start = (bf16[72,256]{1,0:T(8,128)(2,1)S(1)}, bf16[72,256]{1,0:T(8,128)(2,1)S(1)}, u32[]{:S(2)}, u32[]{:S(2)}) collective-permute-start(bf16[72,256]{1,0:T(8,128)(2,1)S(1)} %shard_map.138.own_ref), channel_id=1, source_target_pairs={{0,1},{1,0},{2,3},{3,2},{4,5},{5,4},{6,7},{7,6},{8,9},{9,8},{10,11... | collective-permute-start | bytes 110600 | tf_op jit(solution)/shard_map/ppermute | solution.py:390
  10.0 2.3 %collective-permute-start.1 = (bf16[72,128]{1,0:T(8,128)(2,1)S(1)}, bf16[72,128]{1,0:T(8,128)(2,1)S(1)}, u32[]{:S(2)}, u32[]{:S(2)}) collective-permute-start(bf16[72,128]{1,0:T(8,128)(2,1)S(1)} %shard_map.139), channel_id=1, source_target_pairs={{0,2},{2,0},{1,3},{3,1},{4,6},{6,4},{5,7},{7,5},{8,10},{10,8},{9,1... | collective-permute-start | bytes 55304 | tf_op jit(solution)/shard_map/ppermute | solution.py:399
  36.4 5.5 %slice-start.4 = ((s8[6291456]{0:T(1024)(128)(4,1)}), s8[4194304]{0:T(1024)(128)(4,1)S(1)}, s32[]{:S(2)}) async-start(s8[6291456]{0:T(1024)(128)(4,1)} %bitcast.16), calls=%async_computation.6 | async-start | bytes 8388608
  38.2 3.7 %collective-permute-start.3 = (bf16[112,512]{1,0:T(8,128)(2,1)S(1)}, bf16[112,512]{1,0:T(8,128)(2,1)S(1)}, u32[]{:S(2)}, u32[]{:S(2)}) collective-permute-start(bf16[112,512]{1,0:T(8,128)(2,1)S(1)} %get-tuple-element.16.own_ref), channel_id=1, source_target_pairs={{0,1},{1,0},{2,3},{3,2},{4,5},{5,4},{6,7},{7,6},{8,9},{9,8},{10,11... | collective-permute-start | bytes 344072 | tf_op jit(solution)/shard_map/ppermute | solution.py:421
  38.6 3.3 %slice-start.5 = ((s8[6291456]{0:T(1024)(128)(4,1)}), s8[2097152]{0:T(1024)(128)(4,1)S(1)}, s32[]{:S(2)}) async-start(s8[6291456]{0:T(1024)(128)(4,1)} %bitcast.16), calls=%async_computation.7 | async-start | bytes 4194304
  40.0 4.6 %collective-permute-start.2 = (bf16[96,512]{1,0:T(8,128)(2,1)S(1)}, bf16[96,512]{1,0:T(8,128)(2,1)S(1)}, u32[]{:S(2)}, u32[]{:S(2)}) collective-permute-start(bf16[96,512]{1,0:T(8,128)(2,1)S(1)} %shard_map.141.own_ref), channel_id=1, source_target_pairs={{0,1},{1,0},{2,3},{3,2},{4,5},{5,4},{6,7},{7,6},{8,9},{9,8},{10,11... | collective-permute-start | bytes 294920 | tf_op jit(solution)/shard_map/ppermute | solution.py:429
  61.2 4.6 %collective-permute-start.4 = (f32[72,128]{1,0:T(8,128)S(1)}, f32[72,128]{1,0:T(8,128)S(1)}, u32[]{:S(2)}, u32[]{:S(2)}) collective-permute-start(f32[72,128]{1,0:T(8,128)S(1)} %convert_reduce_fusion.own_ref), channel_id=1, source_target_pairs={{0,2},{2,0},{1,3},{3,1},{4,6},{6,4},{5,7},{7,5},{8,10},{10,8},{9,1... | collective-permute-start | bytes 110600 | tf_op jit(solution)/shard_map/ppermute | solution.py:449

commit v3 on v2

--- a/solution.py
+++ b/solution.py
@@ -13,6 +13,7 @@
 CAP = 48
 PAIRS = 2
 STEPS = 3
+PARTS = 4
 LANES = 128
 
 far_below = -1e30
@@ -157,9 +158,9 @@
     out_ref[:, HD:] = jnp.where(lane == 0, high, jnp.where(lane == 1, middle, low)).astype(bf16)
 
 
-def project_kernel(own_ref, other_ref, weight_ref, out_ref, rows_ref):
-    steps = 3
-    heads = weight_ref.shape[0] // HD
+def join_kernel(own_ref, other_ref, attended_ref, rows_ref):
+    steps = attended_ref.shape[0]
+    heads = own_ref.shape[0] // steps
 
     def read(ref):
         tail = ref[:, HD:].astype(f32)
@@ -171,58 +172,79 @@
     own_factor = jnp.exp(own_level - top)
     other_factor = jnp.exp(other_level - top)
     rows_ref[...] = (own * own_factor + other * other_factor) / (own_factor + other_factor)
-    attended = jnp.concatenate(
+    attended_ref[...] = jnp.concatenate(
         [rows_ref[h * steps : (h + 1) * steps, :] for h in range(heads)], axis=1
     ).astype(bf16)
-    terms = jnp.dot(attended, weight_ref[...], preferred_element_type=f32)
-    for k in range(heads):
+
+
+def project_kernel(attended_ref, weight_ref, out_ref, rows_ref):
+    steps = attended_ref.shape[0]
+    terms = jnp.dot(attended_ref[...], weight_ref[...], preferred_element_type=f32)
+    for k in range(weight_ref.shape[1] // LANES):
         rows_ref[k * steps : (k + 1) * steps, :] = terms[:, k * LANES : (k + 1) * LANES]
     out_ref[...] = rows_ref[...].astype(bf16)
 
 
-def pack_pair(pair, scaled, tables_ref, gate_ref, up_ref, out_ref, both_ref):
-    tokens = scaled.shape[0]
+def pack_pair(pair, scaled_refs, tables_ref, gate_ref, up_ref, out_ref, sums_ref, both_ref):
+    tokens, part = scaled_refs[0].shape
     width = gate_ref.shape[2]
-    both_ref[tokens:, :] = jnp.zeros((LANES - tokens, 2 * width), bf16)
+    both_ref[:, tokens:, :] = jnp.zeros((2, LANES - tokens, 2 * width), bf16)
+    last = len(scaled_refs) - 1
+    for n, scaled_ref in enumerate(scaled_refs):
+        scaled = scaled_ref[...]
+        for i in range(2):
+            for j, weight_ref in enumerate((gate_ref, up_ref)):
+                terms = jnp.dot(
+                    scaled,
+                    weight_ref[2 * pair + i, n * part : (n + 1) * part, :],
+                    preferred_element_type=f32,
+                )
+                if n > 0:
+                    terms = terms + sums_ref[2 * i + j]
+                if n < last:
+                    sums_ref[2 * i + j] = terms
+                else:
+                    both_ref[i, :tokens, j * width : (j + 1) * width] = terms.astype(bf16)
     for i in range(2):
-        e = 2 * pair + i
-        both_ref[:tokens, :width] = jnp.dot(
-            scaled, gate_ref[e], preferred_element_type=f32
-        ).astype(bf16)
-        both_ref[:tokens, width:] = jnp.dot(scaled, up_ref[e], preferred_element_type=f32).astype(
-            bf16
-        )
         out_ref[i * CAP : (i + 1) * CAP, :] = jnp.dot(
             tables_ref[pair, i * CAP : (i + 1) * CAP, :],
-            both_ref[...],
+            both_ref[i],
             preferred_element_type=f32,
         ).astype(bf16)
 
 
 def hidden_kernel(
-    state_ref, gain_ref, router_ref, tables_ref, gate_ref, up_ref, out_ref, scaled_ref, wide_ref, both_ref
+    state_ref, gain_ref, router_ref, tables_ref, gate_ref, up_ref, out_ref, *refs
 ):
-    tokens, width = scaled_ref.shape
-    blocks = width // LANES
+    *scaled_refs, wide_ref, sums_ref, both_ref = refs
+    tokens, part = scaled_refs[0].shape
+    blocks = len(scaled_refs) * part // LANES
     stride = STEPS * blocks
     groups = state_ref.shape[0] // stride
     wide_ref[...] = state_ref[...].astype(f32)
     squares = [jnp.zeros((groups, LANES), f32) for _ in range(STEPS)]
     for k in range(blocks):
         gain = gain_ref[:, k * LANES : (k + 1) * LANES]
+        scaled_ref = scaled_refs[k * LANES // part]
+        column = k * LANES % part
         for s in range(STEPS):
             block = wide_ref[pl.ds(k * STEPS + s, groups, stride=stride), :]
             squares[s] = squares[s] + block * block
-            scaled_ref[s * groups : (s + 1) * groups, k * LANES : (k + 1) * LANES] = (
+            scaled_ref[s * groups : (s + 1) * groups, column : column + LANES] = (
                 block * gain
             ).astype(bf16)
-    scaled = scaled_ref[...]
-    pack_pair(0, scaled, tables_ref, gate_ref, up_ref, out_ref, both_ref)
+    pack_pair(0, scaled_refs, tables_ref, gate_ref, up_ref, out_ref, sums_ref, both_ref)
     square = jnp.sum(jnp.concatenate(squares, axis=0), axis=1, keepdims=True)
     diagonal = iota((tokens, LANES), 0) == iota((tokens, LANES), 1)
     square = jnp.sum(jnp.where(diagonal, square, 0.0), axis=0, keepdims=True)
-    router = lax.dot_general(
-        router_ref[...], scaled, (((1,), (1,)), ((), ())), preferred_element_type=f32
+    router = sum(
+        lax.dot_general(
+            router_ref[:, n * part : (n + 1) * part],
+            ref[...],
+            (((1,), (1,)), ((), ())),
+            preferred_element_type=f32,
+        )
+        for n, ref in enumerate(scaled_refs)
     )
     router = jnp.concatenate([router, jnp.zeros((E, LANES - tokens), f32)], axis=1)
     high, middle, _ = pieces(router)
@@ -237,12 +259,12 @@
         ],
         axis=1,
     )
-    extra = jnp.concatenate([extra, jnp.zeros((8, 4 * LANES), f32)], axis=0)
     out_ref[2 * CAP :, :] = extra.astype(bf16)
 
 
-def hidden_rest_kernel(scaled_ref, tables_ref, gate_ref, up_ref, out_ref, both_ref):
-    pack_pair(1, scaled_ref[...], tables_ref, gate_ref, up_ref, out_ref, both_ref)
+def hidden_rest_kernel(*refs):
+    *scaled_refs, tables_ref, gate_ref, up_ref, out_ref, sums_ref, both_ref = refs
+    pack_pair(1, scaled_refs, tables_ref, gate_ref, up_ref, out_ref, sums_ref, both_ref)
 
 
 def spread_pair(own_ref, other_ref, factors, turned, side_ref, tokens):
@@ -378,7 +400,7 @@
         ),
         [VMEM] * 6,
         [pltpu.VMEM((rows, HD), f32)],
-        beside=7,
+        beside=2,
     )
     square = struct((PAIRS, LANES, LANES), bf16)
     residual_rows, routes_row, tables, turned = call(
@@ -388,11 +410,19 @@
         [VMEM] * 2,
     )
     other = lax.ppermute(partial, "tp", swap)
+    attended = call(
+        join_kernel,
+        struct((steps, query_width), bf16),
+        (partial, other),
+        [VMEM] * 2,
+        [pltpu.VMEM((rows, HD), f32)],
+        beside=2,
+    )
     terms = call(
         project_kernel,
         struct((rows, LANES), bf16),
-        (partial, other, out_weight),
-        [VMEM] * 3,
+        (attended, out_weight),
+        [VMEM] * 2,
         [pltpu.VMEM((rows, LANES), f32)],
         beside=20,
     )
@@ -402,10 +432,14 @@
         jnp.broadcast_to(state[None], (groups, rows, LANES)), "grp", 0, 0
     ).reshape(groups * rows, LANES)
     hidden_width = 2 * expert_gate.shape[2]
-    both = pltpu.VMEM((LANES, hidden_width), bf16)
-    hidden, scaled = call(
+    both = pltpu.VMEM((2, LANES, hidden_width), bf16)
+    sums = pltpu.VMEM((4, token_count, hidden_width // 2), f32)
+    hidden, *scaled = call(
         hidden_kernel,
-        (struct((2 * CAP + 16, hidden_width), bf16), struct((token_count, width), bf16)),
+        (
+            struct((2 * CAP + E, hidden_width), bf16),
+            *[struct((token_count, width // PARTS), bf16)] * PARTS,
+        ),
         (
             all_state,
             norm_gain.reshape(1, -1),
@@ -415,16 +449,16 @@
             expert_up,
         ),
         [VMEM] * 6,
-        [pltpu.VMEM((groups * rows, LANES), f32), both],
+        [pltpu.VMEM((groups * rows, LANES), f32), sums, both],
         limit=8,
     )
     other_hidden = lax.ppermute(hidden, "tp", swap)
     hidden_rest = call(
         hidden_rest_kernel,
         struct((2 * CAP, hidden_width), bf16),
-        (scaled, tables, expert_gate, expert_up),
-        [VMEM] * 4,
-        [both],
+        (*scaled, tables, expert_gate, expert_up),
+        [VMEM] * (PARTS + 3),
+        [sums, both],
     )
     other_hidden_rest = lax.ppermute(hidden_rest, "tp", swap)
     side = pltpu.VMEM((LANES, hidden_width), bf16)

time: 66.5 us -> 66 us (level)
    pallas_call x9 -> x10, Pallas kernels: 9.29 us -> 8.87 us  [call(): pl.pallas_call(kernel, out_shape=out, in_specs=specs, out_specs=jax.tree....]
where the time goes in v3:
time: 66 us; the launch traced here: 65.7 us
  blocking collectives  39.8 us (60%)
  Pallas kernels  8.87 us (13%)
  starting transfers between devices  8.84 us (13%)
  waiting for transfers between devices  4.93 us (7%)
  local copies, waits for them, and re-layouts  2.3 us (3%)
  between operations  0.9 us (1%)
    all_to_all x1, blocking collectives, on_device(): lax.all_to_all(jnp.broadcast_to(state[None], (groups, rows, LANES)), 'grp...  24 us
    all_to_all x1, blocking collectives, on_device(): received = lax.all_to_all(sent.reshape(groups, rows, LANES), 'grp', 0, 0)  15.8 us
    pallas_call x10, Pallas kernels, call(): pl.pallas_call(kernel, out_shape=out, in_specs=specs, out_specs=jax.tree....  8.87 us
    ppermute x1, starting transfers between devices, on_device(): other_summed = lax.ppermute(summed, 'ep', swap)  3.69 us
    unnamed x32, local copies, waits for them, and re-layouts  2.23 us
    ppermute x1, starting transfers between devices, on_device(): other = lax.ppermute(partial, 'tp', swap)  2.12 us
    ppermute x1, waiting for transfers between devices, on_device(): other_hidden_rest = lax.ppermute(hidden_rest, 'tp', swap)  1.43 us
    ppermute x1, starting transfers between devices, on_device(): other_terms = lax.ppermute(terms, 'ep', swap)  1.43 us
  transfers between devices with their start and end apart: 5, of which 5 were waited for; matrix products, arithmetic and copies ran while one was open for 0% of the time, Pallas kernels for 4%

profile of v3, /device:TPU:1, one launch (start us, length us, event | category | flops | bytes accessed | tf_op | source)
XLA Modules:
  0.0 65.7 jit_solution(16138472632004729062)
XLA Ops:
  0.8 0.3 copy-done.6
  1.1 0.2 copy-done.5
  1.2 0.6 shard_map.138.own_ref
  1.8 2.1 %collective-permute-start = (bf16[72,256]{1,0:T(8,128)(2,1)S(1)}, bf16[72,256]{1,0:T(8,128)(2,1)S(1)}, u32[]{:S(2)}, u32[]{:S(2)}) collective-permute-start(bf16[72,256]{1,0:T(8,128)(2,1)S(1)} %shard_map.138.own_ref), channel_id=1, source_target_pairs={{0,1},{1,0},{2,3},{3,2},{4,5},{5,4},{6,7},{7,6},{8,9},{9,8},{10,11... | collective-permute-start | bytes 110600 | tf_op jit(solution)/shard_map/ppermute | solution.py:412
  3.9 1.3 %collective-permute-done.other_ref = bf16[72,256]{1,0:T(8,128)(2,1)S(1)} collective-permute-done((bf16[72,256]{1,0:T(8,128)(2,1)S(1)}, bf16[72,256]{1,0:T(8,128)(2,1)S(1)}, u32[]{:S(2)}, u32[]{:S(2)}) %collective-permute-start) | collective-permute-done | bytes 36896 | tf_op jit(solution)/shard_map/ppermute | solution.py:412
  5.3 0.2 shard_map.139.attended_ref
  5.5 1.7 %copy-done.4 = bf16[3072,3072]{1,0:T(8,128)(2,1)S(1)} copy-done((bf16[3072,3072]{1,0:T(8,128)(2,1)S(1)}, bf16[3072,3072]{1,0:T(8,128)(2,1)}, u32[]{:S(2)}) %copy-start.4) | copy-done | bytes 18874392
  7.2 2.5 %shard_map.140 = bf16[72,128]{1,0:T(8,128)(2,1)S(1)} custom-call(bf16[3,3072]{1,0:T(4,128)(2,1)S(1)} %shard_map.139.attended_ref, bf16[3072,3072]{1,0:T(8,128)(2,1)S(1)} %copy-done.4), custom_call_target="tpu_custom_call" | custom-call | flops 20000000000 | tf_op jit(solution)/shard_map/pallas_call | solution.py:29
  9.8 1.4 %collective-permute-start.1 = (bf16[72,128]{1,0:T(8,128)(2,1)S(1)}, bf16[72,128]{1,0:T(8,128)(2,1)S(1)}, u32[]{:S(2)}, u32[]{:S(2)}) collective-permute-start(bf16[72,128]{1,0:T(8,128)(2,1)S(1)} %shard_map.140), channel_id=1, source_target_pairs={{0,2},{2,0},{1,3},{3,1},{4,6},{6,4},{5,7},{7,5},{8,10},{10,8},{9,1... | collective-permute-start | bytes 55304 | tf_op jit(solution)/shard_map/ppermute | solution.py:429
  11.2 0.3 shard_map.136
  11.5 0.5 collective-permute-done.1
  12.2 24.0 %all_to_all.10 = bf16[32,72,128]{2,1,0:T(8,128)(2,1)S(1)} all-to-all(bf16[32,72,128]{2,1,0:T(8,128)(2,1)S(1)} %broadcast_in_dim.4), channel_id=1, replica_groups=mesh['grp'=32,'ep'=2,'tp'=2] {'grp'}, dimensions={0} | all-to-all | bytes 1179648 | tf_op jit(solution)/shard_map/all_to_all | solution.py:431
  36.2 1.5 %shard_map.141 = (bf16[104,512]{1,0:T(8,128)(2,1)S(1)}, bf16[96,768]{1,0:T(8,128)(2,1)S(1)}, bf16[96,768]{1,0:T(8,128)(2,1)S(1)}, bf16[96,768]{1,0:T(8,128)(2,1)S(1)}, bf16[96,768]{1,0:T(8,128)(2,1)S(1)}) custom-call(bf16[2304,128]{1,0:T(8,128)(2,1)S(1)} %bitcast.19, f32[1,3072]{1,0:T(1,128)S(1)} %bitcast.22, bf16[8,3072]{1,0:T(8,128)(2,1)S(1)} %bitcast.20, ...), custom_call_target="tpu_custom_call" | custom-call | tf_op jit(solution)/shard_map/pallas_call | solution.py:29
  37.8 0.4 collective-permute-start.3
  38.1 1.3 %shard_map.142.own_ref = bf16[96,512]{1,0:T(8,128)(2,1)S(1)} custom-call(bf16[96,768]{1,0:T(8,128)(2,1)S(1)} %get-tuple-element.18.refs_0_, bf16[96,768]{1,0:T(8,128)(2,1)S(1)} %get-tuple-element.19.refs_1_, bf16[96,768]{1,0:T(8,128)(2,1)S(1)} %get-tuple-element.20.refs_2_, bf16[96,768]{1,0:T(8,128)(2,1)S(1)} %get-tuple-element.21.refs_3_, ...), custom_call_target="tpu_custom_call" | custom-call | tf_op jit(solution)/shard_map/pallas_call | solution.py:29
  39.4 1.2 %collective-permute-start.2 = (bf16[96,512]{1,0:T(8,128)(2,1)S(1)}, bf16[96,512]{1,0:T(8,128)(2,1)S(1)}, u32[]{:S(2)}, u32[]{:S(2)}) collective-permute-start(bf16[96,512]{1,0:T(8,128)(2,1)S(1)} %shard_map.142.own_ref), channel_id=1, source_target_pairs={{0,1},{1,0},{2,3},{3,2},{4,5},{5,4},{6,7},{7,6},{8,9},{9,8},{10,11... | collective-permute-start | bytes 294920 | tf_op jit(solution)/shard_map/ppermute | solution.py:463
  40.6 0.7 %collective-permute-done.3.other_ref = bf16[104,512]{1,0:T(8,128)(2,1)S(1)} collective-permute-done((bf16[104,512]{1,0:T(8,128)(2,1)S(1)}, bf16[104,512]{1,0:T(8,128)(2,1)S(1)}, u32[]{:S(2)}, u32[]{:S(2)}) %collective-permute-start.3) | collective-permute-done | bytes 106528 | tf_op jit(solution)/shard_map/ppermute | solution.py:455
  41.4 0.9 %shard_map.143 = (f32[96,3072]{1,0:T(8,128)S(1)}, f32[96,128]{1,0:T(8,128)S(1)}) custom-call(bf16[104,512]{1,0:T(8,128)(2,1)S(1)} %get-tuple-element.22.own_ref, bf16[104,512]{1,0:T(8,128)(2,1)S(1)} %collective-permute-done.3.other_ref, s32[2,128]{1,0:T(2,128)S(1)} %get-tuple-element.23.routes_ref, ...), custom_call_target="tpu_custom_call" | custom-call | tf_op jit(solution)/shard_map/pallas_call | solution.py:29
  42.3 1.4 %collective-permute-done.2.other_ref = bf16[96,512]{1,0:T(8,128)(2,1)S(1)} collective-permute-done((bf16[96,512]{1,0:T(8,128)(2,1)S(1)}, bf16[96,512]{1,0:T(8,128)(2,1)S(1)}, u32[]{:S(2)}, u32[]{:S(2)}) %collective-permute-start.2) | collective-permute-done | bytes 98336 | tf_op jit(solution)/shard_map/ppermute | solution.py:463
  43.7 0.9 %shard_map.144 = bf16[2304,128]{1,0:T(8,128)(2,1)S(1)} custom-call(bf16[96,512]{1,0:T(8,128)(2,1)S(1)} %shard_map.142.own_ref, bf16[96,512]{1,0:T(8,128)(2,1)S(1)} %collective-permute-done.2.other_ref, f32[96,3072]{1,0:T(8,128)S(1)} %get-tuple-element.25.terms_ref, f32[96,128]{1,0:T(8,128)S(1)} %get-tuple-element.26.factors_ref, ...), custom_call_target="tpu_custom_call" | custom-call | tf_op jit(solution)/shard_map/pallas_call | solution.py:29
  44.7 15.8 %all_to_all.11 = bf16[32,72,128]{2,1,0:T(8,128)(2,1)S(1)} all-to-all(bf16[32,72,128]{2,1,0:T(8,128)(2,1)S(1)} %bitcast.18), channel_id=1, replica_groups=mesh['grp'=32,'ep'=2,'tp'=2] {'grp'}, dimensions={0} | all-to-all | bytes 1179648 | tf_op jit(solution)/shard_map/all_to_all | solution.py:481
  60.6 3.7 %collective-permute-start.4 = (f32[72,128]{1,0:T(8,128)S(1)}, f32[72,128]{1,0:T(8,128)S(1)}, u32[]{:S(2)}, u32[]{:S(2)}) collective-permute-start(f32[72,128]{1,0:T(8,128)S(1)} %convert_reduce_fusion.own_ref), channel_id=1, source_target_pairs={{0,2},{2,0},{1,3},{3,1},{4,6},{6,4},{5,7},{7,5},{8,10},{10,8},{9,1... | collective-permute-start | bytes 110600 | tf_op jit(solution)/shard_map/ppermute | solution.py:483
  64.2 0.9 %collective-permute-done.4.other_ref = f32[72,128]{1,0:T(8,128)S(1)} collective-permute-done((f32[72,128]{1,0:T(8,128)S(1)}, f32[72,128]{1,0:T(8,128)S(1)}, u32[]{:S(2)}, u32[]{:S(2)}) %collective-permute-start.4) | collective-permute-done | bytes 36896 | tf_op jit(solution)/shard_map/ppermute | solution.py:483
  65.1 0.6 shard_map.145
  (36 shorter events, 0.3 us)
Async XLA Ops:
  0.0 1.1 %copy-start.6 = (bf16[1,512,512]{2,1,0:T(8,128)(2,1)S(1)}, bf16[1,512,512]{2,1,0:T(8,128)(2,1)}, u32[]{:S(2)}) copy-start(bf16[1,512,512]{2,1,0:T(8,128)(2,1)} %param.18) | copy-start | bytes 1572868
  0.0 1.2 %copy-start.5 = (bf16[1,512,512]{2,1,0:T(8,128)(2,1)S(1)}, bf16[1,512,512]{2,1,0:T(8,128)(2,1)}, u32[]{:S(2)}) copy-start(bf16[1,512,512]{2,1,0:T(8,128)(2,1)} %param.17) | copy-start | bytes 1572868
  0.0 1.2 %copy-start.9 = (bf16[3,1,512]{2,0,1:T(4,128)(2,1)S(1)}, bf16[3,1,512]{2,0,1:T(4,128)(2,1)}, u32[]{:S(2)}) copy-start(bf16[3,1,512]{2,0,1:T(4,128)(2,1)} %param.16) | copy-start | bytes 9220
  0.0 1.2 %copy-start.8 = (bf16[3,1,512]{2,0,1:T(4,128)(2,1)S(1)}, bf16[3,1,512]{2,0,1:T(4,128)(2,1)}, u32[]{:S(2)}) copy-start(bf16[3,1,512]{2,0,1:T(4,128)(2,1)} %param.15) | copy-start | bytes 9220
  0.0 1.2 %copy-start.7 = (bf16[3,1,3072]{2,0,1:T(4,128)(2,1)S(1)}, bf16[3,1,3072]{2,0,1:T(4,128)(2,1)}, u32[]{:S(2)}) copy-start(bf16[3,1,3072]{2,0,1:T(4,128)(2,1)} %param.14) | copy-start | bytes 55300
  0.8 6.4 %copy-start.4 = (bf16[3072,3072]{1,0:T(8,128)(2,1)S(1)}, bf16[3072,3072]{1,0:T(8,128)(2,1)}, u32[]{:S(2)}) copy-start(bf16[3072,3072]{1,0:T(8,128)(2,1)} %weight_ref.1) | copy-start | bytes 56623108
  1.8 3.5 %collective-permute-start = (bf16[72,256]{1,0:T(8,128)(2,1)S(1)}, bf16[72,256]{1,0:T(8,128)(2,1)S(1)}, u32[]{:S(2)}, u32[]{:S(2)}) collective-permute-start(bf16[72,256]{1,0:T(8,128)(2,1)S(1)} %shard_map.138.own_ref), channel_id=1, source_target_pairs={{0,1},{1,0},{2,3},{3,2},{4,5},{5,4},{6,7},{7,6},{8,9},{9,8},{10,11... | collective-permute-start | bytes 110600 | tf_op jit(solution)/shard_map/ppermute | solution.py:412
  5.3 30.9 %slice-start = ((s8[6291456]{0:T(1024)(128)(4,1)}), s8[4194304]{0:T(1024)(128)(4,1)S(1)}, s32[]{:S(2)}) async-start(s8[6291456]{0:T(1024)(128)(4,1)} %bitcast.12), calls=%async_computation.2 | async-start | bytes 8388608
  5.3 30.9 %slice-start.2 = ((s8[6291456]{0:T(1024)(128)(4,1)}), s8[4194304]{0:T(1024)(128)(4,1)S(1)}, s32[]{:S(2)}) async-start(s8[6291456]{0:T(1024)(128)(4,1)} %bitcast.14), calls=%async_computation.4 | async-start | bytes 8388608
  7.2 4.0 %copy-start.1 = (bf16[3,1,3072]{2,0,1:T(4,128)(2,1)S(1)}, bf16[3,1,3072]{2,0,1:T(4,128)(2,1)}, u32[]{:S(2)}) copy-start(bf16[3,1,3072]{2,0,1:T(4,128)(2,1)} %param.20) | copy-start | bytes 55300
  7.2 4.0 %copy-start.3 = (s32[3,32,2]{1,2,0:T(2,128)S(1)}, s32[3,32,2]{1,2,0:T(2,128)}, u32[]{:S(2)}) copy-start(s32[3,32,2]{1,2,0:T(2,128)} %param.24) | copy-start | bytes 2308
  7.2 29.0 %slice-start.1 = ((s8[6291456]{0:T(1024)(128)(4,1)}), s8[2097152]{0:T(1024)(128)(4,1)S(1)}, s32[]{:S(2)}) async-start(s8[6291456]{0:T(1024)(128)(4,1)} %bitcast.12), calls=%async_computation.3 | async-start | bytes 4194304
  7.2 29.0 %slice-start.3 = ((s8[6291456]{0:T(1024)(128)(4,1)}), s8[2097152]{0:T(1024)(128)(4,1)S(1)}, s32[]{:S(2)}) async-start(s8[6291456]{0:T(1024)(128)(4,1)} %bitcast.14), calls=%async_computation.5 | async-start | bytes 4194304
  7.2 29.0 %copy-start = (bf16[3072,8]{0,1:T(8,128)(2,1)S(1)}, bf16[3072,8]{0,1:T(8,128)(2,1)}, u32[]{:S(2)}) copy-start(bf16[3072,8]{0,1:T(8,128)(2,1)} %param.23) | copy-start | bytes 147460
  7.2 29.0 %copy-start.2 = (f32[3072]{0:T(1024)S(1)}, f32[3072]{0:T(1024)}, u32[]{:S(2)}) copy-start(f32[3072]{0:T(1024)} %param.22) | copy-start | bytes 36868
  9.8 2.3 %collective-permute-start.1 = (bf16[72,128]{1,0:T(8,128)(2,1)S(1)}, bf16[72,128]{1,0:T(8,128)(2,1)S(1)}, u32[]{:S(2)}, u32[]{:S(2)}) collective-permute-start(bf16[72,128]{1,0:T(8,128)(2,1)S(1)} %shard_map.140), channel_id=1, source_target_pairs={{0,2},{2,0},{1,3},{3,1},{4,6},{6,4},{5,7},{7,5},{8,10},{10,8},{9,1... | collective-permute-start | bytes 55304 | tf_op jit(solution)/shard_map/ppermute | solution.py:429
  36.2 5.2 %slice-start.4 = ((s8[6291456]{0:T(1024)(128)(4,1)}), s8[4194304]{0:T(1024)(128)(4,1)S(1)}, s32[]{:S(2)}) async-start(s8[6291456]{0:T(1024)(128)(4,1)} %bitcast.16), calls=%async_computation.6 | async-start | bytes 8388608
  37.8 3.6 %collective-permute-start.3 = (bf16[104,512]{1,0:T(8,128)(2,1)S(1)}, bf16[104,512]{1,0:T(8,128)(2,1)S(1)}, u32[]{:S(2)}, u32[]{:S(2)}) collective-permute-start(bf16[104,512]{1,0:T(8,128)(2,1)S(1)} %get-tuple-element.22.own_ref), channel_id=1, source_target_pairs={{0,1},{1,0},{2,3},{3,2},{4,5},{5,4},{6,7},{7,6},{8,9},{9,8},{10,11... | collective-permute-start | bytes 319496 | tf_op jit(solution)/shard_map/ppermute | solution.py:455
  38.1 3.2 %slice-start.5 = ((s8[6291456]{0:T(1024)(128)(4,1)}), s8[2097152]{0:T(1024)(128)(4,1)S(1)}, s32[]{:S(2)}) async-start(s8[6291456]{0:T(1024)(128)(4,1)} %bitcast.16), calls=%async_computation.7 | async-start | bytes 4194304
  39.4 4.3 %collective-permute-start.2 = (bf16[96,512]{1,0:T(8,128)(2,1)S(1)}, bf16[96,512]{1,0:T(8,128)(2,1)S(1)}, u32[]{:S(2)}, u32[]{:S(2)}) collective-permute-start(bf16[96,512]{1,0:T(8,128)(2,1)S(1)} %shard_map.142.own_ref), channel_id=1, source_target_pairs={{0,1},{1,0},{2,3},{3,2},{4,5},{5,4},{6,7},{7,6},{8,9},{9,8},{10,11... | collective-permute-start | bytes 294920 | tf_op jit(solution)/shard_map/ppermute | solution.py:463
  60.6 4.6 %collective-permute-start.4 = (f32[72,128]{1,0:T(8,128)S(1)}, f32[72,128]{1,0:T(8,128)S(1)}, u32[]{:S(2)}, u32[]{:S(2)}) collective-permute-start(f32[72,128]{1,0:T(8,128)S(1)} %convert_reduce_fusion.own_ref), channel_id=1, source_target_pairs={{0,2},{2,0},{1,3},{3,1},{4,6},{6,4},{5,7},{7,5},{8,10},{10,8},{9,1... | collective-permute-start | bytes 110600 | tf_op jit(solution)/shard_map/ppermute | solution.py:483

commit v4 on v3

--- a/solution.py
+++ b/solution.py
@@ -14,6 +14,7 @@
 PAIRS = 2
 STEPS = 3
 PARTS = 4
+EXTRA = 16
 LANES = 128
 
 far_below = -1e30
@@ -152,10 +153,12 @@
     present = totals > 0.0
     safe = jnp.where(present, totals, 1.0)
     out_ref[:, :HD] = (weighted / safe).astype(bf16)
-    level = jnp.where(present, highest + jnp.log(safe), far_below)
-    high, middle, low = pieces(level)
+    tail = pieces(highest) + pieces(totals)
     lane = iota((rows, LANES), 1)
-    out_ref[:, HD:] = jnp.where(lane == 0, high, jnp.where(lane == 1, middle, low)).astype(bf16)
+    row_tail = jnp.zeros((rows, LANES), f32)
+    for i, piece in enumerate(tail):
+        row_tail = jnp.where(lane == i, piece, row_tail)
+    out_ref[:, HD:] = row_tail.astype(bf16)
 
 
 def join_kernel(own_ref, other_ref, attended_ref, rows_ref):
@@ -164,13 +167,15 @@
 
     def read(ref):
         tail = ref[:, HD:].astype(f32)
-        return ref[:, :HD].astype(f32), tail[:, 0:1] + tail[:, 1:2] + tail[:, 2:3]
-
-    own, own_level = read(own_ref)
-    other, other_level = read(other_ref)
-    top = jnp.maximum(own_level, other_level)
-    own_factor = jnp.exp(own_level - top)
-    other_factor = jnp.exp(other_level - top)
+        highest = tail[:, 0:1] + tail[:, 1:2] + tail[:, 2:3]
+        totals = tail[:, 3:4] + tail[:, 4:5] + tail[:, 5:6]
+        return ref[:, :HD].astype(f32), highest, totals
+
+    own, own_highest, own_totals = read(own_ref)
+    other, other_highest, other_totals = read(other_ref)
+    top = jnp.maximum(own_highest, other_highest)
+    own_factor = own_totals * jnp.exp(own_highest - top)
+    other_factor = other_totals * jnp.exp(other_highest - top)
     rows_ref[...] = (own * own_factor + other * other_factor) / (own_factor + other_factor)
     attended_ref[...] = jnp.concatenate(
         [rows_ref[h * steps : (h + 1) * steps, :] for h in range(heads)], axis=1
@@ -259,6 +264,7 @@
         ],
         axis=1,
     )
+    extra = jnp.concatenate([extra, jnp.zeros((EXTRA - E, 4 * LANES), f32)], axis=0)
     out_ref[2 * CAP :, :] = extra.astype(bf16)
 
 
@@ -437,7 +443,7 @@
     hidden, *scaled = call(
         hidden_kernel,
         (
-            struct((2 * CAP + E, hidden_width), bf16),
+            struct((2 * CAP + EXTRA, hidden_width), bf16),
             *[struct((token_count, width // PARTS), bf16)] * PARTS,
         ),
         (

time: 66 us -> 66.1 us (level)
  no operation moved by 1% of the time
where the time goes in v4:
time: 66.1 us; the launch traced here: 65.9 us
  blocking collectives  40.3 us (61%)
  Pallas kernels  8.95 us (14%)
  starting transfers between devices  8.5 us (13%)
  waiting for transfers between devices  4.92 us (7%)
  local copies, waits for them, and re-layouts  2.24 us (3%)
  between operations  0.89 us (1%)
    all_to_all x1, blocking collectives, on_device(): lax.all_to_all(jnp.broadcast_to(state[None], (groups, rows, LANES)), 'grp...  24 us
    all_to_all x1, blocking collectives, on_device(): received = lax.all_to_all(sent.reshape(groups, rows, LANES), 'grp', 0, 0)  16.3 us
    pallas_call x10, Pallas kernels, call(): pl.pallas_call(kernel, out_shape=out, in_specs=specs, out_specs=jax.tree....  8.95 us
    ppermute x1, starting transfers between devices, on_device(): other_summed = lax.ppermute(summed, 'ep', swap)  3.34 us
    unnamed x32, local copies, waits for them, and re-layouts  2.16 us
    ppermute x1, starting transfers between devices, on_device(): other = lax.ppermute(partial, 'tp', swap)  2.12 us
    ppermute x1, starting transfers between devices, on_device(): other_terms = lax.ppermute(terms, 'ep', swap)  1.43 us
    ppermute x1, waiting for transfers between devices, on_device(): other = lax.ppermute(partial, 'tp', swap)  1.35 us
  transfers between devices with their start and end apart: 5, of which 5 were waited for; matrix products, arithmetic and copies ran while one was open for 0% of the time, Pallas kernels for 4%

profile of v4, /device:TPU:1, one launch (start us, length us, event | category | flops | bytes accessed | tf_op | source)
XLA Modules:
  0.0 65.9 jit_solution(7525772092167525030)
XLA Ops:
  0.8 0.3 copy-done.6
  1.1 0.2 copy-done.5
  1.2 0.6 shard_map.138.own_ref
  1.8 2.1 %collective-permute-start = (bf16[72,256]{1,0:T(8,128)(2,1)S(1)}, bf16[72,256]{1,0:T(8,128)(2,1)S(1)}, u32[]{:S(2)}, u32[]{:S(2)}) collective-permute-start(bf16[72,256]{1,0:T(8,128)(2,1)S(1)} %shard_map.138.own_ref), channel_id=1, source_target_pairs={{0,1},{1,0},{2,3},{3,2},{4,5},{5,4},{6,7},{7,6},{8,9},{9,8},{10,11... | collective-permute-start | bytes 110600 | tf_op jit(solution)/shard_map/ppermute | solution.py:418
  3.9 1.3 %collective-permute-done.other_ref = bf16[72,256]{1,0:T(8,128)(2,1)S(1)} collective-permute-done((bf16[72,256]{1,0:T(8,128)(2,1)S(1)}, bf16[72,256]{1,0:T(8,128)(2,1)S(1)}, u32[]{:S(2)}, u32[]{:S(2)}) %collective-permute-start) | collective-permute-done | bytes 36896 | tf_op jit(solution)/shard_map/ppermute | solution.py:418
  5.3 0.3 shard_map.139.attended_ref
  5.5 1.7 %copy-done.4 = bf16[3072,3072]{1,0:T(8,128)(2,1)S(1)} copy-done((bf16[3072,3072]{1,0:T(8,128)(2,1)S(1)}, bf16[3072,3072]{1,0:T(8,128)(2,1)}, u32[]{:S(2)}) %copy-start.4) | copy-done | bytes 18874392
  7.2 2.5 %shard_map.140 = bf16[72,128]{1,0:T(8,128)(2,1)S(1)} custom-call(bf16[3,3072]{1,0:T(4,128)(2,1)S(1)} %shard_map.139.attended_ref, bf16[3072,3072]{1,0:T(8,128)(2,1)S(1)} %copy-done.4), custom_call_target="tpu_custom_call" | custom-call | flops 20000000000 | tf_op jit(solution)/shard_map/pallas_call | solution.py:30
  9.8 1.4 %collective-permute-start.1 = (bf16[72,128]{1,0:T(8,128)(2,1)S(1)}, bf16[72,128]{1,0:T(8,128)(2,1)S(1)}, u32[]{:S(2)}, u32[]{:S(2)}) collective-permute-start(bf16[72,128]{1,0:T(8,128)(2,1)S(1)} %shard_map.140), channel_id=1, source_target_pairs={{0,2},{2,0},{1,3},{3,1},{4,6},{6,4},{5,7},{7,5},{8,10},{10,8},{9,1... | collective-permute-start | bytes 55304 | tf_op jit(solution)/shard_map/ppermute | solution.py:435
  11.2 0.3 shard_map.136
  11.5 0.5 collective-permute-done.1
  12.2 24.0 %all_to_all.10 = bf16[32,72,128]{2,1,0:T(8,128)(2,1)S(1)} all-to-all(bf16[32,72,128]{2,1,0:T(8,128)(2,1)S(1)} %broadcast_in_dim.4), channel_id=1, replica_groups=mesh['grp'=32,'ep'=2,'tp'=2] {'grp'}, dimensions={0} | all-to-all | bytes 1179648 | tf_op jit(solution)/shard_map/all_to_all | solution.py:437
  36.2 1.5 %shard_map.141 = (bf16[112,512]{1,0:T(8,128)(2,1)S(1)}, bf16[96,768]{1,0:T(8,128)(2,1)S(1)}, bf16[96,768]{1,0:T(8,128)(2,1)S(1)}, bf16[96,768]{1,0:T(8,128)(2,1)S(1)}, bf16[96,768]{1,0:T(8,128)(2,1)S(1)}) custom-call(bf16[2304,128]{1,0:T(8,128)(2,1)S(1)} %bitcast.19, f32[1,3072]{1,0:T(1,128)S(1)} %bitcast.22, bf16[8,3072]{1,0:T(8,128)(2,1)S(1)} %bitcast.20, ...), custom_call_target="tpu_custom_call" | custom-call | tf_op jit(solution)/shard_map/pallas_call | solution.py:30
  37.8 0.4 collective-permute-start.3
  38.1 1.3 %shard_map.142.own_ref = bf16[96,512]{1,0:T(8,128)(2,1)S(1)} custom-call(bf16[96,768]{1,0:T(8,128)(2,1)S(1)} %get-tuple-element.18.refs_0_, bf16[96,768]{1,0:T(8,128)(2,1)S(1)} %get-tuple-element.19.refs_1_, bf16[96,768]{1,0:T(8,128)(2,1)S(1)} %get-tuple-element.20.refs_2_, bf16[96,768]{1,0:T(8,128)(2,1)S(1)} %get-tuple-element.21.refs_3_, ...), custom_call_target="tpu_custom_call" | custom-call | tf_op jit(solution)/shard_map/pallas_call | solution.py:30
  39.4 1.2 %collective-permute-start.2 = (bf16[96,512]{1,0:T(8,128)(2,1)S(1)}, bf16[96,512]{1,0:T(8,128)(2,1)S(1)}, u32[]{:S(2)}, u32[]{:S(2)}) collective-permute-start(bf16[96,512]{1,0:T(8,128)(2,1)S(1)} %shard_map.142.own_ref), channel_id=1, source_target_pairs={{0,1},{1,0},{2,3},{3,2},{4,5},{5,4},{6,7},{7,6},{8,9},{9,8},{10,11... | collective-permute-start | bytes 294920 | tf_op jit(solution)/shard_map/ppermute | solution.py:469
  40.6 0.8 %collective-permute-done.3.other_ref = bf16[112,512]{1,0:T(8,128)(2,1)S(1)} collective-permute-done((bf16[112,512]{1,0:T(8,128)(2,1)S(1)}, bf16[112,512]{1,0:T(8,128)(2,1)S(1)}, u32[]{:S(2)}, u32[]{:S(2)}) %collective-permute-start.3) | collective-permute-done | bytes 114720 | tf_op jit(solution)/shard_map/ppermute | solution.py:461
  41.5 0.9 %shard_map.143 = (f32[96,3072]{1,0:T(8,128)S(1)}, f32[96,128]{1,0:T(8,128)S(1)}) custom-call(bf16[112,512]{1,0:T(8,128)(2,1)S(1)} %get-tuple-element.22.own_ref, bf16[112,512]{1,0:T(8,128)(2,1)S(1)} %collective-permute-done.3.other_ref, s32[2,128]{1,0:T(2,128)S(1)} %get-tuple-element.23.routes_ref, ...), custom_call_target="tpu_custom_call" | custom-call | tf_op jit(solution)/shard_map/pallas_call | solution.py:30
  42.4 1.3 %collective-permute-done.2.other_ref = bf16[96,512]{1,0:T(8,128)(2,1)S(1)} collective-permute-done((bf16[96,512]{1,0:T(8,128)(2,1)S(1)}, bf16[96,512]{1,0:T(8,128)(2,1)S(1)}, u32[]{:S(2)}, u32[]{:S(2)}) %collective-permute-start.2) | collective-permute-done | bytes 98336 | tf_op jit(solution)/shard_map/ppermute | solution.py:469
  43.7 0.9 %shard_map.144 = bf16[2304,128]{1,0:T(8,128)(2,1)S(1)} custom-call(bf16[96,512]{1,0:T(8,128)(2,1)S(1)} %shard_map.142.own_ref, bf16[96,512]{1,0:T(8,128)(2,1)S(1)} %collective-permute-done.2.other_ref, f32[96,3072]{1,0:T(8,128)S(1)} %get-tuple-element.25.terms_ref, f32[96,128]{1,0:T(8,128)S(1)} %get-tuple-element.26.factors_ref, ...), custom_call_target="tpu_custom_call" | custom-call | tf_op jit(solution)/shard_map/pallas_call | solution.py:30
  44.7 16.3 %all_to_all.11 = bf16[32,72,128]{2,1,0:T(8,128)(2,1)S(1)} all-to-all(bf16[32,72,128]{2,1,0:T(8,128)(2,1)S(1)} %bitcast.18), channel_id=1, replica_groups=mesh['grp'=32,'ep'=2,'tp'=2] {'grp'}, dimensions={0} | all-to-all | bytes 1179648 | tf_op jit(solution)/shard_map/all_to_all | solution.py:487
  61.1 3.3 %collective-permute-start.4 = (f32[72,128]{1,0:T(8,128)S(1)}, f32[72,128]{1,0:T(8,128)S(1)}, u32[]{:S(2)}, u32[]{:S(2)}) collective-permute-start(f32[72,128]{1,0:T(8,128)S(1)} %convert_reduce_fusion.own_ref), channel_id=1, source_target_pairs={{0,2},{2,0},{1,3},{3,1},{4,6},{6,4},{5,7},{7,5},{8,10},{10,8},{9,1... | collective-permute-start | bytes 110600 | tf_op jit(solution)/shard_map/ppermute | solution.py:489
  64.4 0.9 %collective-permute-done.4.other_ref = f32[72,128]{1,0:T(8,128)S(1)} collective-permute-done((f32[72,128]{1,0:T(8,128)S(1)}, f32[72,128]{1,0:T(8,128)S(1)}, u32[]{:S(2)}, u32[]{:S(2)}) %collective-permute-start.4) | collective-permute-done | bytes 36896 | tf_op jit(solution)/shard_map/ppermute | solution.py:489
  65.3 0.6 shard_map.145
  (36 shorter events, 0.3 us)
Async XLA Ops:
  0.0 1.1 %copy-start.6 = (bf16[1,512,512]{2,1,0:T(8,128)(2,1)S(1)}, bf16[1,512,512]{2,1,0:T(8,128)(2,1)}, u32[]{:S(2)}) copy-start(bf16[1,512,512]{2,1,0:T(8,128)(2,1)} %param.18) | copy-start | bytes 1572868
  0.0 1.2 %copy-start.5 = (bf16[1,512,512]{2,1,0:T(8,128)(2,1)S(1)}, bf16[1,512,512]{2,1,0:T(8,128)(2,1)}, u32[]{:S(2)}) copy-start(bf16[1,512,512]{2,1,0:T(8,128)(2,1)} %param.17) | copy-start | bytes 1572868
  0.0 1.2 %copy-start.9 = (bf16[3,1,512]{2,0,1:T(4,128)(2,1)S(1)}, bf16[3,1,512]{2,0,1:T(4,128)(2,1)}, u32[]{:S(2)}) copy-start(bf16[3,1,512]{2,0,1:T(4,128)(2,1)} %param.16) | copy-start | bytes 9220
  0.0 1.2 %copy-start.8 = (bf16[3,1,512]{2,0,1:T(4,128)(2,1)S(1)}, bf16[3,1,512]{2,0,1:T(4,128)(2,1)}, u32[]{:S(2)}) copy-start(bf16[3,1,512]{2,0,1:T(4,128)(2,1)} %param.15) | copy-start | bytes 9220
  0.0 1.2 %copy-start.7 = (bf16[3,1,3072]{2,0,1:T(4,128)(2,1)S(1)}, bf16[3,1,3072]{2,0,1:T(4,128)(2,1)}, u32[]{:S(2)}) copy-start(bf16[3,1,3072]{2,0,1:T(4,128)(2,1)} %param.14) | copy-start | bytes 55300
  0.8 6.4 %copy-start.4 = (bf16[3072,3072]{1,0:T(8,128)(2,1)S(1)}, bf16[3072,3072]{1,0:T(8,128)(2,1)}, u32[]{:S(2)}) copy-start(bf16[3072,3072]{1,0:T(8,128)(2,1)} %weight_ref.1) | copy-start | bytes 56623108
  1.8 3.5 %collective-permute-start = (bf16[72,256]{1,0:T(8,128)(2,1)S(1)}, bf16[72,256]{1,0:T(8,128)(2,1)S(1)}, u32[]{:S(2)}, u32[]{:S(2)}) collective-permute-start(bf16[72,256]{1,0:T(8,128)(2,1)S(1)} %shard_map.138.own_ref), channel_id=1, source_target_pairs={{0,1},{1,0},{2,3},{3,2},{4,5},{5,4},{6,7},{7,6},{8,9},{9,8},{10,11... | collective-permute-start | bytes 110600 | tf_op jit(solution)/shard_map/ppermute | solution.py:418
  5.3 30.9 %slice-start = ((s8[6291456]{0:T(1024)(128)(4,1)}), s8[4194304]{0:T(1024)(128)(4,1)S(1)}, s32[]{:S(2)}) async-start(s8[6291456]{0:T(1024)(128)(4,1)} %bitcast.12), calls=%async_computation.2 | async-start | bytes 8388608
  5.3 30.9 %slice-start.2 = ((s8[6291456]{0:T(1024)(128)(4,1)}), s8[4194304]{0:T(1024)(128)(4,1)S(1)}, s32[]{:S(2)}) async-start(s8[6291456]{0:T(1024)(128)(4,1)} %bitcast.14), calls=%async_computation.4 | async-start | bytes 8388608
  7.2 4.0 %copy-start.1 = (bf16[3,1,3072]{2,0,1:T(4,128)(2,1)S(1)}, bf16[3,1,3072]{2,0,1:T(4,128)(2,1)}, u32[]{:S(2)}) copy-start(bf16[3,1,3072]{2,0,1:T(4,128)(2,1)} %param.20) | copy-start | bytes 55300
  7.2 4.0 %copy-start.3 = (s32[3,32,2]{1,2,0:T(2,128)S(1)}, s32[3,32,2]{1,2,0:T(2,128)}, u32[]{:S(2)}) copy-start(s32[3,32,2]{1,2,0:T(2,128)} %param.24) | copy-start | bytes 2308
  7.2 29.0 %slice-start.1 = ((s8[6291456]{0:T(1024)(128)(4,1)}), s8[2097152]{0:T(1024)(128)(4,1)S(1)}, s32[]{:S(2)}) async-start(s8[6291456]{0:T(1024)(128)(4,1)} %bitcast.12), calls=%async_computation.3 | async-start | bytes 4194304
  7.2 29.0 %slice-start.3 = ((s8[6291456]{0:T(1024)(128)(4,1)}), s8[2097152]{0:T(1024)(128)(4,1)S(1)}, s32[]{:S(2)}) async-start(s8[6291456]{0:T(1024)(128)(4,1)} %bitcast.14), calls=%async_computation.5 | async-start | bytes 4194304
  7.2 29.0 %copy-start = (bf16[3072,8]{0,1:T(8,128)(2,1)S(1)}, bf16[3072,8]{0,1:T(8,128)(2,1)}, u32[]{:S(2)}) copy-start(bf16[3072,8]{0,1:T(8,128)(2,1)} %param.23) | copy-start | bytes 147460
  7.2 29.0 %copy-start.2 = (f32[3072]{0:T(1024)S(1)}, f32[3072]{0:T(1024)}, u32[]{:S(2)}) copy-start(f32[3072]{0:T(1024)} %param.22) | copy-start | bytes 36868
  9.8 2.3 %collective-permute-start.1 = (bf16[72,128]{1,0:T(8,128)(2,1)S(1)}, bf16[72,128]{1,0:T(8,128)(2,1)S(1)}, u32[]{:S(2)}, u32[]{:S(2)}) collective-permute-start(bf16[72,128]{1,0:T(8,128)(2,1)S(1)} %shard_map.140), channel_id=1, source_target_pairs={{0,2},{2,0},{1,3},{3,1},{4,6},{6,4},{5,7},{7,5},{8,10},{10,8},{9,1... | collective-permute-start | bytes 55304 | tf_op jit(solution)/shard_map/ppermute | solution.py:435
  36.2 5.3 %slice-start.4 = ((s8[6291456]{0:T(1024)(128)(4,1)}), s8[4194304]{0:T(1024)(128)(4,1)S(1)}, s32[]{:S(2)}) async-start(s8[6291456]{0:T(1024)(128)(4,1)} %bitcast.16), calls=%async_computation.6 | async-start | bytes 8388608
  37.8 3.7 %collective-permute-start.3 = (bf16[112,512]{1,0:T(8,128)(2,1)S(1)}, bf16[112,512]{1,0:T(8,128)(2,1)S(1)}, u32[]{:S(2)}, u32[]{:S(2)}) collective-permute-start(bf16[112,512]{1,0:T(8,128)(2,1)S(1)} %get-tuple-element.22.own_ref), channel_id=1, source_target_pairs={{0,1},{1,0},{2,3},{3,2},{4,5},{5,4},{6,7},{7,6},{8,9},{9,8},{10,11... | collective-permute-start | bytes 344072 | tf_op jit(solution)/shard_map/ppermute | solution.py:461
  38.1 3.3 %slice-start.5 = ((s8[6291456]{0:T(1024)(128)(4,1)}), s8[2097152]{0:T(1024)(128)(4,1)S(1)}, s32[]{:S(2)}) async-start(s8[6291456]{0:T(1024)(128)(4,1)} %bitcast.16), calls=%async_computation.7 | async-start | bytes 4194304
  39.4 4.3 %collective-permute-start.2 = (bf16[96,512]{1,0:T(8,128)(2,1)S(1)}, bf16[96,512]{1,0:T(8,128)(2,1)S(1)}, u32[]{:S(2)}, u32[]{:S(2)}) collective-permute-start(bf16[96,512]{1,0:T(8,128)(2,1)S(1)} %shard_map.142.own_ref), channel_id=1, source_target_pairs={{0,1},{1,0},{2,3},{3,2},{4,5},{5,4},{6,7},{7,6},{8,9},{9,8},{10,11... | collective-permute-start | bytes 294920 | tf_op jit(solution)/shard_map/ppermute | solution.py:469
  61.1 4.2 %collective-permute-start.4 = (f32[72,128]{1,0:T(8,128)S(1)}, f32[72,128]{1,0:T(8,128)S(1)}, u32[]{:S(2)}, u32[]{:S(2)}) collective-permute-start(f32[72,128]{1,0:T(8,128)S(1)} %convert_reduce_fusion.own_ref), channel_id=1, source_target_pairs={{0,2},{2,0},{1,3},{3,1},{4,6},{6,4},{5,7},{7,5},{8,10},{10,8},{9,1... | collective-permute-start | bytes 110600 | tf_op jit(solution)/shard_map/ppermute | solution.py:489

commit v5 on v4

--- a/solution.py
+++ b/solution.py
@@ -13,7 +13,8 @@
 CAP = 48
 PAIRS = 2
 STEPS = 3
-PARTS = 4
+HALF_PARTS = 2
+PIECE = 40
 EXTRA = 16
 LANES = 128
 
@@ -190,26 +191,101 @@
     out_ref[...] = rows_ref[...].astype(bf16)
 
 
-def pack_pair(pair, scaled_refs, tables_ref, gate_ref, up_ref, out_ref, sums_ref, both_ref):
-    tokens, part = scaled_refs[0].shape
-    width = gate_ref.shape[2]
-    both_ref[:, tokens:, :] = jnp.zeros((2, LANES - tokens, 2 * width), bf16)
+def state_kernel(residual_ref, own_ref, other_ref, state_ref, sent_ref, rows_ref, wide_ref):
+    rows = state_ref.shape[0]
+    half = rows // 2
+    state = (
+        residual_ref[...] + (own_ref[...].astype(f32) + other_ref[...].astype(f32))
+    ).astype(bf16)
+    state_ref[...] = state
+    rows_ref[:rows, :] = state.astype(f32)
+    rows_ref[rows:, :] = jnp.zeros((rows_ref.shape[0] - rows, LANES), f32)
+    piece = jnp.where(
+        lax.axis_index("ep") == 0, rows_ref[:PIECE, :], rows_ref[half : half + PIECE, :]
+    )
+    for g in range(wide_ref.shape[0] // PIECE):
+        wide_ref[g * PIECE : (g + 1) * PIECE, :] = piece
+    sent_ref[...] = wide_ref[...].astype(bf16)
+
+
+def scale_half(first, state_ref, gain_ref, scaled_refs, wide_ref):
+    part = scaled_refs[0].shape[1]
+    groups = state_ref.shape[0] // PIECE
+    wide_ref[...] = state_ref[...].astype(f32)
+    squares = [jnp.zeros((groups, LANES), f32) for _ in range(STEPS)]
+    for k in range(len(scaled_refs) * part // LANES):
+        gain = gain_ref[:, pl.ds(pl.multiple_of(first + k * LANES, LANES), LANES)]
+        scaled_ref = scaled_refs[k * LANES // part]
+        column = k * LANES % part
+        for s in range(STEPS):
+            block = wide_ref[pl.ds(k * STEPS + s, groups, stride=PIECE), :]
+            squares[s] = squares[s] + block * block
+            scaled_ref[s * groups : (s + 1) * groups, column : column + LANES] = (
+                block * gain
+            ).astype(bf16)
+    return jnp.concatenate(squares, axis=0)
+
+
+def route_half(first, router_ref, scaled_refs):
+    part = scaled_refs[0].shape[1]
+    return sum(
+        lax.dot_general(
+            router_ref[:, pl.ds(pl.multiple_of(first + n * part, LANES), part)],
+            ref[...],
+            (((1,), (1,)), ((), ())),
+            preferred_element_type=f32,
+        )
+        for n, ref in enumerate(scaled_refs)
+    )
+
+
+def add_half(first, pair, scaled_refs, gate_ref, up_ref, before_ref, sums_ref, put):
+    part = scaled_refs[0].shape[1]
     last = len(scaled_refs) - 1
     for n, scaled_ref in enumerate(scaled_refs):
         scaled = scaled_ref[...]
+        depth = pl.ds(pl.multiple_of(first + n * part, LANES), part)
         for i in range(2):
             for j, weight_ref in enumerate((gate_ref, up_ref)):
                 terms = jnp.dot(
-                    scaled,
-                    weight_ref[2 * pair + i, n * part : (n + 1) * part, :],
-                    preferred_element_type=f32,
+                    scaled, weight_ref[2 * pair + i, depth, :], preferred_element_type=f32
                 )
                 if n > 0:
                     terms = terms + sums_ref[2 * i + j]
+                elif before_ref is not None:
+                    terms = terms + before_ref[4 * pair + 2 * i + j]
                 if n < last:
                     sums_ref[2 * i + j] = terms
                 else:
-                    both_ref[i, :tokens, j * width : (j + 1) * width] = terms.astype(bf16)
+                    put(i, j, terms)
+
+
+def own_half_kernel(
+    state_ref, gain_ref, router_ref, gate_ref, up_ref, terms_ref, square_ref, logits_ref, *refs
+):
+    *scaled_refs, wide_ref, sums_ref = refs
+    first = lax.axis_index("ep") * (len(scaled_refs) * scaled_refs[0].shape[1])
+    square_ref[...] = scale_half(first, state_ref, gain_ref, scaled_refs, wide_ref)
+    for pair in range(PAIRS):
+
+        def put(i, j, terms, pair=pair):
+            terms_ref[4 * pair + 2 * i + j] = terms
+
+        add_half(first, pair, scaled_refs, gate_ref, up_ref, None, sums_ref, put)
+    logits_ref[...] = route_half(first, router_ref, scaled_refs)
+
+
+def pack_pair(
+    first, pair, scaled_refs, tables_ref, gate_ref, up_ref, terms_ref, out_ref, sums_ref, both_ref
+):
+    tokens = scaled_refs[0].shape[0]
+    width = gate_ref.shape[2]
+    both_ref[:, tokens:, :] = jnp.zeros((2, LANES - tokens, 2 * width), bf16)
+
+    def put(i, j, terms):
+        both_ref[i, :tokens, j * width : (j + 1) * width] = terms.astype(bf16)
+
+    add_half(first, pair, scaled_refs, gate_ref, up_ref, terms_ref, sums_ref, put)
     for i in range(2):
         out_ref[i * CAP : (i + 1) * CAP, :] = jnp.dot(
             tables_ref[pair, i * CAP : (i + 1) * CAP, :],
@@ -219,38 +295,29 @@
 
 
 def hidden_kernel(
-    state_ref, gain_ref, router_ref, tables_ref, gate_ref, up_ref, out_ref, *refs
+    state_ref,
+    gain_ref,
+    router_ref,
+    tables_ref,
+    gate_ref,
+    up_ref,
+    terms_ref,
+    square_ref,
+    logits_ref,
+    out_ref,
+    *refs,
 ):
     *scaled_refs, wide_ref, sums_ref, both_ref = refs
-    tokens, part = scaled_refs[0].shape
-    blocks = len(scaled_refs) * part // LANES
-    stride = STEPS * blocks
-    groups = state_ref.shape[0] // stride
-    wide_ref[...] = state_ref[...].astype(f32)
-    squares = [jnp.zeros((groups, LANES), f32) for _ in range(STEPS)]
-    for k in range(blocks):
-        gain = gain_ref[:, k * LANES : (k + 1) * LANES]
-        scaled_ref = scaled_refs[k * LANES // part]
-        column = k * LANES % part
-        for s in range(STEPS):
-            block = wide_ref[pl.ds(k * STEPS + s, groups, stride=stride), :]
-            squares[s] = squares[s] + block * block
-            scaled_ref[s * groups : (s + 1) * groups, column : column + LANES] = (
-                block * gain
-            ).astype(bf16)
-    pack_pair(0, scaled_refs, tables_ref, gate_ref, up_ref, out_ref, sums_ref, both_ref)
-    square = jnp.sum(jnp.concatenate(squares, axis=0), axis=1, keepdims=True)
+    tokens = scaled_refs[0].shape[0]
+    first = (1 - lax.axis_index("ep")) * (len(scaled_refs) * scaled_refs[0].shape[1])
+    squares = square_ref[...] + scale_half(first, state_ref, gain_ref, scaled_refs, wide_ref)
+    pack_pair(
+        first, 0, scaled_refs, tables_ref, gate_ref, up_ref, terms_ref, out_ref, sums_ref, both_ref
+    )
+    square = jnp.sum(squares, axis=1, keepdims=True)
     diagonal = iota((tokens, LANES), 0) == iota((tokens, LANES), 1)
     square = jnp.sum(jnp.where(diagonal, square, 0.0), axis=0, keepdims=True)
-    router = sum(
-        lax.dot_general(
-            router_ref[:, n * part : (n + 1) * part],
-            ref[...],
-            (((1,), (1,)), ((), ())),
-            preferred_element_type=f32,
-        )
-        for n, ref in enumerate(scaled_refs)
-    )
+    router = logits_ref[...] + route_half(first, router_ref, scaled_refs)
     router = jnp.concatenate([router, jnp.zeros((E, LANES - tokens), f32)], axis=1)
     high, middle, _ = pieces(router)
     square_high, square_middle, _ = pieces(square)
@@ -269,8 +336,11 @@
 
 
 def hidden_rest_kernel(*refs):
-    *scaled_refs, tables_ref, gate_ref, up_ref, out_ref, sums_ref, both_ref = refs
-    pack_pair(1, scaled_refs, tables_ref, gate_ref, up_ref, out_ref, sums_ref, both_ref)
+    *scaled_refs, tables_ref, gate_ref, up_ref, terms_ref, out_ref, sums_ref, both_ref = refs
+    first = (1 - lax.axis_index("ep")) * (len(scaled_refs) * scaled_refs[0].shape[1])
+    pack_pair(
+        first, 1, scaled_refs, tables_ref, gate_ref, up_ref, terms_ref, out_ref, sums_ref, both_ref
+    )
 
 
 def spread_pair(own_ref, other_ref, factors, turned, side_ref, tokens):
@@ -332,36 +402,66 @@
     )
 
 
-def down_rest_kernel(
-    own_ref, other_ref, terms_ref, factors_ref, turned_ref, down_ref, out_ref, side_ref, wide_ref
-):
-    tokens = terms_ref.shape[0]
-    width = down_ref.shape[1]
-    blocks = down_ref.shape[2] // LANES
-    stride = STEPS * blocks
-    groups = tokens // STEPS
-    mixed = spread_pair(own_ref, other_ref, factors_ref[...], turned_ref[1], side_ref, tokens)
+def half_terms(first, mixed, terms_ref, down_ref, width, put):
+    depth = down_ref.shape[1]
     chunk = 4 * LANES
-    for n in range(down_ref.shape[2] // chunk):
-        terms = terms_ref[:, n * chunk : (n + 1) * chunk]
+    for n in range(width // chunk):
+        columns = pl.ds(pl.multiple_of(first + n * chunk, LANES), chunk)
+        terms = terms_ref[:, columns]
         for i in range(2):
             terms = terms + jnp.dot(
-                mixed[:, i * width : (i + 1) * width],
-                down_ref[2 + i, :, n * chunk : (n + 1) * chunk],
+                mixed[:, i * depth : (i + 1) * depth],
+                down_ref[2 + i, :, columns],
                 preferred_element_type=f32,
             )
-        for j in range(chunk // LANES):
-            k = n * (chunk // LANES) + j
-            for s in range(STEPS):
-                wide_ref[pl.ds(k * STEPS + s, groups, stride=stride), :] = terms[
-                    s * groups : (s + 1) * groups, j * LANES : (j + 1) * LANES
-                ]
+        put(n * chunk, terms)
+
+
+def down_away_kernel(
+    own_ref, other_ref, terms_ref, factors_ref, turned_ref, down_ref, away_ref, mixed_ref, side_ref
+):
+    tokens, width = away_ref.shape
+    mixed = spread_pair(own_ref, other_ref, factors_ref[...], turned_ref[1], side_ref, tokens)
+    mixed_ref[...] = mixed
+
+    def put(column, terms):
+        away_ref[:, column : column + terms.shape[1]] = terms.astype(bf16)
+
+    first = (1 - lax.axis_index("ep")) * width
+    half_terms(first, mixed, terms_ref, down_ref, width, put)
+
+
+def down_here_kernel(mixed_ref, terms_ref, down_ref, here_ref):
+    width = here_ref.shape[1]
+
+    def put(column, terms):
+        here_ref[:, column : column + terms.shape[1]] = terms
+
+    half_terms(lax.axis_index("ep") * width, mixed_ref[...], terms_ref, down_ref, width, put)
+
+
+def send_kernel(here_ref, came_ref, out_ref, wide_ref):
+    groups = here_ref.shape[0] // STEPS
+    blocks = here_ref.shape[1] // LANES
+    wide_ref[...] = jnp.zeros(wide_ref.shape, f32)
+    for k in range(blocks):
+        columns = slice(k * LANES, (k + 1) * LANES)
+        for s in range(STEPS):
+            tokens = slice(s * groups, (s + 1) * groups)
+            wide_ref[pl.ds(k * STEPS + s, groups, stride=PIECE), :] = here_ref[
+                tokens, columns
+            ] + came_ref[tokens, columns].astype(f32)
     out_ref[...] = wide_ref[...].astype(bf16)
 
 
 def output_kernel(state_ref, own_ref, other_ref, out_ref, rows_ref):
     steps, width = out_ref.shape
-    rows_ref[...] = state_ref[...].astype(f32) + (own_ref[...] + other_ref[...])
+    half = state_ref.shape[0] // 2
+    lower = lax.axis_index("ep") == 0
+    own, other = own_ref[...], other_ref[...]
+    rows_ref[:PIECE, :] = jnp.where(lower, own, other)
+    rows_ref[half : half + PIECE, :] = jnp.where(lower, other, own)
+    rows_ref[: 2 * half, :] = state_ref[...].astype(f32) + rows_ref[: 2 * half, :]
     for k in range(width // LANES):
         out_ref[:, k * LANES : (k + 1) * LANES] = rows_ref[k * steps : (k + 1) * steps, :].astype(
             bf16
@@ -433,37 +533,62 @@
         beside=20,
     )
     other_terms = lax.ppermute(terms, "ep", swap)
-    state = (residual_rows + (terms.astype(f32) + other_terms.astype(f32))).astype(bf16)
-    all_state = lax.all_to_all(
-        jnp.broadcast_to(state[None], (groups, rows, LANES)), "grp", 0, 0
-    ).reshape(groups * rows, LANES)
-    hidden_width = 2 * expert_gate.shape[2]
+    state, sent_state = call(
+        state_kernel,
+        (struct((rows, LANES), bf16), struct((groups * PIECE, LANES), bf16)),
+        (residual_rows, terms, other_terms),
+        [VMEM] * 3,
+        [pltpu.VMEM((2 * PIECE, LANES), f32), pltpu.VMEM((groups * PIECE, LANES), f32)],
+    )
+    own_state = lax.all_to_all(
+        sent_state.reshape(groups, PIECE, LANES), "grp", 0, 0
+    ).reshape(groups * PIECE, LANES)
+    other_state = lax.ppermute(own_state, "ep", swap)
+    gain = norm_gain.reshape(1, -1)
+    router = router_weight.T
+    expert_width = expert_gate.shape[2]
+    hidden_width = 2 * expert_width
+    part = (token_count, width // (2 * HALF_PARTS))
+    wide = pltpu.VMEM((groups * PIECE, LANES), f32)
+    sums = pltpu.VMEM((4, token_count, expert_width), f32)
     both = pltpu.VMEM((2, LANES, hidden_width), bf16)
-    sums = pltpu.VMEM((4, token_count, hidden_width // 2), f32)
+    own_terms, squares, logits = call(
+        own_half_kernel,
+        (
+            struct((4 * PAIRS, token_count, expert_width), f32),
+            struct((token_count, LANES), f32),
+            struct((E, token_count), f32),
+        ),
+        (own_state, gain, router, expert_gate, expert_up),
+        [VMEM] * 5,
+        [pltpu.VMEM(part, bf16)] * HALF_PARTS + [wide, sums],
+    )
     hidden, *scaled = call(
         hidden_kernel,
         (
             struct((2 * CAP + EXTRA, hidden_width), bf16),
-            *[struct((token_count, width // PARTS), bf16)] * PARTS,
+            *[struct(part, bf16)] * HALF_PARTS,
         ),
         (
-            all_state,
-            norm_gain.reshape(1, -1),
-            router_weight.T,
+            other_state,
+            gain,
+            router,
             tables,
             expert_gate,
             expert_up,
+            own_terms,
+            squares,
+            logits,
         ),
-        [VMEM] * 6,
-        [pltpu.VMEM((groups * rows, LANES), f32), sums, both],
-        limit=8,
+        [VMEM] * 9,
+        [wide, sums, both],
     )
     other_hidden = lax.ppermute(hidden, "tp", swap)
     hidden_rest = call(
         hidden_rest_kernel,
         struct((2 * CAP, hidden_width), bf16),
-        (*scaled, tables, expert_gate, expert_up),
-        [VMEM] * (PARTS + 3),
+        (*scaled, tables, expert_gate, expert_up, own_terms),
+        [VMEM] * (HALF_PARTS + 4),
         [sums, both],
     )
     other_hidden_rest = lax.ppermute(hidden_rest, "tp", swap)
@@ -476,15 +601,29 @@
         [side],
         limit=8,
     )
-    sent = call(
-        down_rest_kernel,
-        struct((groups * rows, LANES), bf16),
+    half = width // 2
+    away, spread = call(
+        down_away_kernel,
+        (struct((token_count, half), bf16), struct((token_count, hidden_width), bf16)),
         (hidden_rest, other_hidden_rest, down_terms, factors, turned, expert_down),
         [VMEM] * 6,
-        [side, pltpu.VMEM((groups * rows, LANES), f32)],
-        limit=8,
-    )
-    received = lax.all_to_all(sent.reshape(groups, rows, LANES), "grp", 0, 0)
+        [side],
+    )
+    came = lax.ppermute(away, "ep", swap)
+    here = call(
+        down_here_kernel,
+        struct((token_count, half), f32),
+        (spread, down_terms, expert_down),
+        [VMEM] * 3,
+    )
+    sent = call(
+        send_kernel,
+        struct((groups * PIECE, LANES), bf16),
+        (here, came),
+        [VMEM] * 2,
+        [wide],
+    )
+    received = lax.all_to_all(sent.reshape(groups, PIECE, LANES), "grp", 0, 0)
     summed = jnp.sum(received.astype(f32), axis=0)
     other_summed = lax.ppermute(summed, "ep", swap)
     mixed = call(
@@ -492,7 +631,7 @@
         struct((steps, width), bf16),
         (state, summed, other_summed),
         [VMEM] * 3,
-        [pltpu.VMEM((rows, LANES), f32)],
+        [pltpu.VMEM((2 * PIECE, LANES), f32)],
     )
     return mixed[:, None]
 

time: 66.1 us -> 64.8 us (0.980)
  blocking collectives: 40.3 us -> 35.7 us
  waiting for transfers between devices: 4.92 us -> 6.85 us
  starting transfers between devices: 8.5 us -> 9.47 us
    all_to_all x2, blocking collectives: 40.3 us -> 35.7 us  [the longest x1 21.4 us: on_device(): lax.all_to_all(sent_state.reshape(groups, PIECE, LANES), 'grp', 0, 0)]
    ppermute x0 -> x2, starting transfers between devices: none -> 2.72 us  [the longest x1 1.54 us: on_device(): other_state = lax.ppermute(own_state, 'ep', swap)]
    ppermute x1, starting transfers between devices: 3.34 us -> 1.61 us  [on_device(): other_summed = lax.ppermute(summed, 'ep', swap)]
    ppermute x1, waiting for transfers between devices: 0.83 us -> 2.13 us  [on_device(): other_hidden = lax.ppermute(hidden, 'tp', swap)]
    ppermute x0 -> x2, waiting for transfers between devices: none -> 0.81 us  [the longest x1 0.81 us: on_device(): came = lax.ppermute(away, 'ep', swap)]
    pallas_call x10 -> x14, Pallas kernels: 8.95 us -> 9.42 us  [call(): pl.pallas_call(kernel, out_shape=out, in_specs=specs, out_specs=jax.tree....]
  transfers between devices with their start and end apart: 5 -> 7, of which waited for: 5 -> 6; matrix products, arithmetic and copies ran while one was open for 0% -> 0% of each run, Pallas kernels for 4% -> 6%
where the time goes in v5:
time: 64.8 us; the launch traced here: 64.6 us
  blocking collectives  35.7 us (55%)
  starting transfers between devices  9.47 us (15%)
  Pallas kernels  9.42 us (15%)
  waiting for transfers between devices  6.85 us (11%)
  local copies, waits for them, and re-layouts  2.16 us (3%)
  between operations  0.91 us (1%)
    all_to_all x1, blocking collectives, on_device(): lax.all_to_all(sent_state.reshape(groups, PIECE, LANES), 'grp', 0, 0)  21.4 us
    all_to_all x1, blocking collectives, on_device(): received = lax.all_to_all(sent.reshape(groups, PIECE, LANES), 'grp', 0, 0)  14.3 us
    pallas_call x14, Pallas kernels, call(): pl.pallas_call(kernel, out_shape=out, in_specs=specs, out_specs=jax.tree....  9.42 us
    unnamed x32, local copies, waits for them, and re-layouts  2.16 us
    ppermute x1, waiting for transfers between devices, on_device(): other_hidden = lax.ppermute(hidden, 'tp', swap)  2.13 us
    ppermute x1, starting transfers between devices, on_device(): other = lax.ppermute(partial, 'tp', swap)  2.12 us
    ppermute x1, starting transfers between devices, on_device(): other_summed = lax.ppermute(summed, 'ep', swap)  1.61 us
    ppermute x1, starting transfers between devices, on_device(): other_state = lax.ppermute(own_state, 'ep', swap)  1.54 us
  transfers between devices with their start and end apart: 7, of which 6 were waited for; matrix products, arithmetic and copies ran while one was open for 0% of the time, Pallas kernels for 6%

profile of v5, /device:TPU:1, one launch (start us, length us, event | category | flops | bytes accessed | tf_op | source)
XLA Modules:
  0.0 64.6 jit_solution(12005984179391099686)
XLA Ops:
  1.2 0.6 shard_map.138.own_ref
  1.8 2.1 %collective-permute-start = (bf16[72,256]{1,0:T(8,128)(2,1)S(1)}, bf16[72,256]{1,0:T(8,128)(2,1)S(1)}, u32[]{:S(2)}, u32[]{:S(2)}) collective-permute-start(bf16[72,256]{1,0:T(8,128)(2,1)S(1)} %shard_map.138.own_ref), channel_id=1, source_target_pairs={{0,1},{1,0},{2,3},{3,2},{4,5},{5,4},{6,7},{7,6},{8,9},{9,8},{10,11... | collective-permute-start | bytes 110600 | tf_op jit(solution)/shard_map/ppermute | solution.py:518
  3.9 1.3 %collective-permute-done.other_ref = bf16[72,256]{1,0:T(8,128)(2,1)S(1)} collective-permute-done((bf16[72,256]{1,0:T(8,128)(2,1)S(1)}, bf16[72,256]{1,0:T(8,128)(2,1)S(1)}, u32[]{:S(2)}, u32[]{:S(2)}) %collective-permute-start) | collective-permute-done | bytes 36896 | tf_op jit(solution)/shard_map/ppermute | solution.py:518
  5.5 1.7 %copy-done.4 = bf16[3072,3072]{1,0:T(8,128)(2,1)S(1)} copy-done((bf16[3072,3072]{1,0:T(8,128)(2,1)S(1)}, bf16[3072,3072]{1,0:T(8,128)(2,1)}, u32[]{:S(2)}) %copy-start.4) | copy-done | bytes 18874392
  7.2 2.5 %shard_map.140.own_ref = bf16[72,128]{1,0:T(8,128)(2,1)S(1)} custom-call(bf16[3,3072]{1,0:T(4,128)(2,1)S(1)} %shard_map.139.attended_ref, bf16[3072,3072]{1,0:T(8,128)(2,1)S(1)} %copy-done.4), custom_call_target="tpu_custom_call" | custom-call | flops 20000000000 | tf_op jit(solution)/shard_map/pallas_call | solution.py:31
  9.8 1.4 %collective-permute-start.1 = (bf16[72,128]{1,0:T(8,128)(2,1)S(1)}, bf16[72,128]{1,0:T(8,128)(2,1)S(1)}, u32[]{:S(2)}, u32[]{:S(2)}) collective-permute-start(bf16[72,128]{1,0:T(8,128)(2,1)S(1)} %shard_map.140.own_ref), channel_id=1, source_target_pairs={{0,2},{2,0},{1,3},{3,1},{4,6},{6,4},{5,7},{7,5},{8,10},{10,8},{9,1... | collective-permute-start | bytes 55304 | tf_op jit(solution)/shard_map/ppermute | solution.py:535
  11.5 0.5 collective-permute-done.1.other_ref
  12.1 21.4 %all_to_all.10 = bf16[32,40,128]{2,1,0:T(8,128)(2,1)S(1)} all-to-all(bf16[32,40,128]{2,1,0:T(8,128)(2,1)S(1)} %bitcast.22), channel_id=1, replica_groups=mesh['grp'=32,'ep'=2,'tp'=2] {'grp'}, dimensions={0} | all-to-all | bytes 655360 | tf_op jit(solution)/shard_map/all_to_all | solution.py:543
  33.5 1.5 %collective-permute-start.2 = (bf16[1280,128]{1,0:T(8,128)(2,1)S(1)}, bf16[1280,128]{1,0:T(8,128)(2,1)S(1)}, u32[]{:S(2)}, u32[]{:S(2)}) collective-permute-start(bf16[1280,128]{1,0:T(8,128)(2,1)S(1)} %bitcast.20), channel_id=1, source_target_pairs={{0,2},{2,0},{1,3},{3,1},{4,6},{6,4},{5,7},{7,5},{8,10},{10,8},{9,1... | collective-permute-start | bytes 983048 | tf_op jit(solution)/shard_map/ppermute | solution.py:546
  35.1 1.3 %shard_map.142 = (f32[8,96,256]{2,1,0:T(8,128)S(1)}, f32[96,128]{1,0:T(8,128)S(1)}, f32[8,96]{1,0:T(8,128)S(1)}) custom-call(bf16[1280,128]{1,0:T(8,128)(2,1)S(1)} %bitcast.21, f32[1,3072]{1,0:T(1,128)S(1)} %bitcast.25, bf16[8,3072]{1,0:T(8,128)(2,1)S(1)} %bitcast.23, bf16[4,3072,256]{2,1,0:T(8,128)(2,1)S(1)} %bitcast.14, bf16[4,3072,256]{2,1,0:T(8,128)(2,1)S(1)} %bitcast.16), custom_call_target="tpu_custom_call" | custom-call | tf_op jit(solution)/shard_map/pallas_call | solution.py:31
  36.4 0.9 %shard_map.143 = (bf16[112,512]{1,0:T(8,128)(2,1)S(1)}, bf16[96,768]{1,0:T(8,128)(2,1)S(1)}, bf16[96,768]{1,0:T(8,128)(2,1)S(1)}) custom-call(bf16[1280,128]{1,0:T(8,128)(2,1)S(1)} %collective-permute-done.2.state_ref, f32[1,3072]{1,0:T(1,128)S(1)} %bitcast.26, bf16[8,3072]{1,0:T(8,128)(2,1)S(1)} %bitcast.24, ...), custom_call_target="tpu_custom_call" | custom-call | tf_op jit(solution)/shard_map/pallas_call | solution.py:31
  37.7 0.8 %shard_map.144.own_ref = bf16[96,512]{1,0:T(8,128)(2,1)S(1)} custom-call(bf16[96,768]{1,0:T(8,128)(2,1)S(1)} %get-tuple-element.28.refs_0_, bf16[96,768]{1,0:T(8,128)(2,1)S(1)} %get-tuple-element.29.refs_1_, bf16[2,128,128]{2,1,0:T(8,128)(2,1)S(1)} %get-tuple-element.24.tables_ref.refs_2_, bf16[4,3072,256]{2,1,0:T(8,128)(2,1)S(1)} %bitcast.14, ...), custom_call_target="tpu_custom_call" | custom-call | tf_op jit(solution)/shard_map/pallas_call | solution.py:31
  38.5 1.2 %collective-permute-start.3 = (bf16[96,512]{1,0:T(8,128)(2,1)S(1)}, bf16[96,512]{1,0:T(8,128)(2,1)S(1)}, u32[]{:S(2)}, u32[]{:S(2)}) collective-permute-start(bf16[96,512]{1,0:T(8,128)(2,1)S(1)} %shard_map.144.own_ref), channel_id=1, source_target_pairs={{0,1},{1,0},{2,3},{3,2},{4,5},{5,4},{6,7},{7,6},{8,9},{9,8},{10,11... | collective-permute-start | bytes 294920 | tf_op jit(solution)/shard_map/ppermute | solution.py:594
  39.7 2.1 %collective-permute-done.4.other_ref = bf16[112,512]{1,0:T(8,128)(2,1)S(1)} collective-permute-done((bf16[112,512]{1,0:T(8,128)(2,1)S(1)}, bf16[112,512]{1,0:T(8,128)(2,1)S(1)}, u32[]{:S(2)}, u32[]{:S(2)}) %collective-permute-start.4) | collective-permute-done | bytes 114720 | tf_op jit(solution)/shard_map/ppermute | solution.py:586
  41.9 0.9 %shard_map.145 = (f32[96,3072]{1,0:T(8,128)S(1)}, f32[96,128]{1,0:T(8,128)S(1)}) custom-call(bf16[112,512]{1,0:T(8,128)(2,1)S(1)} %get-tuple-element.30.own_ref, bf16[112,512]{1,0:T(8,128)(2,1)S(1)} %collective-permute-done.4.other_ref, s32[2,128]{1,0:T(2,128)S(1)} %get-tuple-element.31.routes_ref, ...), custom_call_target="tpu_custom_call" | custom-call | tf_op jit(solution)/shard_map/pallas_call | solution.py:31
  42.8 1.2 %collective-permute-done.3.other_ref = bf16[96,512]{1,0:T(8,128)(2,1)S(1)} collective-permute-done((bf16[96,512]{1,0:T(8,128)(2,1)S(1)}, bf16[96,512]{1,0:T(8,128)(2,1)S(1)}, u32[]{:S(2)}, u32[]{:S(2)}) %collective-permute-start.3) | collective-permute-done | bytes 98336 | tf_op jit(solution)/shard_map/ppermute | solution.py:594
  44.0 0.6 shard_map.146
  44.6 1.2 %collective-permute-start.5 = (bf16[96,1536]{1,0:T(8,128)(2,1)S(1)}, bf16[96,1536]{1,0:T(8,128)(2,1)S(1)}, u32[]{:S(2)}, u32[]{:S(2)}) collective-permute-start(bf16[96,1536]{1,0:T(8,128)(2,1)S(1)} %get-tuple-element.36), channel_id=1, source_target_pairs={{0,2},{2,0},{1,3},{3,1},{4,6},{6,4},{5,7},{7,5},{8,10},{10,8},{9,1... | collective-permute-start | bytes 884744 | tf_op jit(solution)/shard_map/ppermute | solution.py:612
  45.7 0.4 shard_map.147.here_ref
  46.1 0.8 %collective-permute-done.5.came_ref = bf16[96,1536]{1,0:T(8,128)(2,1)S(1)} collective-permute-done((bf16[96,1536]{1,0:T(8,128)(2,1)S(1)}, bf16[96,1536]{1,0:T(8,128)(2,1)S(1)}, u32[]{:S(2)}, u32[]{:S(2)}) %collective-permute-start.5) | collective-permute-done | bytes 294944 | tf_op jit(solution)/shard_map/ppermute | solution.py:612
  47.2 14.3 %all_to_all.11 = bf16[32,40,128]{2,1,0:T(8,128)(2,1)S(1)} all-to-all(bf16[32,40,128]{2,1,0:T(8,128)(2,1)S(1)} %bitcast.19), channel_id=1, replica_groups=mesh['grp'=32,'ep'=2,'tp'=2] {'grp'}, dimensions={0} | all-to-all | bytes 655360 | tf_op jit(solution)/shard_map/all_to_all | solution.py:626
  61.5 1.6 %collective-permute-start.6 = (f32[40,128]{1,0:T(8,128)S(1)}, f32[40,128]{1,0:T(8,128)S(1)}, u32[]{:S(2)}, u32[]{:S(2)}) collective-permute-start(f32[40,128]{1,0:T(8,128)S(1)} %convert_reduce_fusion.own_ref), channel_id=1, source_target_pairs={{0,2},{2,0},{1,3},{3,1},{4,6},{6,4},{5,7},{7,5},{8,10},{10,8},{9,1... | collective-permute-start | bytes 61448 | tf_op jit(solution)/shard_map/ppermute | solution.py:628
  63.1 0.8 %collective-permute-done.6.other_ref = f32[40,128]{1,0:T(8,128)S(1)} collective-permute-done((f32[40,128]{1,0:T(8,128)S(1)}, f32[40,128]{1,0:T(8,128)S(1)}, u32[]{:S(2)}, u32[]{:S(2)}) %collective-permute-start.6) | collective-permute-done | bytes 20512 | tf_op jit(solution)/shard_map/ppermute | solution.py:628
  63.9 0.6 shard_map.149
  (42 shorter events, 1.7 us)
Async XLA Ops:
  0.0 1.1 %copy-start.6 = (bf16[1,512,512]{2,1,0:T(8,128)(2,1)S(1)}, bf16[1,512,512]{2,1,0:T(8,128)(2,1)}, u32[]{:S(2)}) copy-start(bf16[1,512,512]{2,1,0:T(8,128)(2,1)} %param.18) | copy-start | bytes 1572868
  0.0 1.2 %copy-start.5 = (bf16[1,512,512]{2,1,0:T(8,128)(2,1)S(1)}, bf16[1,512,512]{2,1,0:T(8,128)(2,1)}, u32[]{:S(2)}) copy-start(bf16[1,512,512]{2,1,0:T(8,128)(2,1)} %param.17) | copy-start | bytes 1572868
  0.0 1.2 %copy-start.9 = (bf16[3,1,512]{2,0,1:T(4,128)(2,1)S(1)}, bf16[3,1,512]{2,0,1:T(4,128)(2,1)}, u32[]{:S(2)}) copy-start(bf16[3,1,512]{2,0,1:T(4,128)(2,1)} %param.16) | copy-start | bytes 9220
  0.0 1.2 %copy-start.8 = (bf16[3,1,512]{2,0,1:T(4,128)(2,1)S(1)}, bf16[3,1,512]{2,0,1:T(4,128)(2,1)}, u32[]{:S(2)}) copy-start(bf16[3,1,512]{2,0,1:T(4,128)(2,1)} %param.15) | copy-start | bytes 9220
  0.0 1.2 %copy-start.7 = (bf16[3,1,3072]{2,0,1:T(4,128)(2,1)S(1)}, bf16[3,1,3072]{2,0,1:T(4,128)(2,1)}, u32[]{:S(2)}) copy-start(bf16[3,1,3072]{2,0,1:T(4,128)(2,1)} %param.14) | copy-start | bytes 55300
  0.8 6.4 %copy-start.4 = (bf16[3072,3072]{1,0:T(8,128)(2,1)S(1)}, bf16[3072,3072]{1,0:T(8,128)(2,1)}, u32[]{:S(2)}) copy-start(bf16[3072,3072]{1,0:T(8,128)(2,1)} %weight_ref.1) | copy-start | bytes 56623108
  1.8 3.5 %collective-permute-start = (bf16[72,256]{1,0:T(8,128)(2,1)S(1)}, bf16[72,256]{1,0:T(8,128)(2,1)S(1)}, u32[]{:S(2)}, u32[]{:S(2)}) collective-permute-start(bf16[72,256]{1,0:T(8,128)(2,1)S(1)} %shard_map.138.own_ref), channel_id=1, source_target_pairs={{0,1},{1,0},{2,3},{3,2},{4,5},{5,4},{6,7},{7,6},{8,9},{9,8},{10,11... | collective-permute-start | bytes 110600 | tf_op jit(solution)/shard_map/ppermute | solution.py:518
  5.3 29.8 %slice-start = ((s8[6291456]{0:T(1024)(128)(4,1)}), s8[4194304]{0:T(1024)(128)(4,1)S(1)}, s32[]{:S(2)}) async-start(s8[6291456]{0:T(1024)(128)(4,1)} %bitcast.13), calls=%async_computation.2 | async-start | bytes 8388608
  5.3 29.8 %slice-start.2 = ((s8[6291456]{0:T(1024)(128)(4,1)}), s8[4194304]{0:T(1024)(128)(4,1)S(1)}, s32[]{:S(2)}) async-start(s8[6291456]{0:T(1024)(128)(4,1)} %bitcast.15), calls=%async_computation.4 | async-start | bytes 8388608
  7.2 4.0 %copy-start.2 = (bf16[3,1,3072]{2,0,1:T(4,128)(2,1)S(1)}, bf16[3,1,3072]{2,0,1:T(4,128)(2,1)}, u32[]{:S(2)}) copy-start(bf16[3,1,3072]{2,0,1:T(4,128)(2,1)} %param.20) | copy-start | bytes 55300
  7.2 4.0 %copy-start.3 = (s32[3,32,2]{1,2,0:T(2,128)S(1)}, s32[3,32,2]{1,2,0:T(2,128)}, u32[]{:S(2)}) copy-start(s32[3,32,2]{1,2,0:T(2,128)} %param.24) | copy-start | bytes 2308
  7.2 27.9 %slice-start.1 = ((s8[6291456]{0:T(1024)(128)(4,1)}), s8[2097152]{0:T(1024)(128)(4,1)S(1)}, s32[]{:S(2)}) async-start(s8[6291456]{0:T(1024)(128)(4,1)} %bitcast.13), calls=%async_computation.3 | async-start | bytes 4194304
  7.2 27.9 %slice-start.3 = ((s8[6291456]{0:T(1024)(128)(4,1)}), s8[2097152]{0:T(1024)(128)(4,1)S(1)}, s32[]{:S(2)}) async-start(s8[6291456]{0:T(1024)(128)(4,1)} %bitcast.15), calls=%async_computation.5 | async-start | bytes 4194304
  7.2 27.9 %copy-start = (bf16[3072,8]{0,1:T(8,128)(2,1)S(1)}, bf16[3072,8]{0,1:T(8,128)(2,1)}, u32[]{:S(2)}) copy-start(bf16[3072,8]{0,1:T(8,128)(2,1)} %param.23) | copy-start | bytes 147460
  7.2 27.9 %copy-start.1 = (f32[3072]{0:T(1024)S(1)}, f32[3072]{0:T(1024)}, u32[]{:S(2)}) copy-start(f32[3072]{0:T(1024)} %param.22) | copy-start | bytes 36868
  9.8 2.3 %collective-permute-start.1 = (bf16[72,128]{1,0:T(8,128)(2,1)S(1)}, bf16[72,128]{1,0:T(8,128)(2,1)S(1)}, u32[]{:S(2)}, u32[]{:S(2)}) collective-permute-start(bf16[72,128]{1,0:T(8,128)(2,1)S(1)} %shard_map.140.own_ref), channel_id=1, source_target_pairs={{0,2},{2,0},{1,3},{3,1},{4,6},{6,4},{5,7},{7,5},{8,10},{10,8},{9,1... | collective-permute-start | bytes 55304 | tf_op jit(solution)/shard_map/ppermute | solution.py:535
  33.5 2.9 %collective-permute-start.2 = (bf16[1280,128]{1,0:T(8,128)(2,1)S(1)}, bf16[1280,128]{1,0:T(8,128)(2,1)S(1)}, u32[]{:S(2)}, u32[]{:S(2)}) collective-permute-start(bf16[1280,128]{1,0:T(8,128)(2,1)S(1)} %bitcast.20), channel_id=1, source_target_pairs={{0,2},{2,0},{1,3},{3,1},{4,6},{6,4},{5,7},{7,5},{8,10},{10,8},{9,1... | collective-permute-start | bytes 983048 | tf_op jit(solution)/shard_map/ppermute | solution.py:546
  35.1 6.7 %slice-start.4 = ((s8[6291456]{0:T(1024)(128)(4,1)}), s8[4194304]{0:T(1024)(128)(4,1)S(1)}, s32[]{:S(2)}) async-start(s8[6291456]{0:T(1024)(128)(4,1)} %bitcast.17), calls=%async_computation.6 | async-start | bytes 8388608
  36.4 5.4 %slice-start.5 = ((s8[6291456]{0:T(1024)(128)(4,1)}), s8[2097152]{0:T(1024)(128)(4,1)S(1)}, s32[]{:S(2)}) async-start(s8[6291456]{0:T(1024)(128)(4,1)} %bitcast.17), calls=%async_computation.7 | async-start | bytes 4194304
  37.4 4.5 %collective-permute-start.4 = (bf16[112,512]{1,0:T(8,128)(2,1)S(1)}, bf16[112,512]{1,0:T(8,128)(2,1)S(1)}, u32[]{:S(2)}, u32[]{:S(2)}) collective-permute-start(bf16[112,512]{1,0:T(8,128)(2,1)S(1)} %get-tuple-element.30.own_ref), channel_id=1, source_target_pairs={{0,1},{1,0},{2,3},{3,2},{4,5},{5,4},{6,7},{7,6},{8,9},{9,8},{10,11... | collective-permute-start | bytes 344072 | tf_op jit(solution)/shard_map/ppermute | solution.py:586
  38.5 5.5 %collective-permute-start.3 = (bf16[96,512]{1,0:T(8,128)(2,1)S(1)}, bf16[96,512]{1,0:T(8,128)(2,1)S(1)}, u32[]{:S(2)}, u32[]{:S(2)}) collective-permute-start(bf16[96,512]{1,0:T(8,128)(2,1)S(1)} %shard_map.144.own_ref), channel_id=1, source_target_pairs={{0,1},{1,0},{2,3},{3,2},{4,5},{5,4},{6,7},{7,6},{8,9},{9,8},{10,11... | collective-permute-start | bytes 294920 | tf_op jit(solution)/shard_map/ppermute | solution.py:594
  44.6 2.4 %collective-permute-start.5 = (bf16[96,1536]{1,0:T(8,128)(2,1)S(1)}, bf16[96,1536]{1,0:T(8,128)(2,1)S(1)}, u32[]{:S(2)}, u32[]{:S(2)}) collective-permute-start(bf16[96,1536]{1,0:T(8,128)(2,1)S(1)} %get-tuple-element.36), channel_id=1, source_target_pairs={{0,2},{2,0},{1,3},{3,1},{4,6},{6,4},{5,7},{7,5},{8,10},{10,8},{9,1... | collective-permute-start | bytes 884744 | tf_op jit(solution)/shard_map/ppermute | solution.py:612
  61.5 2.5 %collective-permute-start.6 = (f32[40,128]{1,0:T(8,128)S(1)}, f32[40,128]{1,0:T(8,128)S(1)}, u32[]{:S(2)}, u32[]{:S(2)}) collective-permute-start(f32[40,128]{1,0:T(8,128)S(1)} %convert_reduce_fusion.own_ref), channel_id=1, source_target_pairs={{0,2},{2,0},{1,3},{3,1},{4,6},{6,4},{5,7},{7,5},{8,10},{10,8},{9,1... | collective-permute-start | bytes 61448 | tf_op jit(solution)/shard_map/ppermute | solution.py:628

commit v6 on v5

--- a/solution.py
+++ b/solution.py
@@ -14,6 +14,7 @@
 PAIRS = 2
 STEPS = 3
 HALF_PARTS = 2
+HALF_ROWS = 36
 PIECE = 40
 EXTRA = 16
 LANES = 128
@@ -67,6 +68,8 @@
         rows_ref[k * steps : (k + 1) * steps, :] = residual_ref[
             :, k * LANES : (k + 1) * LANES
         ].astype(f32)
+    used = steps * width // LANES
+    rows_ref[used:, :] = jnp.zeros((rows_ref.shape[0] - used, LANES), f32)
     routes_row_ref[...] = jnp.full(routes_row_ref.shape, -1, jnp.int32)
     for s in range(steps):
         routes_row_ref[:, s * groups : (s + 1) * groups] = routes_ref[s]
@@ -183,28 +186,31 @@
     ).astype(bf16)
 
 
-def project_kernel(attended_ref, weight_ref, out_ref, rows_ref):
+def project_kernel(away, attended_ref, weight_ref, out_ref, rows_ref):
     steps = attended_ref.shape[0]
-    terms = jnp.dot(attended_ref[...], weight_ref[...], preferred_element_type=f32)
-    for k in range(weight_ref.shape[1] // LANES):
+    width = weight_ref.shape[1] // 2
+    half = lax.axis_index("ep")
+    if away:
+        half = 1 - half
+    columns = pl.ds(pl.multiple_of(half * width, LANES), width)
+    terms = jnp.dot(attended_ref[...], weight_ref[:, columns], preferred_element_type=f32)
+    used = steps * width // LANES
+    rows_ref[used:, :] = jnp.zeros((rows_ref.shape[0] - used, LANES), f32)
+    for k in range(width // LANES):
         rows_ref[k * steps : (k + 1) * steps, :] = terms[:, k * LANES : (k + 1) * LANES]
-    out_ref[...] = rows_ref[...].astype(bf16)
-
-
-def state_kernel(residual_ref, own_ref, other_ref, state_ref, sent_ref, rows_ref, wide_ref):
-    rows = state_ref.shape[0]
-    half = rows // 2
-    state = (
-        residual_ref[...] + (own_ref[...].astype(f32) + other_ref[...].astype(f32))
-    ).astype(bf16)
+    out_ref[...] = rows_ref[...].astype(out_ref.dtype)
+
+
+def state_kernel(residual_ref, here_ref, came_ref, state_ref, sent_ref, wide_ref):
+    residual = jnp.where(
+        lax.axis_index("ep") == 0,
+        residual_ref[:PIECE, :],
+        residual_ref[HALF_ROWS : HALF_ROWS + PIECE, :],
+    )
+    state = (residual + (here_ref[...] + came_ref[...].astype(f32))).astype(bf16).astype(f32)
     state_ref[...] = state
-    rows_ref[:rows, :] = state.astype(f32)
-    rows_ref[rows:, :] = jnp.zeros((rows_ref.shape[0] - rows, LANES), f32)
-    piece = jnp.where(
-        lax.axis_index("ep") == 0, rows_ref[:PIECE, :], rows_ref[half : half + PIECE, :]
-    )
     for g in range(wide_ref.shape[0] // PIECE):
-        wide_ref[g * PIECE : (g + 1) * PIECE, :] = piece
+        wide_ref[g * PIECE : (g + 1) * PIECE, :] = state
     sent_ref[...] = wide_ref[...].astype(bf16)
 
 
@@ -454,14 +460,12 @@
     out_ref[...] = wide_ref[...].astype(bf16)
 
 
-def output_kernel(state_ref, own_ref, other_ref, out_ref, rows_ref):
+def output_kernel(own_ref, other_ref, out_ref, rows_ref):
     steps, width = out_ref.shape
-    half = state_ref.shape[0] // 2
     lower = lax.axis_index("ep") == 0
     own, other = own_ref[...], other_ref[...]
     rows_ref[:PIECE, :] = jnp.where(lower, own, other)
-    rows_ref[half : half + PIECE, :] = jnp.where(lower, other, own)
-    rows_ref[: 2 * half, :] = state_ref[...].astype(f32) + rows_ref[: 2 * half, :]
+    rows_ref[HALF_ROWS : HALF_ROWS + PIECE, :] = jnp.where(lower, other, own)
     for k in range(width // LANES):
         out_ref[:, k * LANES : (k + 1) * LANES] = rows_ref[k * steps : (k + 1) * steps, :].astype(
             bf16
@@ -511,7 +515,7 @@
     square = struct((PAIRS, LANES, LANES), bf16)
     residual_rows, routes_row, tables, turned = call(
         rows_kernel,
-        (struct((rows, LANES), f32), struct((2, LANES), jnp.int32), square, square),
+        (struct((2 * PIECE, LANES), f32), struct((2, LANES), jnp.int32), square, square),
         (residual.reshape(steps, width), routes.transpose(0, 2, 1)),
         [VMEM] * 2,
     )
@@ -524,21 +528,24 @@
         [pltpu.VMEM((rows, HD), f32)],
         beside=2,
     )
-    terms = call(
-        project_kernel,
-        struct((rows, LANES), bf16),
-        (attended, out_weight),
-        [VMEM] * 2,
-        [pltpu.VMEM((rows, LANES), f32)],
-        beside=20,
-    )
-    other_terms = lax.ppermute(terms, "ep", swap)
+    away, here = (
+        call(
+            functools.partial(project_kernel, is_away),
+            struct((PIECE, LANES), kind),
+            (attended, out_weight),
+            [VMEM] * 2,
+            [pltpu.VMEM((PIECE, LANES), f32)],
+            beside=beside,
+        )
+        for is_away, kind, beside in ((True, bf16, 20), (False, f32, 3))
+    )
+    came = lax.ppermute(away, "ep", swap)
     state, sent_state = call(
         state_kernel,
-        (struct((rows, LANES), bf16), struct((groups * PIECE, LANES), bf16)),
-        (residual_rows, terms, other_terms),
+        (struct((PIECE, LANES), f32), struct((groups * PIECE, LANES), bf16)),
+        (residual_rows, here, came),
         [VMEM] * 3,
-        [pltpu.VMEM((2 * PIECE, LANES), f32), pltpu.VMEM((groups * PIECE, LANES), f32)],
+        [pltpu.VMEM((groups * PIECE, LANES), f32)],
     )
     own_state = lax.all_to_all(
         sent_state.reshape(groups, PIECE, LANES), "grp", 0, 0
@@ -624,13 +631,13 @@
         [wide],
     )
     received = lax.all_to_all(sent.reshape(groups, PIECE, LANES), "grp", 0, 0)
-    summed = jnp.sum(received.astype(f32), axis=0)
+    summed = state + jnp.sum(received.astype(f32), axis=0)
     other_summed = lax.ppermute(summed, "ep", swap)
     mixed = call(
         output_kernel,
         struct((steps, width), bf16),
-        (state, summed, other_summed),
-        [VMEM] * 3,
+        (summed, other_summed),
+        [VMEM] * 2,
         [pltpu.VMEM((2 * PIECE, LANES), f32)],
     )
     return mixed[:, None]

time: 64.8 us -> 64.1 us (0.989)
  waiting for transfers between devices: 6.85 us -> 6.01 us
    ppermute x1 -> x0, starting transfers between devices: 1.43 us -> none  [on_device(): other_terms = lax.ppermute(terms, 'ep', swap)]
    ppermute x1 -> x2, starting transfers between devices: 1.18 us -> 2.6 us  [on_device(): came = lax.ppermute(away, 'ep', swap)]
    pallas_call x14 -> x15, Pallas kernels: 9.42 us -> 9.54 us  [call(): pl.pallas_call(kernel, out_shape=out, in_specs=specs, out_specs=jax.tree....]
  transfers between devices with their start and end apart: 7 -> 7, of which waited for: 6 -> 5; matrix products, arithmetic and copies ran while one was open for 0% -> 0% of each run, Pallas kernels for 6% -> 8%
where the time goes in v6:
time: 64.1 us; the launch traced here: 63.9 us
  blocking collectives  35.8 us (56%)
  Pallas kernels  9.54 us (15%)
  starting transfers between devices  9.34 us (15%)
  waiting for transfers between devices  6.01 us (9%)
  local copies, waits for them, and re-layouts  2.16 us (3%)
  between operations  0.91 us (1%)
    all_to_all x1, blocking collectives, on_device(): lax.all_to_all(sent_state.reshape(groups, PIECE, LANES), 'grp', 0, 0)  21.6 us
    all_to_all x1, blocking collectives, on_device(): received = lax.all_to_all(sent.reshape(groups, PIECE, LANES), 'grp', 0, 0)  14.3 us
    pallas_call x15, Pallas kernels, call(): pl.pallas_call(kernel, out_shape=out, in_specs=specs, out_specs=jax.tree....  9.54 us
    ppermute x2, starting transfers between devices, on_device(): came = lax.ppermute(away, 'ep', swap)  2.6 us
    unnamed x32, local copies, waits for them, and re-layouts  2.16 us
    ppermute x1, waiting for transfers between devices, on_device(): other_hidden = lax.ppermute(hidden, 'tp', swap)  2.14 us
    ppermute x1, starting transfers between devices, on_device(): other = lax.ppermute(partial, 'tp', swap)  2.12 us
    ppermute x1, starting transfers between devices, on_device(): other_summed = lax.ppermute(summed, 'ep', swap)  1.61 us
  transfers between devices with their start and end apart: 7, of which 5 were waited for; matrix products, arithmetic and copies ran while one was open for 0% of the time, Pallas kernels for 8%

profile of v6, /device:TPU:1, one launch (start us, length us, event | category | flops | bytes accessed | tf_op | source)
XLA Modules:
  0.0 63.9 jit_solution(11299909974252385170)
XLA Ops:
  1.2 0.6 shard_map.138.own_ref
  1.8 2.1 %collective-permute-start = (bf16[72,256]{1,0:T(8,128)(2,1)S(1)}, bf16[72,256]{1,0:T(8,128)(2,1)S(1)}, u32[]{:S(2)}, u32[]{:S(2)}) collective-permute-start(bf16[72,256]{1,0:T(8,128)(2,1)S(1)} %shard_map.138.own_ref), channel_id=1, source_target_pairs={{0,1},{1,0},{2,3},{3,2},{4,5},{5,4},{6,7},{7,6},{8,9},{9,8},{10,11... | collective-permute-start | bytes 110600 | tf_op jit(solution)/shard_map/ppermute | solution.py:522
  4.2 1.0 %collective-permute-done.other_ref = bf16[72,256]{1,0:T(8,128)(2,1)S(1)} collective-permute-done((bf16[72,256]{1,0:T(8,128)(2,1)S(1)}, bf16[72,256]{1,0:T(8,128)(2,1)S(1)}, u32[]{:S(2)}, u32[]{:S(2)}) %collective-permute-start) | collective-permute-done | bytes 36896 | tf_op jit(solution)/shard_map/ppermute | solution.py:522
  5.5 1.7 %copy-done = bf16[3072,3072]{1,0:T(8,128)(2,1)S(1)} copy-done((bf16[3072,3072]{1,0:T(8,128)(2,1)S(1)}, bf16[3072,3072]{1,0:T(8,128)(2,1)}, u32[]{:S(2)}) %copy-start) | copy-done | bytes 18874392
  7.2 1.3 %shard_map.141 = bf16[40,128]{1,0:T(8,128)(2,1)S(1)} custom-call(bf16[3,3072]{1,0:T(4,128)(2,1)S(1)} %shard_map.139.attended_ref, bf16[3072,3072]{1,0:T(8,128)(2,1)S(1)} %copy-done), custom_call_target="tpu_custom_call" | custom-call | flops 20000000000 | tf_op jit(solution)/shard_map/pallas_call | solution.py:32
  8.6 1.4 %collective-permute-start.1 = (bf16[40,128]{1,0:T(8,128)(2,1)S(1)}, bf16[40,128]{1,0:T(8,128)(2,1)S(1)}, u32[]{:S(2)}, u32[]{:S(2)}) collective-permute-start(bf16[40,128]{1,0:T(8,128)(2,1)S(1)} %shard_map.141), channel_id=1, source_target_pairs={{0,2},{2,0},{1,3},{3,1},{4,6},{6,4},{5,7},{7,5},{8,10},{10,8},{9,1... | collective-permute-start | bytes 30728 | tf_op jit(solution)/shard_map/ppermute | solution.py:542
  10.0 1.3 %shard_map.140.here_ref = f32[40,128]{1,0:T(8,128)S(1)} custom-call(bf16[3,3072]{1,0:T(4,128)(2,1)S(1)} %shard_map.139.attended_ref, bf16[3072,3072]{1,0:T(8,128)(2,1)S(1)} %copy-done), custom_call_target="tpu_custom_call" | custom-call | flops 3000000000 | tf_op jit(solution)/shard_map/pallas_call | solution.py:32
  11.4 21.6 %all_to_all.10 = bf16[32,40,128]{2,1,0:T(8,128)(2,1)S(1)} all-to-all(bf16[32,40,128]{2,1,0:T(8,128)(2,1)S(1)} %bitcast.22), channel_id=1, replica_groups=mesh['grp'=32,'ep'=2,'tp'=2] {'grp'}, dimensions={0} | all-to-all | bytes 655360 | tf_op jit(solution)/shard_map/all_to_all | solution.py:550
  33.0 1.4 %collective-permute-start.2 = (bf16[1280,128]{1,0:T(8,128)(2,1)S(1)}, bf16[1280,128]{1,0:T(8,128)(2,1)S(1)}, u32[]{:S(2)}, u32[]{:S(2)}) collective-permute-start(bf16[1280,128]{1,0:T(8,128)(2,1)S(1)} %bitcast.20), channel_id=1, source_target_pairs={{0,2},{2,0},{1,3},{3,1},{4,6},{6,4},{5,7},{7,5},{8,10},{10,8},{9,1... | collective-permute-start | bytes 983048 | tf_op jit(solution)/shard_map/ppermute | solution.py:553
  34.4 1.3 %shard_map.143 = (f32[8,96,256]{2,1,0:T(8,128)S(1)}, f32[96,128]{1,0:T(8,128)S(1)}, f32[8,96]{1,0:T(8,128)S(1)}) custom-call(bf16[1280,128]{1,0:T(8,128)(2,1)S(1)} %bitcast.21, f32[1,3072]{1,0:T(1,128)S(1)} %bitcast.25, bf16[8,3072]{1,0:T(8,128)(2,1)S(1)} %bitcast.23, bf16[4,3072,256]{2,1,0:T(8,128)(2,1)S(1)} %bitcast.14, bf16[4,3072,256]{2,1,0:T(8,128)(2,1)S(1)} %bitcast.16), custom_call_target="tpu_custom_call" | custom-call | tf_op jit(solution)/shard_map/pallas_call | solution.py:32
  35.7 0.9 %shard_map.144 = (bf16[112,512]{1,0:T(8,128)(2,1)S(1)}, bf16[96,768]{1,0:T(8,128)(2,1)S(1)}, bf16[96,768]{1,0:T(8,128)(2,1)S(1)}) custom-call(bf16[1280,128]{1,0:T(8,128)(2,1)S(1)} %collective-permute-done.2.state_ref, f32[1,3072]{1,0:T(1,128)S(1)} %bitcast.26, bf16[8,3072]{1,0:T(8,128)(2,1)S(1)} %bitcast.24, ...), custom_call_target="tpu_custom_call" | custom-call | tf_op jit(solution)/shard_map/pallas_call | solution.py:32
  37.0 0.8 %shard_map.145.own_ref = bf16[96,512]{1,0:T(8,128)(2,1)S(1)} custom-call(bf16[96,768]{1,0:T(8,128)(2,1)S(1)} %get-tuple-element.28.refs_0_, bf16[96,768]{1,0:T(8,128)(2,1)S(1)} %get-tuple-element.29.refs_1_, bf16[2,128,128]{2,1,0:T(8,128)(2,1)S(1)} %get-tuple-element.24.tables_ref.refs_2_, bf16[4,3072,256]{2,1,0:T(8,128)(2,1)S(1)} %bitcast.14, ...), custom_call_target="tpu_custom_call" | custom-call | tf_op jit(solution)/shard_map/pallas_call | solution.py:32
  37.8 1.2 %collective-permute-start.3 = (bf16[96,512]{1,0:T(8,128)(2,1)S(1)}, bf16[96,512]{1,0:T(8,128)(2,1)S(1)}, u32[]{:S(2)}, u32[]{:S(2)}) collective-permute-start(bf16[96,512]{1,0:T(8,128)(2,1)S(1)} %shard_map.145.own_ref), channel_id=1, source_target_pairs={{0,1},{1,0},{2,3},{3,2},{4,5},{5,4},{6,7},{7,6},{8,9},{9,8},{10,11... | collective-permute-start | bytes 294920 | tf_op jit(solution)/shard_map/ppermute | solution.py:601
  39.0 2.1 %collective-permute-done.4.other_ref = bf16[112,512]{1,0:T(8,128)(2,1)S(1)} collective-permute-done((bf16[112,512]{1,0:T(8,128)(2,1)S(1)}, bf16[112,512]{1,0:T(8,128)(2,1)S(1)}, u32[]{:S(2)}, u32[]{:S(2)}) %collective-permute-start.4) | collective-permute-done | bytes 114720 | tf_op jit(solution)/shard_map/ppermute | solution.py:593
  41.2 0.9 %shard_map.146 = (f32[96,3072]{1,0:T(8,128)S(1)}, f32[96,128]{1,0:T(8,128)S(1)}) custom-call(bf16[112,512]{1,0:T(8,128)(2,1)S(1)} %get-tuple-element.30.own_ref, bf16[112,512]{1,0:T(8,128)(2,1)S(1)} %collective-permute-done.4.other_ref, s32[2,128]{1,0:T(2,128)S(1)} %get-tuple-element.31.routes_ref, ...), custom_call_target="tpu_custom_call" | custom-call | tf_op jit(solution)/shard_map/pallas_call | solution.py:32
  42.1 1.2 %collective-permute-done.3.other_ref = bf16[96,512]{1,0:T(8,128)(2,1)S(1)} collective-permute-done((bf16[96,512]{1,0:T(8,128)(2,1)S(1)}, bf16[96,512]{1,0:T(8,128)(2,1)S(1)}, u32[]{:S(2)}, u32[]{:S(2)}) %collective-permute-start.3) | collective-permute-done | bytes 98336 | tf_op jit(solution)/shard_map/ppermute | solution.py:601
  43.3 0.6 shard_map.147
  43.9 1.2 %collective-permute-start.5 = (bf16[96,1536]{1,0:T(8,128)(2,1)S(1)}, bf16[96,1536]{1,0:T(8,128)(2,1)S(1)}, u32[]{:S(2)}, u32[]{:S(2)}) collective-permute-start(bf16[96,1536]{1,0:T(8,128)(2,1)S(1)} %get-tuple-element.36), channel_id=1, source_target_pairs={{0,2},{2,0},{1,3},{3,1},{4,6},{6,4},{5,7},{7,5},{8,10},{10,8},{9,1... | collective-permute-start | bytes 884744 | tf_op jit(solution)/shard_map/ppermute | solution.py:619
  45.0 0.4 shard_map.148.here_ref
  45.4 0.8 %collective-permute-done.5.came_ref = bf16[96,1536]{1,0:T(8,128)(2,1)S(1)} collective-permute-done((bf16[96,1536]{1,0:T(8,128)(2,1)S(1)}, bf16[96,1536]{1,0:T(8,128)(2,1)S(1)}, u32[]{:S(2)}, u32[]{:S(2)}) %collective-permute-start.5) | collective-permute-done | bytes 294944 | tf_op jit(solution)/shard_map/ppermute | solution.py:619
  46.4 14.3 %all_to_all.11 = bf16[32,40,128]{2,1,0:T(8,128)(2,1)S(1)} all-to-all(bf16[32,40,128]{2,1,0:T(8,128)(2,1)S(1)} %bitcast.19), channel_id=1, replica_groups=mesh['grp'=32,'ep'=2,'tp'=2] {'grp'}, dimensions={0} | all-to-all | bytes 655360 | tf_op jit(solution)/shard_map/all_to_all | solution.py:633
  60.8 1.6 %collective-permute-start.6 = (f32[40,128]{1,0:T(8,128)S(1)}, f32[40,128]{1,0:T(8,128)S(1)}, u32[]{:S(2)}, u32[]{:S(2)}) collective-permute-start(f32[40,128]{1,0:T(8,128)S(1)} %add.3.own_ref), channel_id=1, source_target_pairs={{0,2},{2,0},{1,3},{3,1},{4,6},{6,4},{5,7},{7,5},{8,10},{10,8},{9,1... | collective-permute-start | bytes 61448 | tf_op jit(solution)/shard_map/ppermute | solution.py:635
  62.4 0.8 %collective-permute-done.6.other_ref = f32[40,128]{1,0:T(8,128)S(1)} collective-permute-done((f32[40,128]{1,0:T(8,128)S(1)}, f32[40,128]{1,0:T(8,128)S(1)}, u32[]{:S(2)}, u32[]{:S(2)}) %collective-permute-start.6) | collective-permute-done | bytes 20512 | tf_op jit(solution)/shard_map/ppermute | solution.py:635
  63.2 0.6 shard_map.150
  (44 shorter events, 1.7 us)
Async XLA Ops:
  0.0 1.1 %copy-start.6 = (bf16[1,512,512]{2,1,0:T(8,128)(2,1)S(1)}, bf16[1,512,512]{2,1,0:T(8,128)(2,1)}, u32[]{:S(2)}) copy-start(bf16[1,512,512]{2,1,0:T(8,128)(2,1)} %param.18) | copy-start | bytes 1572868
  0.0 1.2 %copy-start.5 = (bf16[1,512,512]{2,1,0:T(8,128)(2,1)S(1)}, bf16[1,512,512]{2,1,0:T(8,128)(2,1)}, u32[]{:S(2)}) copy-start(bf16[1,512,512]{2,1,0:T(8,128)(2,1)} %param.17) | copy-start | bytes 1572868
  0.0 1.2 %copy-start.9 = (bf16[3,1,512]{2,0,1:T(4,128)(2,1)S(1)}, bf16[3,1,512]{2,0,1:T(4,128)(2,1)}, u32[]{:S(2)}) copy-start(bf16[3,1,512]{2,0,1:T(4,128)(2,1)} %param.16) | copy-start | bytes 9220
  0.0 1.2 %copy-start.8 = (bf16[3,1,512]{2,0,1:T(4,128)(2,1)S(1)}, bf16[3,1,512]{2,0,1:T(4,128)(2,1)}, u32[]{:S(2)}) copy-start(bf16[3,1,512]{2,0,1:T(4,128)(2,1)} %param.15) | copy-start | bytes 9220
  0.0 1.2 %copy-start.7 = (bf16[3,1,3072]{2,0,1:T(4,128)(2,1)S(1)}, bf16[3,1,3072]{2,0,1:T(4,128)(2,1)}, u32[]{:S(2)}) copy-start(bf16[3,1,3072]{2,0,1:T(4,128)(2,1)} %param.14) | copy-start | bytes 55300
  0.0 3.9 %copy-start.3 = (bf16[3,1,3072]{2,0,1:T(4,128)(2,1)S(1)}, bf16[3,1,3072]{2,0,1:T(4,128)(2,1)}, u32[]{:S(2)}) copy-start(bf16[3,1,3072]{2,0,1:T(4,128)(2,1)} %param.20) | copy-start | bytes 55300
  0.0 3.9 %copy-start.4 = (s32[3,32,2]{1,2,0:T(2,128)S(1)}, s32[3,32,2]{1,2,0:T(2,128)}, u32[]{:S(2)}) copy-start(s32[3,32,2]{1,2,0:T(2,128)} %param.24) | copy-start | bytes 2308
  0.8 6.5 %copy-start = (bf16[3072,3072]{1,0:T(8,128)(2,1)S(1)}, bf16[3072,3072]{1,0:T(8,128)(2,1)}, u32[]{:S(2)}) copy-start(bf16[3072,3072]{1,0:T(8,128)(2,1)} %weight_ref.3) | copy-start | bytes 56623108
  1.8 3.5 %collective-permute-start = (bf16[72,256]{1,0:T(8,128)(2,1)S(1)}, bf16[72,256]{1,0:T(8,128)(2,1)S(1)}, u32[]{:S(2)}, u32[]{:S(2)}) collective-permute-start(bf16[72,256]{1,0:T(8,128)(2,1)S(1)} %shard_map.138.own_ref), channel_id=1, source_target_pairs={{0,1},{1,0},{2,3},{3,2},{4,5},{5,4},{6,7},{7,6},{8,9},{9,8},{10,11... | collective-permute-start | bytes 110600 | tf_op jit(solution)/shard_map/ppermute | solution.py:522
  5.3 29.1 %slice-start = ((s8[6291456]{0:T(1024)(128)(4,1)}), s8[4194304]{0:T(1024)(128)(4,1)S(1)}, s32[]{:S(2)}) async-start(s8[6291456]{0:T(1024)(128)(4,1)} %bitcast.13), calls=%async_computation.2 | async-start | bytes 8388608
  5.3 29.1 %slice-start.2 = ((s8[6291456]{0:T(1024)(128)(4,1)}), s8[4194304]{0:T(1024)(128)(4,1)S(1)}, s32[]{:S(2)}) async-start(s8[6291456]{0:T(1024)(128)(4,1)} %bitcast.15), calls=%async_computation.4 | async-start | bytes 8388608
  7.2 27.1 %slice-start.1 = ((s8[6291456]{0:T(1024)(128)(4,1)}), s8[2097152]{0:T(1024)(128)(4,1)S(1)}, s32[]{:S(2)}) async-start(s8[6291456]{0:T(1024)(128)(4,1)} %bitcast.13), calls=%async_computation.3 | async-start | bytes 4194304
  7.2 27.1 %slice-start.3 = ((s8[6291456]{0:T(1024)(128)(4,1)}), s8[2097152]{0:T(1024)(128)(4,1)S(1)}, s32[]{:S(2)}) async-start(s8[6291456]{0:T(1024)(128)(4,1)} %bitcast.15), calls=%async_computation.5 | async-start | bytes 4194304
  8.6 25.8 %copy-start.1 = (bf16[3072,8]{0,1:T(8,128)(2,1)S(1)}, bf16[3072,8]{0,1:T(8,128)(2,1)}, u32[]{:S(2)}) copy-start(bf16[3072,8]{0,1:T(8,128)(2,1)} %param.23) | copy-start | bytes 147460
  8.6 25.8 %copy-start.2 = (f32[3072]{0:T(1024)S(1)}, f32[3072]{0:T(1024)}, u32[]{:S(2)}) copy-start(f32[3072]{0:T(1024)} %param.22) | copy-start | bytes 36868
  8.6 2.8 %collective-permute-start.1 = (bf16[40,128]{1,0:T(8,128)(2,1)S(1)}, bf16[40,128]{1,0:T(8,128)(2,1)S(1)}, u32[]{:S(2)}, u32[]{:S(2)}) collective-permute-start(bf16[40,128]{1,0:T(8,128)(2,1)S(1)} %shard_map.141), channel_id=1, source_target_pairs={{0,2},{2,0},{1,3},{3,1},{4,6},{6,4},{5,7},{7,5},{8,10},{10,8},{9,1... | collective-permute-start | bytes 30728 | tf_op jit(solution)/shard_map/ppermute | solution.py:542
  33.0 2.7 %collective-permute-start.2 = (bf16[1280,128]{1,0:T(8,128)(2,1)S(1)}, bf16[1280,128]{1,0:T(8,128)(2,1)S(1)}, u32[]{:S(2)}, u32[]{:S(2)}) collective-permute-start(bf16[1280,128]{1,0:T(8,128)(2,1)S(1)} %bitcast.20), channel_id=1, source_target_pairs={{0,2},{2,0},{1,3},{3,1},{4,6},{6,4},{5,7},{7,5},{8,10},{10,8},{9,1... | collective-permute-start | bytes 983048 | tf_op jit(solution)/shard_map/ppermute | solution.py:553
  34.4 6.7 %slice-start.4 = ((s8[6291456]{0:T(1024)(128)(4,1)}), s8[4194304]{0:T(1024)(128)(4,1)S(1)}, s32[]{:S(2)}) async-start(s8[6291456]{0:T(1024)(128)(4,1)} %bitcast.17), calls=%async_computation.6 | async-start | bytes 8388608
  35.7 5.5 %slice-start.5 = ((s8[6291456]{0:T(1024)(128)(4,1)}), s8[2097152]{0:T(1024)(128)(4,1)S(1)}, s32[]{:S(2)}) async-start(s8[6291456]{0:T(1024)(128)(4,1)} %bitcast.17), calls=%async_computation.7 | async-start | bytes 4194304
  36.6 4.5 %collective-permute-start.4 = (bf16[112,512]{1,0:T(8,128)(2,1)S(1)}, bf16[112,512]{1,0:T(8,128)(2,1)S(1)}, u32[]{:S(2)}, u32[]{:S(2)}) collective-permute-start(bf16[112,512]{1,0:T(8,128)(2,1)S(1)} %get-tuple-element.30.own_ref), channel_id=1, source_target_pairs={{0,1},{1,0},{2,3},{3,2},{4,5},{5,4},{6,7},{7,6},{8,9},{9,8},{10,11... | collective-permute-start | bytes 344072 | tf_op jit(solution)/shard_map/ppermute | solution.py:593
  37.8 5.5 %collective-permute-start.3 = (bf16[96,512]{1,0:T(8,128)(2,1)S(1)}, bf16[96,512]{1,0:T(8,128)(2,1)S(1)}, u32[]{:S(2)}, u32[]{:S(2)}) collective-permute-start(bf16[96,512]{1,0:T(8,128)(2,1)S(1)} %shard_map.145.own_ref), channel_id=1, source_target_pairs={{0,1},{1,0},{2,3},{3,2},{4,5},{5,4},{6,7},{7,6},{8,9},{9,8},{10,11... | collective-permute-start | bytes 294920 | tf_op jit(solution)/shard_map/ppermute | solution.py:601
  43.9 2.4 %collective-permute-start.5 = (bf16[96,1536]{1,0:T(8,128)(2,1)S(1)}, bf16[96,1536]{1,0:T(8,128)(2,1)S(1)}, u32[]{:S(2)}, u32[]{:S(2)}) collective-permute-start(bf16[96,1536]{1,0:T(8,128)(2,1)S(1)} %get-tuple-element.36), channel_id=1, source_target_pairs={{0,2},{2,0},{1,3},{3,1},{4,6},{6,4},{5,7},{7,5},{8,10},{10,8},{9,1... | collective-permute-start | bytes 884744 | tf_op jit(solution)/shard_map/ppermute | solution.py:619
  60.8 2.5 %collective-permute-start.6 = (f32[40,128]{1,0:T(8,128)S(1)}, f32[40,128]{1,0:T(8,128)S(1)}, u32[]{:S(2)}, u32[]{:S(2)}) collective-permute-start(f32[40,128]{1,0:T(8,128)S(1)} %add.3.own_ref), channel_id=1, source_target_pairs={{0,2},{2,0},{1,3},{3,1},{4,6},{6,4},{5,7},{7,5},{8,10},{10,8},{9,1... | collective-permute-start | bytes 61448 | tf_op jit(solution)/shard_map/ppermute | solution.py:635

commit v7 on v6

--- a/solution.py
+++ b/solution.py
@@ -16,7 +16,7 @@
 HALF_PARTS = 2
 HALF_ROWS = 36
 PIECE = 40
-EXTRA = 16
+EXTRA = 8
 LANES = 128
 
 far_below = -1e30
@@ -337,7 +337,6 @@
         ],
         axis=1,
     )
-    extra = jnp.concatenate([extra, jnp.zeros((EXTRA - E, 4 * LANES), f32)], axis=0)
     out_ref[2 * CAP :, :] = extra.astype(bf16)
 
 

time: 64.1 us -> 63.9 us (level)
  no operation moved by 1% of the time
where the time goes in v7:
time: 63.9 us; the launch traced here: 63.7 us
  blocking collectives  35.8 us (56%)
  Pallas kernels  9.55 us (15%)
  starting transfers between devices  9.34 us (15%)
  waiting for transfers between devices  5.84 us (9%)
  local copies, waits for them, and re-layouts  2.16 us (3%)
  between operations  0.92 us (1%)
    all_to_all x1, blocking collectives, on_device(): lax.all_to_all(sent_state.reshape(groups, PIECE, LANES), 'grp', 0, 0)  21.6 us
    all_to_all x1, blocking collectives, on_device(): received = lax.all_to_all(sent.reshape(groups, PIECE, LANES), 'grp', 0, 0)  14.3 us
    pallas_call x15, Pallas kernels, call(): pl.pallas_call(kernel, out_shape=out, in_specs=specs, out_specs=jax.tree....  9.55 us
    ppermute x2, starting transfers between devices, on_device(): came = lax.ppermute(away, 'ep', swap)  2.6 us
    unnamed x32, local copies, waits for them, and re-layouts  2.16 us
    ppermute x1, starting transfers between devices, on_device(): other = lax.ppermute(partial, 'tp', swap)  2.12 us
    ppermute x1, waiting for transfers between devices, on_device(): other_hidden = lax.ppermute(hidden, 'tp', swap)  1.96 us
    ppermute x1, starting transfers between devices, on_device(): other_summed = lax.ppermute(summed, 'ep', swap)  1.61 us
  transfers between devices with their start and end apart: 7, of which 5 were waited for; matrix products, arithmetic and copies ran while one was open for 0% of the time, Pallas kernels for 8%

profile of v7, /device:TPU:1, one launch (start us, length us, event | category | flops | bytes accessed | tf_op | source)
XLA Modules:
  0.0 63.7 jit_solution(5092894403395087410)
XLA Ops:
  1.2 0.6 shard_map.138.own_ref
  1.8 2.1 %collective-permute-start = (bf16[72,256]{1,0:T(8,128)(2,1)S(1)}, bf16[72,256]{1,0:T(8,128)(2,1)S(1)}, u32[]{:S(2)}, u32[]{:S(2)}) collective-permute-start(bf16[72,256]{1,0:T(8,128)(2,1)S(1)} %shard_map.138.own_ref), channel_id=1, source_target_pairs={{0,1},{1,0},{2,3},{3,2},{4,5},{5,4},{6,7},{7,6},{8,9},{9,8},{10,11... | collective-permute-start | bytes 110600 | tf_op jit(solution)/shard_map/ppermute | solution.py:521
  4.2 1.0 %collective-permute-done.other_ref = bf16[72,256]{1,0:T(8,128)(2,1)S(1)} collective-permute-done((bf16[72,256]{1,0:T(8,128)(2,1)S(1)}, bf16[72,256]{1,0:T(8,128)(2,1)S(1)}, u32[]{:S(2)}, u32[]{:S(2)}) %collective-permute-start) | collective-permute-done | bytes 36896 | tf_op jit(solution)/shard_map/ppermute | solution.py:521
  5.5 1.7 %copy-done = bf16[3072,3072]{1,0:T(8,128)(2,1)S(1)} copy-done((bf16[3072,3072]{1,0:T(8,128)(2,1)S(1)}, bf16[3072,3072]{1,0:T(8,128)(2,1)}, u32[]{:S(2)}) %copy-start) | copy-done | bytes 18874392
  7.2 1.3 %shard_map.141 = bf16[40,128]{1,0:T(8,128)(2,1)S(1)} custom-call(bf16[3,3072]{1,0:T(4,128)(2,1)S(1)} %shard_map.139.attended_ref, bf16[3072,3072]{1,0:T(8,128)(2,1)S(1)} %copy-done), custom_call_target="tpu_custom_call" | custom-call | flops 20000000000 | tf_op jit(solution)/shard_map/pallas_call | solution.py:32
  8.6 1.4 %collective-permute-start.1 = (bf16[40,128]{1,0:T(8,128)(2,1)S(1)}, bf16[40,128]{1,0:T(8,128)(2,1)S(1)}, u32[]{:S(2)}, u32[]{:S(2)}) collective-permute-start(bf16[40,128]{1,0:T(8,128)(2,1)S(1)} %shard_map.141), channel_id=1, source_target_pairs={{0,2},{2,0},{1,3},{3,1},{4,6},{6,4},{5,7},{7,5},{8,10},{10,8},{9,1... | collective-permute-start | bytes 30728 | tf_op jit(solution)/shard_map/ppermute | solution.py:541
  10.0 1.3 %shard_map.140.here_ref = f32[40,128]{1,0:T(8,128)S(1)} custom-call(bf16[3,3072]{1,0:T(4,128)(2,1)S(1)} %shard_map.139.attended_ref, bf16[3072,3072]{1,0:T(8,128)(2,1)S(1)} %copy-done), custom_call_target="tpu_custom_call" | custom-call | flops 3000000000 | tf_op jit(solution)/shard_map/pallas_call | solution.py:32
  11.4 21.6 %all_to_all.10 = bf16[32,40,128]{2,1,0:T(8,128)(2,1)S(1)} all-to-all(bf16[32,40,128]{2,1,0:T(8,128)(2,1)S(1)} %bitcast.22), channel_id=1, replica_groups=mesh['grp'=32,'ep'=2,'tp'=2] {'grp'}, dimensions={0} | all-to-all | bytes 655360 | tf_op jit(solution)/shard_map/all_to_all | solution.py:549
  33.0 1.4 %collective-permute-start.2 = (bf16[1280,128]{1,0:T(8,128)(2,1)S(1)}, bf16[1280,128]{1,0:T(8,128)(2,1)S(1)}, u32[]{:S(2)}, u32[]{:S(2)}) collective-permute-start(bf16[1280,128]{1,0:T(8,128)(2,1)S(1)} %bitcast.20), channel_id=1, source_target_pairs={{0,2},{2,0},{1,3},{3,1},{4,6},{6,4},{5,7},{7,5},{8,10},{10,8},{9,1... | collective-permute-start | bytes 983048 | tf_op jit(solution)/shard_map/ppermute | solution.py:552
  34.4 1.3 %shard_map.143 = (f32[8,96,256]{2,1,0:T(8,128)S(1)}, f32[96,128]{1,0:T(8,128)S(1)}, f32[8,96]{1,0:T(8,128)S(1)}) custom-call(bf16[1280,128]{1,0:T(8,128)(2,1)S(1)} %bitcast.21, f32[1,3072]{1,0:T(1,128)S(1)} %bitcast.25, bf16[8,3072]{1,0:T(8,128)(2,1)S(1)} %bitcast.23, bf16[4,3072,256]{2,1,0:T(8,128)(2,1)S(1)} %bitcast.14, bf16[4,3072,256]{2,1,0:T(8,128)(2,1)S(1)} %bitcast.16), custom_call_target="tpu_custom_call" | custom-call | tf_op jit(solution)/shard_map/pallas_call | solution.py:32
  35.7 0.9 %shard_map.144 = (bf16[104,512]{1,0:T(8,128)(2,1)S(1)}, bf16[96,768]{1,0:T(8,128)(2,1)S(1)}, bf16[96,768]{1,0:T(8,128)(2,1)S(1)}) custom-call(bf16[1280,128]{1,0:T(8,128)(2,1)S(1)} %collective-permute-done.2.state_ref, f32[1,3072]{1,0:T(1,128)S(1)} %bitcast.26, bf16[8,3072]{1,0:T(8,128)(2,1)S(1)} %bitcast.24, ...), custom_call_target="tpu_custom_call" | custom-call | tf_op jit(solution)/shard_map/pallas_call | solution.py:32
  37.0 0.8 %shard_map.145.own_ref = bf16[96,512]{1,0:T(8,128)(2,1)S(1)} custom-call(bf16[96,768]{1,0:T(8,128)(2,1)S(1)} %get-tuple-element.28.refs_0_, bf16[96,768]{1,0:T(8,128)(2,1)S(1)} %get-tuple-element.29.refs_1_, bf16[2,128,128]{2,1,0:T(8,128)(2,1)S(1)} %get-tuple-element.24.tables_ref.refs_2_, bf16[4,3072,256]{2,1,0:T(8,128)(2,1)S(1)} %bitcast.14, ...), custom_call_target="tpu_custom_call" | custom-call | tf_op jit(solution)/shard_map/pallas_call | solution.py:32
  37.8 1.2 %collective-permute-start.3 = (bf16[96,512]{1,0:T(8,128)(2,1)S(1)}, bf16[96,512]{1,0:T(8,128)(2,1)S(1)}, u32[]{:S(2)}, u32[]{:S(2)}) collective-permute-start(bf16[96,512]{1,0:T(8,128)(2,1)S(1)} %shard_map.145.own_ref), channel_id=1, source_target_pairs={{0,1},{1,0},{2,3},{3,2},{4,5},{5,4},{6,7},{7,6},{8,9},{9,8},{10,11... | collective-permute-start | bytes 294920 | tf_op jit(solution)/shard_map/ppermute | solution.py:600
  39.0 2.0 %collective-permute-done.4.other_ref = bf16[104,512]{1,0:T(8,128)(2,1)S(1)} collective-permute-done((bf16[104,512]{1,0:T(8,128)(2,1)S(1)}, bf16[104,512]{1,0:T(8,128)(2,1)S(1)}, u32[]{:S(2)}, u32[]{:S(2)}) %collective-permute-start.4) | collective-permute-done | bytes 106528 | tf_op jit(solution)/shard_map/ppermute | solution.py:592
  41.0 0.9 %shard_map.146 = (f32[96,3072]{1,0:T(8,128)S(1)}, f32[96,128]{1,0:T(8,128)S(1)}) custom-call(bf16[104,512]{1,0:T(8,128)(2,1)S(1)} %get-tuple-element.30.own_ref, bf16[104,512]{1,0:T(8,128)(2,1)S(1)} %collective-permute-done.4.other_ref, s32[2,128]{1,0:T(2,128)S(1)} %get-tuple-element.31.routes_ref, ...), custom_call_target="tpu_custom_call" | custom-call | tf_op jit(solution)/shard_map/pallas_call | solution.py:32
  41.9 1.2 %collective-permute-done.3.other_ref = bf16[96,512]{1,0:T(8,128)(2,1)S(1)} collective-permute-done((bf16[96,512]{1,0:T(8,128)(2,1)S(1)}, bf16[96,512]{1,0:T(8,128)(2,1)S(1)}, u32[]{:S(2)}, u32[]{:S(2)}) %collective-permute-start.3) | collective-permute-done | bytes 98336 | tf_op jit(solution)/shard_map/ppermute | solution.py:600
  43.1 0.6 shard_map.147
  43.7 1.2 %collective-permute-start.5 = (bf16[96,1536]{1,0:T(8,128)(2,1)S(1)}, bf16[96,1536]{1,0:T(8,128)(2,1)S(1)}, u32[]{:S(2)}, u32[]{:S(2)}) collective-permute-start(bf16[96,1536]{1,0:T(8,128)(2,1)S(1)} %get-tuple-element.36), channel_id=1, source_target_pairs={{0,2},{2,0},{1,3},{3,1},{4,6},{6,4},{5,7},{7,5},{8,10},{10,8},{9,1... | collective-permute-start | bytes 884744 | tf_op jit(solution)/shard_map/ppermute | solution.py:618
  44.9 0.4 shard_map.148.here_ref
  45.3 0.8 %collective-permute-done.5.came_ref = bf16[96,1536]{1,0:T(8,128)(2,1)S(1)} collective-permute-done((bf16[96,1536]{1,0:T(8,128)(2,1)S(1)}, bf16[96,1536]{1,0:T(8,128)(2,1)S(1)}, u32[]{:S(2)}, u32[]{:S(2)}) %collective-permute-start.5) | collective-permute-done | bytes 294944 | tf_op jit(solution)/shard_map/ppermute | solution.py:618
  46.3 14.3 %all_to_all.11 = bf16[32,40,128]{2,1,0:T(8,128)(2,1)S(1)} all-to-all(bf16[32,40,128]{2,1,0:T(8,128)(2,1)S(1)} %bitcast.19), channel_id=1, replica_groups=mesh['grp'=32,'ep'=2,'tp'=2] {'grp'}, dimensions={0} | all-to-all | bytes 655360 | tf_op jit(solution)/shard_map/all_to_all | solution.py:632
  60.6 1.6 %collective-permute-start.6 = (f32[40,128]{1,0:T(8,128)S(1)}, f32[40,128]{1,0:T(8,128)S(1)}, u32[]{:S(2)}, u32[]{:S(2)}) collective-permute-start(f32[40,128]{1,0:T(8,128)S(1)} %add.3.own_ref), channel_id=1, source_target_pairs={{0,2},{2,0},{1,3},{3,1},{4,6},{6,4},{5,7},{7,5},{8,10},{10,8},{9,1... | collective-permute-start | bytes 61448 | tf_op jit(solution)/shard_map/ppermute | solution.py:634
  62.2 0.8 %collective-permute-done.6.other_ref = f32[40,128]{1,0:T(8,128)S(1)} collective-permute-done((f32[40,128]{1,0:T(8,128)S(1)}, f32[40,128]{1,0:T(8,128)S(1)}, u32[]{:S(2)}, u32[]{:S(2)}) %collective-permute-start.6) | collective-permute-done | bytes 20512 | tf_op jit(solution)/shard_map/ppermute | solution.py:634
  63.1 0.6 shard_map.150
  (44 shorter events, 1.7 us)
Async XLA Ops:
  0.0 1.1 %copy-start.6 = (bf16[1,512,512]{2,1,0:T(8,128)(2,1)S(1)}, bf16[1,512,512]{2,1,0:T(8,128)(2,1)}, u32[]{:S(2)}) copy-start(bf16[1,512,512]{2,1,0:T(8,128)(2,1)} %param.18) | copy-start | bytes 1572868
  0.0 1.2 %copy-start.5 = (bf16[1,512,512]{2,1,0:T(8,128)(2,1)S(1)}, bf16[1,512,512]{2,1,0:T(8,128)(2,1)}, u32[]{:S(2)}) copy-start(bf16[1,512,512]{2,1,0:T(8,128)(2,1)} %param.17) | copy-start | bytes 1572868
  0.0 1.2 %copy-start.9 = (bf16[3,1,512]{2,0,1:T(4,128)(2,1)S(1)}, bf16[3,1,512]{2,0,1:T(4,128)(2,1)}, u32[]{:S(2)}) copy-start(bf16[3,1,512]{2,0,1:T(4,128)(2,1)} %param.16) | copy-start | bytes 9220
  0.0 1.2 %copy-start.8 = (bf16[3,1,512]{2,0,1:T(4,128)(2,1)S(1)}, bf16[3,1,512]{2,0,1:T(4,128)(2,1)}, u32[]{:S(2)}) copy-start(bf16[3,1,512]{2,0,1:T(4,128)(2,1)} %param.15) | copy-start | bytes 9220
  0.0 1.2 %copy-start.7 = (bf16[3,1,3072]{2,0,1:T(4,128)(2,1)S(1)}, bf16[3,1,3072]{2,0,1:T(4,128)(2,1)}, u32[]{:S(2)}) copy-start(bf16[3,1,3072]{2,0,1:T(4,128)(2,1)} %param.14) | copy-start | bytes 55300
  0.0 3.9 %copy-start.3 = (bf16[3,1,3072]{2,0,1:T(4,128)(2,1)S(1)}, bf16[3,1,3072]{2,0,1:T(4,128)(2,1)}, u32[]{:S(2)}) copy-start(bf16[3,1,3072]{2,0,1:T(4,128)(2,1)} %param.20) | copy-start | bytes 55300
  0.0 3.9 %copy-start.4 = (s32[3,32,2]{1,2,0:T(2,128)S(1)}, s32[3,32,2]{1,2,0:T(2,128)}, u32[]{:S(2)}) copy-start(s32[3,32,2]{1,2,0:T(2,128)} %param.24) | copy-start | bytes 2308
  0.8 6.5 %copy-start = (bf16[3072,3072]{1,0:T(8,128)(2,1)S(1)}, bf16[3072,3072]{1,0:T(8,128)(2,1)}, u32[]{:S(2)}) copy-start(bf16[3072,3072]{1,0:T(8,128)(2,1)} %weight_ref.3) | copy-start | bytes 56623108
  1.8 3.5 %collective-permute-start = (bf16[72,256]{1,0:T(8,128)(2,1)S(1)}, bf16[72,256]{1,0:T(8,128)(2,1)S(1)}, u32[]{:S(2)}, u32[]{:S(2)}) collective-permute-start(bf16[72,256]{1,0:T(8,128)(2,1)S(1)} %shard_map.138.own_ref), channel_id=1, source_target_pairs={{0,1},{1,0},{2,3},{3,2},{4,5},{5,4},{6,7},{7,6},{8,9},{9,8},{10,11... | collective-permute-start | bytes 110600 | tf_op jit(solution)/shard_map/ppermute | solution.py:521
  5.3 29.1 %slice-start = ((s8[6291456]{0:T(1024)(128)(4,1)}), s8[4194304]{0:T(1024)(128)(4,1)S(1)}, s32[]{:S(2)}) async-start(s8[6291456]{0:T(1024)(128)(4,1)} %bitcast.13), calls=%async_computation.2 | async-start | bytes 8388608
  5.3 29.1 %slice-start.2 = ((s8[6291456]{0:T(1024)(128)(4,1)}), s8[4194304]{0:T(1024)(128)(4,1)S(1)}, s32[]{:S(2)}) async-start(s8[6291456]{0:T(1024)(128)(4,1)} %bitcast.15), calls=%async_computation.4 | async-start | bytes 8388608
  7.2 27.1 %slice-start.1 = ((s8[6291456]{0:T(1024)(128)(4,1)}), s8[2097152]{0:T(1024)(128)(4,1)S(1)}, s32[]{:S(2)}) async-start(s8[6291456]{0:T(1024)(128)(4,1)} %bitcast.13), calls=%async_computation.3 | async-start | bytes 4194304
  7.2 27.1 %slice-start.3 = ((s8[6291456]{0:T(1024)(128)(4,1)}), s8[2097152]{0:T(1024)(128)(4,1)S(1)}, s32[]{:S(2)}) async-start(s8[6291456]{0:T(1024)(128)(4,1)} %bitcast.15), calls=%async_computation.5 | async-start | bytes 4194304
  8.6 25.8 %copy-start.1 = (bf16[3072,8]{0,1:T(8,128)(2,1)S(1)}, bf16[3072,8]{0,1:T(8,128)(2,1)}, u32[]{:S(2)}) copy-start(bf16[3072,8]{0,1:T(8,128)(2,1)} %param.23) | copy-start | bytes 147460
  8.6 25.8 %copy-start.2 = (f32[3072]{0:T(1024)S(1)}, f32[3072]{0:T(1024)}, u32[]{:S(2)}) copy-start(f32[3072]{0:T(1024)} %param.22) | copy-start | bytes 36868
  8.6 2.8 %collective-permute-start.1 = (bf16[40,128]{1,0:T(8,128)(2,1)S(1)}, bf16[40,128]{1,0:T(8,128)(2,1)S(1)}, u32[]{:S(2)}, u32[]{:S(2)}) collective-permute-start(bf16[40,128]{1,0:T(8,128)(2,1)S(1)} %shard_map.141), channel_id=1, source_target_pairs={{0,2},{2,0},{1,3},{3,1},{4,6},{6,4},{5,7},{7,5},{8,10},{10,8},{9,1... | collective-permute-start | bytes 30728 | tf_op jit(solution)/shard_map/ppermute | solution.py:541
  33.0 2.7 %collective-permute-start.2 = (bf16[1280,128]{1,0:T(8,128)(2,1)S(1)}, bf16[1280,128]{1,0:T(8,128)(2,1)S(1)}, u32[]{:S(2)}, u32[]{:S(2)}) collective-permute-start(bf16[1280,128]{1,0:T(8,128)(2,1)S(1)} %bitcast.20), channel_id=1, source_target_pairs={{0,2},{2,0},{1,3},{3,1},{4,6},{6,4},{5,7},{7,5},{8,10},{10,8},{9,1... | collective-permute-start | bytes 983048 | tf_op jit(solution)/shard_map/ppermute | solution.py:552
  34.4 6.6 %slice-start.4 = ((s8[6291456]{0:T(1024)(128)(4,1)}), s8[4194304]{0:T(1024)(128)(4,1)S(1)}, s32[]{:S(2)}) async-start(s8[6291456]{0:T(1024)(128)(4,1)} %bitcast.17), calls=%async_computation.6 | async-start | bytes 8388608
  35.7 5.3 %slice-start.5 = ((s8[6291456]{0:T(1024)(128)(4,1)}), s8[2097152]{0:T(1024)(128)(4,1)S(1)}, s32[]{:S(2)}) async-start(s8[6291456]{0:T(1024)(128)(4,1)} %bitcast.17), calls=%async_computation.7 | async-start | bytes 4194304
  36.7 4.3 %collective-permute-start.4 = (bf16[104,512]{1,0:T(8,128)(2,1)S(1)}, bf16[104,512]{1,0:T(8,128)(2,1)S(1)}, u32[]{:S(2)}, u32[]{:S(2)}) collective-permute-start(bf16[104,512]{1,0:T(8,128)(2,1)S(1)} %get-tuple-element.30.own_ref), channel_id=1, source_target_pairs={{0,1},{1,0},{2,3},{3,2},{4,5},{5,4},{6,7},{7,6},{8,9},{9,8},{10,11... | collective-permute-start | bytes 319496 | tf_op jit(solution)/shard_map/ppermute | solution.py:592
  37.8 5.3 %collective-permute-start.3 = (bf16[96,512]{1,0:T(8,128)(2,1)S(1)}, bf16[96,512]{1,0:T(8,128)(2,1)S(1)}, u32[]{:S(2)}, u32[]{:S(2)}) collective-permute-start(bf16[96,512]{1,0:T(8,128)(2,1)S(1)} %shard_map.145.own_ref), channel_id=1, source_target_pairs={{0,1},{1,0},{2,3},{3,2},{4,5},{5,4},{6,7},{7,6},{8,9},{9,8},{10,11... | collective-permute-start | bytes 294920 | tf_op jit(solution)/shard_map/ppermute | solution.py:600
  43.7 2.4 %collective-permute-start.5 = (bf16[96,1536]{1,0:T(8,128)(2,1)S(1)}, bf16[96,1536]{1,0:T(8,128)(2,1)S(1)}, u32[]{:S(2)}, u32[]{:S(2)}) collective-permute-start(bf16[96,1536]{1,0:T(8,128)(2,1)S(1)} %get-tuple-element.36), channel_id=1, source_target_pairs={{0,2},{2,0},{1,3},{3,1},{4,6},{6,4},{5,7},{7,5},{8,10},{10,8},{9,1... | collective-permute-start | bytes 884744 | tf_op jit(solution)/shard_map/ppermute | solution.py:618
  60.6 2.5 %collective-permute-start.6 = (f32[40,128]{1,0:T(8,128)S(1)}, f32[40,128]{1,0:T(8,128)S(1)}, u32[]{:S(2)}, u32[]{:S(2)}) collective-permute-start(f32[40,128]{1,0:T(8,128)S(1)} %add.3.own_ref), channel_id=1, source_target_pairs={{0,2},{2,0},{1,3},{3,1},{4,6},{6,4},{5,7},{7,5},{8,10},{10,8},{9,1... | collective-permute-start | bytes 61448 | tf_op jit(solution)/shard_map/ppermute | solution.py:634

commit v8 on v6

--- a/solution.py
+++ b/solution.py
@@ -463,7 +463,7 @@
 def output_kernel(own_ref, other_ref, out_ref, rows_ref):
     steps, width = out_ref.shape
     lower = lax.axis_index("ep") == 0
-    own, other = own_ref[...], other_ref[...]
+    own, other = own_ref[...].astype(f32), other_ref[...].astype(f32)
     rows_ref[:PIECE, :] = jnp.where(lower, own, other)
     rows_ref[HALF_ROWS : HALF_ROWS + PIECE, :] = jnp.where(lower, other, own)
     for k in range(width // LANES):
@@ -631,7 +631,7 @@
         [wide],
     )
     received = lax.all_to_all(sent.reshape(groups, PIECE, LANES), "grp", 0, 0)
-    summed = state + jnp.sum(received.astype(f32), axis=0)
+    summed = (state + jnp.sum(received.astype(f32), axis=0)).astype(bf16)
     other_summed = lax.ppermute(summed, "ep", swap)
     mixed = call(
         output_kernel,

time: 64.1 us -> 64.1 us (level)
  no operation moved by 1% of the time
where the time goes in v8:
time: 64.1 us; the launch traced here: 63.9 us
  blocking collectives  35.8 us (56%)
  Pallas kernels  9.54 us (15%)
  starting transfers between devices  9.34 us (15%)
  waiting for transfers between devices  6 us (9%)
  local copies, waits for them, and re-layouts  2.16 us (3%)
  between operations  0.91 us (1%)
    all_to_all x1, blocking collectives, on_device(): lax.all_to_all(sent_state.reshape(groups, PIECE, LANES), 'grp', 0, 0)  21.6 us
    all_to_all x1, blocking collectives, on_device(): received = lax.all_to_all(sent.reshape(groups, PIECE, LANES), 'grp', 0, 0)  14.3 us
    pallas_call x15, Pallas kernels, call(): pl.pallas_call(kernel, out_shape=out, in_specs=specs, out_specs=jax.tree....  9.54 us
    ppermute x2, starting transfers between devices, on_device(): came = lax.ppermute(away, 'ep', swap)  2.6 us
    unnamed x32, local copies, waits for them, and re-layouts  2.16 us
    ppermute x1, waiting for transfers between devices, on_device(): other_hidden = lax.ppermute(hidden, 'tp', swap)  2.14 us
    ppermute x1, starting transfers between devices, on_device(): other = lax.ppermute(partial, 'tp', swap)  2.12 us
    ppermute x1, starting transfers between devices, on_device(): other_summed = lax.ppermute(summed, 'ep', swap)  1.61 us
  transfers between devices with their start and end apart: 7, of which 5 were waited for; matrix products, arithmetic and copies ran while one was open for 0% of the time, Pallas kernels for 8%

profile of v8, /device:TPU:1, one launch (start us, length us, event | category | flops | bytes accessed | tf_op | source)
XLA Modules:
  0.0 63.9 jit_solution(5672987069753272863)
XLA Ops:
  1.2 0.6 shard_map.138.own_ref
  1.8 2.1 %collective-permute-start = (bf16[72,256]{1,0:T(8,128)(2,1)S(1)}, bf16[72,256]{1,0:T(8,128)(2,1)S(1)}, u32[]{:S(2)}, u32[]{:S(2)}) collective-permute-start(bf16[72,256]{1,0:T(8,128)(2,1)S(1)} %shard_map.138.own_ref), channel_id=1, source_target_pairs={{0,1},{1,0},{2,3},{3,2},{4,5},{5,4},{6,7},{7,6},{8,9},{9,8},{10,11... | collective-permute-start | bytes 110600 | tf_op jit(solution)/shard_map/ppermute | solution.py:522
  4.2 1.0 %collective-permute-done.other_ref = bf16[72,256]{1,0:T(8,128)(2,1)S(1)} collective-permute-done((bf16[72,256]{1,0:T(8,128)(2,1)S(1)}, bf16[72,256]{1,0:T(8,128)(2,1)S(1)}, u32[]{:S(2)}, u32[]{:S(2)}) %collective-permute-start) | collective-permute-done | bytes 36896 | tf_op jit(solution)/shard_map/ppermute | solution.py:522
  5.5 1.7 %copy-done = bf16[3072,3072]{1,0:T(8,128)(2,1)S(1)} copy-done((bf16[3072,3072]{1,0:T(8,128)(2,1)S(1)}, bf16[3072,3072]{1,0:T(8,128)(2,1)}, u32[]{:S(2)}) %copy-start) | copy-done | bytes 18874392
  7.2 1.3 %shard_map.141 = bf16[40,128]{1,0:T(8,128)(2,1)S(1)} custom-call(bf16[3,3072]{1,0:T(4,128)(2,1)S(1)} %shard_map.139.attended_ref, bf16[3072,3072]{1,0:T(8,128)(2,1)S(1)} %copy-done), custom_call_target="tpu_custom_call" | custom-call | flops 20000000000 | tf_op jit(solution)/shard_map/pallas_call | solution.py:32
  8.6 1.4 %collective-permute-start.1 = (bf16[40,128]{1,0:T(8,128)(2,1)S(1)}, bf16[40,128]{1,0:T(8,128)(2,1)S(1)}, u32[]{:S(2)}, u32[]{:S(2)}) collective-permute-start(bf16[40,128]{1,0:T(8,128)(2,1)S(1)} %shard_map.141), channel_id=1, source_target_pairs={{0,2},{2,0},{1,3},{3,1},{4,6},{6,4},{5,7},{7,5},{8,10},{10,8},{9,1... | collective-permute-start | bytes 30728 | tf_op jit(solution)/shard_map/ppermute | solution.py:542
  10.0 1.3 %shard_map.140.here_ref = f32[40,128]{1,0:T(8,128)S(1)} custom-call(bf16[3,3072]{1,0:T(4,128)(2,1)S(1)} %shard_map.139.attended_ref, bf16[3072,3072]{1,0:T(8,128)(2,1)S(1)} %copy-done), custom_call_target="tpu_custom_call" | custom-call | flops 3000000000 | tf_op jit(solution)/shard_map/pallas_call | solution.py:32
  11.4 21.6 %all_to_all.10 = bf16[32,40,128]{2,1,0:T(8,128)(2,1)S(1)} all-to-all(bf16[32,40,128]{2,1,0:T(8,128)(2,1)S(1)} %bitcast.22), channel_id=1, replica_groups=mesh['grp'=32,'ep'=2,'tp'=2] {'grp'}, dimensions={0} | all-to-all | bytes 655360 | tf_op jit(solution)/shard_map/all_to_all | solution.py:550
  33.0 1.4 %collective-permute-start.2 = (bf16[1280,128]{1,0:T(8,128)(2,1)S(1)}, bf16[1280,128]{1,0:T(8,128)(2,1)S(1)}, u32[]{:S(2)}, u32[]{:S(2)}) collective-permute-start(bf16[1280,128]{1,0:T(8,128)(2,1)S(1)} %bitcast.20), channel_id=1, source_target_pairs={{0,2},{2,0},{1,3},{3,1},{4,6},{6,4},{5,7},{7,5},{8,10},{10,8},{9,1... | collective-permute-start | bytes 983048 | tf_op jit(solution)/shard_map/ppermute | solution.py:553
  34.4 1.3 %shard_map.143 = (f32[8,96,256]{2,1,0:T(8,128)S(1)}, f32[96,128]{1,0:T(8,128)S(1)}, f32[8,96]{1,0:T(8,128)S(1)}) custom-call(bf16[1280,128]{1,0:T(8,128)(2,1)S(1)} %bitcast.21, f32[1,3072]{1,0:T(1,128)S(1)} %bitcast.25, bf16[8,3072]{1,0:T(8,128)(2,1)S(1)} %bitcast.23, bf16[4,3072,256]{2,1,0:T(8,128)(2,1)S(1)} %bitcast.14, bf16[4,3072,256]{2,1,0:T(8,128)(2,1)S(1)} %bitcast.16), custom_call_target="tpu_custom_call" | custom-call | tf_op jit(solution)/shard_map/pallas_call | solution.py:32
  35.7 0.9 %shard_map.144 = (bf16[112,512]{1,0:T(8,128)(2,1)S(1)}, bf16[96,768]{1,0:T(8,128)(2,1)S(1)}, bf16[96,768]{1,0:T(8,128)(2,1)S(1)}) custom-call(bf16[1280,128]{1,0:T(8,128)(2,1)S(1)} %collective-permute-done.2.state_ref, f32[1,3072]{1,0:T(1,128)S(1)} %bitcast.26, bf16[8,3072]{1,0:T(8,128)(2,1)S(1)} %bitcast.24, ...), custom_call_target="tpu_custom_call" | custom-call | tf_op jit(solution)/shard_map/pallas_call | solution.py:32
  37.0 0.8 %shard_map.145.own_ref = bf16[96,512]{1,0:T(8,128)(2,1)S(1)} custom-call(bf16[96,768]{1,0:T(8,128)(2,1)S(1)} %get-tuple-element.28.refs_0_, bf16[96,768]{1,0:T(8,128)(2,1)S(1)} %get-tuple-element.29.refs_1_, bf16[2,128,128]{2,1,0:T(8,128)(2,1)S(1)} %get-tuple-element.24.tables_ref.refs_2_, bf16[4,3072,256]{2,1,0:T(8,128)(2,1)S(1)} %bitcast.14, ...), custom_call_target="tpu_custom_call" | custom-call | tf_op jit(solution)/shard_map/pallas_call | solution.py:32
  37.8 1.2 %collective-permute-start.3 = (bf16[96,512]{1,0:T(8,128)(2,1)S(1)}, bf16[96,512]{1,0:T(8,128)(2,1)S(1)}, u32[]{:S(2)}, u32[]{:S(2)}) collective-permute-start(bf16[96,512]{1,0:T(8,128)(2,1)S(1)} %shard_map.145.own_ref), channel_id=1, source_target_pairs={{0,1},{1,0},{2,3},{3,2},{4,5},{5,4},{6,7},{7,6},{8,9},{9,8},{10,11... | collective-permute-start | bytes 294920 | tf_op jit(solution)/shard_map/ppermute | solution.py:601
  39.0 2.1 %collective-permute-done.4.other_ref = bf16[112,512]{1,0:T(8,128)(2,1)S(1)} collective-permute-done((bf16[112,512]{1,0:T(8,128)(2,1)S(1)}, bf16[112,512]{1,0:T(8,128)(2,1)S(1)}, u32[]{:S(2)}, u32[]{:S(2)}) %collective-permute-start.4) | collective-permute-done | bytes 114720 | tf_op jit(solution)/shard_map/ppermute | solution.py:593
  41.2 0.9 %shard_map.146 = (f32[96,3072]{1,0:T(8,128)S(1)}, f32[96,128]{1,0:T(8,128)S(1)}) custom-call(bf16[112,512]{1,0:T(8,128)(2,1)S(1)} %get-tuple-element.30.own_ref, bf16[112,512]{1,0:T(8,128)(2,1)S(1)} %collective-permute-done.4.other_ref, s32[2,128]{1,0:T(2,128)S(1)} %get-tuple-element.31.routes_ref, ...), custom_call_target="tpu_custom_call" | custom-call | tf_op jit(solution)/shard_map/pallas_call | solution.py:32
  42.1 1.2 %collective-permute-done.3.other_ref = bf16[96,512]{1,0:T(8,128)(2,1)S(1)} collective-permute-done((bf16[96,512]{1,0:T(8,128)(2,1)S(1)}, bf16[96,512]{1,0:T(8,128)(2,1)S(1)}, u32[]{:S(2)}, u32[]{:S(2)}) %collective-permute-start.3) | collective-permute-done | bytes 98336 | tf_op jit(solution)/shard_map/ppermute | solution.py:601
  43.3 0.6 shard_map.147
  43.9 1.2 %collective-permute-start.5 = (bf16[96,1536]{1,0:T(8,128)(2,1)S(1)}, bf16[96,1536]{1,0:T(8,128)(2,1)S(1)}, u32[]{:S(2)}, u32[]{:S(2)}) collective-permute-start(bf16[96,1536]{1,0:T(8,128)(2,1)S(1)} %get-tuple-element.36), channel_id=1, source_target_pairs={{0,2},{2,0},{1,3},{3,1},{4,6},{6,4},{5,7},{7,5},{8,10},{10,8},{9,1... | collective-permute-start | bytes 884744 | tf_op jit(solution)/shard_map/ppermute | solution.py:619
  45.0 0.4 shard_map.148.here_ref
  45.4 0.8 %collective-permute-done.5.came_ref = bf16[96,1536]{1,0:T(8,128)(2,1)S(1)} collective-permute-done((bf16[96,1536]{1,0:T(8,128)(2,1)S(1)}, bf16[96,1536]{1,0:T(8,128)(2,1)S(1)}, u32[]{:S(2)}, u32[]{:S(2)}) %collective-permute-start.5) | collective-permute-done | bytes 294944 | tf_op jit(solution)/shard_map/ppermute | solution.py:619
  46.4 14.3 %all_to_all.11 = bf16[32,40,128]{2,1,0:T(8,128)(2,1)S(1)} all-to-all(bf16[32,40,128]{2,1,0:T(8,128)(2,1)S(1)} %bitcast.19), channel_id=1, replica_groups=mesh['grp'=32,'ep'=2,'tp'=2] {'grp'}, dimensions={0} | all-to-all | bytes 655360 | tf_op jit(solution)/shard_map/all_to_all | solution.py:633
  60.8 1.6 %collective-permute-start.6 = (bf16[40,128]{1,0:T(8,128)(2,1)S(1)}, bf16[40,128]{1,0:T(8,128)(2,1)S(1)}, u32[]{:S(2)}, u32[]{:S(2)}) collective-permute-start(bf16[40,128]{1,0:T(8,128)(2,1)S(1)} %add_convert_fusion.own_ref), channel_id=1, source_target_pairs={{0,2},{2,0},{1,3},{3,1},{4,6},{6,4},{5,7},{7,5},{8,10},{10,8},{9,1... | collective-permute-start | bytes 30728 | tf_op jit(solution)/shard_map/ppermute | solution.py:635
  62.4 0.8 %collective-permute-done.6.other_ref = bf16[40,128]{1,0:T(8,128)(2,1)S(1)} collective-permute-done((bf16[40,128]{1,0:T(8,128)(2,1)S(1)}, bf16[40,128]{1,0:T(8,128)(2,1)S(1)}, u32[]{:S(2)}, u32[]{:S(2)}) %collective-permute-start.6) | collective-permute-done | bytes 10272 | tf_op jit(solution)/shard_map/ppermute | solution.py:635
  63.2 0.6 shard_map.150
  (44 shorter events, 1.7 us)
Async XLA Ops:
  0.0 1.1 %copy-start.6 = (bf16[1,512,512]{2,1,0:T(8,128)(2,1)S(1)}, bf16[1,512,512]{2,1,0:T(8,128)(2,1)}, u32[]{:S(2)}) copy-start(bf16[1,512,512]{2,1,0:T(8,128)(2,1)} %param.18) | copy-start | bytes 1572868
  0.0 1.2 %copy-start.5 = (bf16[1,512,512]{2,1,0:T(8,128)(2,1)S(1)}, bf16[1,512,512]{2,1,0:T(8,128)(2,1)}, u32[]{:S(2)}) copy-start(bf16[1,512,512]{2,1,0:T(8,128)(2,1)} %param.17) | copy-start | bytes 1572868
  0.0 1.2 %copy-start.9 = (bf16[3,1,512]{2,0,1:T(4,128)(2,1)S(1)}, bf16[3,1,512]{2,0,1:T(4,128)(2,1)}, u32[]{:S(2)}) copy-start(bf16[3,1,512]{2,0,1:T(4,128)(2,1)} %param.16) | copy-start | bytes 9220
  0.0 1.2 %copy-start.8 = (bf16[3,1,512]{2,0,1:T(4,128)(2,1)S(1)}, bf16[3,1,512]{2,0,1:T(4,128)(2,1)}, u32[]{:S(2)}) copy-start(bf16[3,1,512]{2,0,1:T(4,128)(2,1)} %param.15) | copy-start | bytes 9220
  0.0 1.2 %copy-start.7 = (bf16[3,1,3072]{2,0,1:T(4,128)(2,1)S(1)}, bf16[3,1,3072]{2,0,1:T(4,128)(2,1)}, u32[]{:S(2)}) copy-start(bf16[3,1,3072]{2,0,1:T(4,128)(2,1)} %param.14) | copy-start | bytes 55300
  0.0 3.9 %copy-start.3 = (bf16[3,1,3072]{2,0,1:T(4,128)(2,1)S(1)}, bf16[3,1,3072]{2,0,1:T(4,128)(2,1)}, u32[]{:S(2)}) copy-start(bf16[3,1,3072]{2,0,1:T(4,128)(2,1)} %param.20) | copy-start | bytes 55300
  0.0 3.9 %copy-start.4 = (s32[3,32,2]{1,2,0:T(2,128)S(1)}, s32[3,32,2]{1,2,0:T(2,128)}, u32[]{:S(2)}) copy-start(s32[3,32,2]{1,2,0:T(2,128)} %param.24) | copy-start | bytes 2308
  0.8 6.5 %copy-start = (bf16[3072,3072]{1,0:T(8,128)(2,1)S(1)}, bf16[3072,3072]{1,0:T(8,128)(2,1)}, u32[]{:S(2)}) copy-start(bf16[3072,3072]{1,0:T(8,128)(2,1)} %weight_ref.3) | copy-start | bytes 56623108
  1.8 3.5 %collective-permute-start = (bf16[72,256]{1,0:T(8,128)(2,1)S(1)}, bf16[72,256]{1,0:T(8,128)(2,1)S(1)}, u32[]{:S(2)}, u32[]{:S(2)}) collective-permute-start(bf16[72,256]{1,0:T(8,128)(2,1)S(1)} %shard_map.138.own_ref), channel_id=1, source_target_pairs={{0,1},{1,0},{2,3},{3,2},{4,5},{5,4},{6,7},{7,6},{8,9},{9,8},{10,11... | collective-permute-start | bytes 110600 | tf_op jit(solution)/shard_map/ppermute | solution.py:522
  5.3 29.1 %slice-start = ((s8[6291456]{0:T(1024)(128)(4,1)}), s8[4194304]{0:T(1024)(128)(4,1)S(1)}, s32[]{:S(2)}) async-start(s8[6291456]{0:T(1024)(128)(4,1)} %bitcast.13), calls=%async_computation.2 | async-start | bytes 8388608
  5.3 29.1 %slice-start.2 = ((s8[6291456]{0:T(1024)(128)(4,1)}), s8[4194304]{0:T(1024)(128)(4,1)S(1)}, s32[]{:S(2)}) async-start(s8[6291456]{0:T(1024)(128)(4,1)} %bitcast.15), calls=%async_computation.4 | async-start | bytes 8388608
  7.2 27.1 %slice-start.1 = ((s8[6291456]{0:T(1024)(128)(4,1)}), s8[2097152]{0:T(1024)(128)(4,1)S(1)}, s32[]{:S(2)}) async-start(s8[6291456]{0:T(1024)(128)(4,1)} %bitcast.13), calls=%async_computation.3 | async-start | bytes 4194304
  7.2 27.1 %slice-start.3 = ((s8[6291456]{0:T(1024)(128)(4,1)}), s8[2097152]{0:T(1024)(128)(4,1)S(1)}, s32[]{:S(2)}) async-start(s8[6291456]{0:T(1024)(128)(4,1)} %bitcast.15), calls=%async_computation.5 | async-start | bytes 4194304
  8.6 25.8 %copy-start.1 = (bf16[3072,8]{0,1:T(8,128)(2,1)S(1)}, bf16[3072,8]{0,1:T(8,128)(2,1)}, u32[]{:S(2)}) copy-start(bf16[3072,8]{0,1:T(8,128)(2,1)} %param.23) | copy-start | bytes 147460
  8.6 25.8 %copy-start.2 = (f32[3072]{0:T(1024)S(1)}, f32[3072]{0:T(1024)}, u32[]{:S(2)}) copy-start(f32[3072]{0:T(1024)} %param.22) | copy-start | bytes 36868
  8.6 2.8 %collective-permute-start.1 = (bf16[40,128]{1,0:T(8,128)(2,1)S(1)}, bf16[40,128]{1,0:T(8,128)(2,1)S(1)}, u32[]{:S(2)}, u32[]{:S(2)}) collective-permute-start(bf16[40,128]{1,0:T(8,128)(2,1)S(1)} %shard_map.141), channel_id=1, source_target_pairs={{0,2},{2,0},{1,3},{3,1},{4,6},{6,4},{5,7},{7,5},{8,10},{10,8},{9,1... | collective-permute-start | bytes 30728 | tf_op jit(solution)/shard_map/ppermute | solution.py:542
  33.0 2.7 %collective-permute-start.2 = (bf16[1280,128]{1,0:T(8,128)(2,1)S(1)}, bf16[1280,128]{1,0:T(8,128)(2,1)S(1)}, u32[]{:S(2)}, u32[]{:S(2)}) collective-permute-start(bf16[1280,128]{1,0:T(8,128)(2,1)S(1)} %bitcast.20), channel_id=1, source_target_pairs={{0,2},{2,0},{1,3},{3,1},{4,6},{6,4},{5,7},{7,5},{8,10},{10,8},{9,1... | collective-permute-start | bytes 983048 | tf_op jit(solution)/shard_map/ppermute | solution.py:553
  34.4 6.7 %slice-start.4 = ((s8[6291456]{0:T(1024)(128)(4,1)}), s8[4194304]{0:T(1024)(128)(4,1)S(1)}, s32[]{:S(2)}) async-start(s8[6291456]{0:T(1024)(128)(4,1)} %bitcast.17), calls=%async_computation.6 | async-start | bytes 8388608
  35.7 5.5 %slice-start.5 = ((s8[6291456]{0:T(1024)(128)(4,1)}), s8[2097152]{0:T(1024)(128)(4,1)S(1)}, s32[]{:S(2)}) async-start(s8[6291456]{0:T(1024)(128)(4,1)} %bitcast.17), calls=%async_computation.7 | async-start | bytes 4194304
  36.6 4.5 %collective-permute-start.4 = (bf16[112,512]{1,0:T(8,128)(2,1)S(1)}, bf16[112,512]{1,0:T(8,128)(2,1)S(1)}, u32[]{:S(2)}, u32[]{:S(2)}) collective-permute-start(bf16[112,512]{1,0:T(8,128)(2,1)S(1)} %get-tuple-element.30.own_ref), channel_id=1, source_target_pairs={{0,1},{1,0},{2,3},{3,2},{4,5},{5,4},{6,7},{7,6},{8,9},{9,8},{10,11... | collective-permute-start | bytes 344072 | tf_op jit(solution)/shard_map/ppermute | solution.py:593
  37.8 5.5 %collective-permute-start.3 = (bf16[96,512]{1,0:T(8,128)(2,1)S(1)}, bf16[96,512]{1,0:T(8,128)(2,1)S(1)}, u32[]{:S(2)}, u32[]{:S(2)}) collective-permute-start(bf16[96,512]{1,0:T(8,128)(2,1)S(1)} %shard_map.145.own_ref), channel_id=1, source_target_pairs={{0,1},{1,0},{2,3},{3,2},{4,5},{5,4},{6,7},{7,6},{8,9},{9,8},{10,11... | collective-permute-start | bytes 294920 | tf_op jit(solution)/shard_map/ppermute | solution.py:601
  43.9 2.4 %collective-permute-start.5 = (bf16[96,1536]{1,0:T(8,128)(2,1)S(1)}, bf16[96,1536]{1,0:T(8,128)(2,1)S(1)}, u32[]{:S(2)}, u32[]{:S(2)}) collective-permute-start(bf16[96,1536]{1,0:T(8,128)(2,1)S(1)} %get-tuple-element.36), channel_id=1, source_target_pairs={{0,2},{2,0},{1,3},{3,1},{4,6},{6,4},{5,7},{7,5},{8,10},{10,8},{9,1... | collective-permute-start | bytes 884744 | tf_op jit(solution)/shard_map/ppermute | solution.py:619
  60.8 2.4 %collective-permute-start.6 = (bf16[40,128]{1,0:T(8,128)(2,1)S(1)}, bf16[40,128]{1,0:T(8,128)(2,1)S(1)}, u32[]{:S(2)}, u32[]{:S(2)}) collective-permute-start(bf16[40,128]{1,0:T(8,128)(2,1)S(1)} %add_convert_fusion.own_ref), channel_id=1, source_target_pairs={{0,2},{2,0},{1,3},{3,1},{4,6},{6,4},{5,7},{7,5},{8,10},{10,8},{9,1... | collective-permute-start | bytes 30728 | tf_op jit(solution)/shard_map/ppermute | solution.py:635
